TPU v7x, 256 devices: a whole 4x4x8 slice. The times are simulated.
256 devices in a mesh: fsdp: 8 (over y, core), tensor: 4 (over x), replica: 8 (over z).
Axes of the slice: x: 4, y: 4, z: 8, core: 2. Of those that a mesh axis runs over, the one named last changes fastest.
Arguments:
- gradient: bfloat16 [8, 4096, 8192], P('replica', 'fsdp', 'tensor'), may hold values from -400 to 400, as said below
- momentum: float32 [8, 4096, 8192], P('replica', 'fsdp', 'tensor'), may hold values from -6 to 6
- basis: float32 [8192, 256], P('tensor', 'fsdp'), may hold values from -0.0625 to 0.0625
Outputs:
- update: bfloat16 [4096, 8192], P('fsdp', 'tensor')
- momentum_new: float32 [8, 4096, 8192], P('replica', 'fsdp', 'tensor')
- basis_new: float32 [8192, 256], P('tensor', 'fsdp')
Inputs may be any that keep to these rules, and one draw needn't show every extreme that they name: gradient entries are finite real numbers.
All inputs are finite; a program needn't handle non-finite values.
Results may differ from a plain program's by a relative error of at most 0.001.
Values sent between devices are 32-bit elements; how exact they have to be, the bound alone decides.
No kernel may reach another device: no remote copies, remote signals or barrier semaphores. Data moves between devices by JAX's collectives and lax.ppermute only.
A program may use at most 64 MiB of HBM per device.

v0:
```python
import jax
import jax.numpy as jnp
from jax import lax
from jax.sharding import Mesh
from jax.sharding import PartitionSpec as P

M_ROWS = 4096
NCOLS = 8192
RANK = 256
FSDP = ("fsdp_0", "fsdp_1")
FSDP_REPLICA = ("fsdp_0", "fsdp_1", "replica")


HIGH = lax.Precision.HIGHEST


def from_everyone(value, axis):
    size = lax.axis_size(axis)
    return lax.all_to_all(
        jnp.broadcast_to(value[None], (size, *value.shape)), axis, 0, 0, tiled=True
    )


def in_order(blocks, dim):
    dims = list(blocks.shape[1:])
    dims[dim] *= blocks.shape[0]
    return jnp.moveaxis(blocks, 0, dim).reshape(dims)


def whole_of(value, axes, dim):
    far, near = axes
    first = from_everyone(value, far)
    blocks = jnp.swapaxes(from_everyone(first, near), 0, 1)
    return in_order(blocks.reshape(-1, *value.shape), dim)


def in_blocks(value, dim, size):
    dims = value.shape
    blocks = value.reshape(*dims[:dim], size, dims[dim] // size, *dims[dim + 1 :])
    return jnp.moveaxis(blocks, dim, 0)


def sum_at_owner(value, axis, dim):
    blocks = in_blocks(value, dim, lax.axis_size(axis))
    arrived = lax.all_to_all(blocks, axis, split_axis=0, concat_axis=0, tiled=True)
    return arrived.sum(axis=0)


def filled_up(lines, size):
    spare = -len(lines) % size
    return jnp.pad(lines, [(0, spare)] + [(0, 0)] * (lines.ndim - 1))


def collect(value, axis, dim):
    return in_order(from_everyone(value, axis), dim)


def sum_by_parts(value, axes):
    lines = value.reshape(-1, value.shape[-1])
    own = sum_at_owner(filled_up(lines, lax.axis_size(axes)), axes, 0)
    whole = collect(own, axes, 0)
    return whole[: len(lines)].reshape(value.shape)


def over_copies(value, axis):
    return from_everyone(value, axis).sum(axis=0)


def local(gradient, momentum, basis):
    replicas = lax.axis_size("replica")
    rank_local = basis.shape[1]
    buffer = momentum[0] + gradient[0].astype(jnp.float32)
    partial_value = jnp.dot(
        buffer,
        whole_of(basis, ("fsdp_0", "fsdp_1"), 1),
        precision=HIGH,
        preferred_element_type=jnp.float32,
    )
    left = sum_by_parts(partial_value, ("tensor", "replica")) / replicas
    local_gram = jnp.dot(left.T, left, precision=HIGH, preferred_element_type=jnp.float32)
    gram = over_copies(local_gram, FSDP)
    chol = jnp.linalg.cholesky(gram)
    ortho = lax.linalg.triangular_solve(chol, left, left_side=False, lower=True, transpose_a=True)
    right_part = jnp.dot(buffer.T, ortho, precision=HIGH, preferred_element_type=jnp.float32)
    right = sum_by_parts(right_part, FSDP_REPLICA) / replicas
    squares = over_copies(jnp.sum(right * right, axis=0), "tensor")
    norms = jnp.sqrt(squares + 1e-12)
    basis_full = right / norms
    lowrank = jnp.dot(ortho, right.T, precision=HIGH, preferred_element_type=jnp.float32)
    momentum_new = (buffer - 0.05 * lowrank)[None]
    scale = (M_ROWS * NCOLS / RANK) ** 0.5
    update = (
        scale * jnp.dot(ortho, basis_full.T, precision=HIGH, preferred_element_type=jnp.float32)
    ).astype(jnp.bfloat16)
    offset = lax.axis_index(FSDP) * rank_local
    basis_new = lax.dynamic_slice_in_dim(basis_full, offset, rank_local, 1)
    return (update, momentum_new, basis_new)


def solution(mesh):
    finer = Mesh(
        mesh.devices.reshape(4, 2, mesh.shape["tensor"], mesh.shape["replica"]),
        ("fsdp_0", "fsdp_1", "tensor", "replica"),
    )
    placed = (P("replica", FSDP, "tensor"), P("replica", FSDP, "tensor"), P("tensor", FSDP))
    return jax.shard_map(
        local,
        mesh=finer,
        in_specs=placed,
        out_specs=(P(FSDP, "tensor"), P("replica", FSDP, "tensor"), P("tensor", FSDP)),
        check_vma=False,
    )
```

profile of v0, /device:TPU:1, one launch (start us, length us, event | category | flops | bytes accessed | tf_op | source)
XLA Modules:
  0.0 328.7 jit_solution(12473270289452058507)
XLA Ops:
  0.6 2.2 broadcast_in_dim.15
  2.8 5.0 %all-to-all-start = ((f32[4,2048,32]{1,2,0:T(8,128)}), f32[4,2048,32]{1,2,0:T(8,128)S(1)}, u32[]{:S(2)}, u32[]{:S(2)}) async-start(f32[4,2048,32]{1,2,0:T(8,128)} %broadcast_in_dim.15), calls=%async_computation | async-start | bytes 2097152 | tf_op jit(solution)/shard_map/all_to_all | solution.py:19
  7.8 5.1 %convert_add_fusion = f32[1,512,2048]{2,1,0:T(8,128)} fusion(f32[1,512,2048]{2,1,0:T(8,128)} %param.4, bf16[1,512,2048]{2,1,0:T(8,128)(2,1)S(1)} %copy-done.1), kind=kLoop, calls=%fused_computation.5 | loop fusion | flops 2097152 | bytes 10485760 | tf_op jit(solution)/shard_map/add | solution.py:72
  12.9 8.3 %all-to-all-done = f32[4,2048,32]{1,2,0:T(8,128)S(1)} async-done(((f32[4,2048,32]{1,2,0:T(8,128)}), f32[4,2048,32]{1,2,0:T(8,128)S(1)}, u32[]{:S(2)}, u32[]{:S(2)}) %all-to-all-start) | async-done | bytes 1048608 | tf_op jit(solution)/shard_map/all_to_all | solution.py:19
  21.2 0.2 broadcast_in_dim.16
  21.5 7.7 %all_to_all.41 = f32[2,4,2048,32]{2,3,1,0:T(8,128)S(1)} all-to-all(f32[2,4,2048,32]{2,3,1,0:T(8,128)S(1)} %broadcast_in_dim.16), channel_id=1, replica_groups=mesh['fsdp_0'=4,'fsdp_1'=2,'tensor'=4,'replica'=8] {'fsdp_1'}, dimensions={0} | all-to-all | bytes 4194304 | tf_op jit(solution)/shard_map/all_to_all | solution.py:19
  29.2 0.1 copy.32
  29.3 2.0 copy-done
  31.3 3.5 %fusion.15 = f32[32,16,256]{2,1,0:T(8,128)S(1)} fusion(f32[32,16,2048]{2,1,0:T(8,128)S(1)} %bitcast.63, f32[2048,256,1]{0,1,2:T(8,128)S(1)} %bitcast.67), kind=kOutput, calls=%fused_computation.45 | convolution fusion | flops 3221225472 | bytes 6815744 | tf_op jit(solution)/shard_map/dot_general | solution.py:73
  34.8 25.0 %all_to_all.42 = f32[32,16,256]{2,1,0:T(8,128)S(1)} all-to-all(f32[32,16,256]{2,1,0:T(8,128)S(1)} %fusion.15), channel_id=1, replica_groups=mesh['fsdp_0'=4,'fsdp_1'=2,'tensor'=4,'replica'=8] {'tensor','replica'}, dimensions={0} | all-to-all | bytes 1048576 | tf_op jit(solution)/shard_map/all_to_all | solution.py:45
  59.9 22.0 %all_to_all.43 = f32[32,16,256]{2,1,0:T(8,128)S(1)} all-to-all(f32[32,16,256]{2,1,0:T(8,128)S(1)} %broadcast_in_dim.18), channel_id=1, replica_groups=mesh['fsdp_0'=4,'fsdp_1'=2,'tensor'=4,'replica'=8] {'tensor','replica'}, dimensions={0} | all-to-all | bytes 1048576 | tf_op jit(solution)/shard_map/all_to_all | solution.py:19
  81.9 1.5 convolution_bitcast_fusion
  83.4 1.5 broadcast_in_dim.19
  84.9 7.5 %all-to-all-start.4 = ((f32[8,256,256]{2,1,0:T(8,128)}), f32[8,256,256]{2,1,0:T(8,128)S(1)}, u32[]{:S(2)}, u32[]{:S(2)}) async-start(f32[8,256,256]{2,1,0:T(8,128)} %broadcast_in_dim.19), calls=%async_computation.4 | async-start | bytes 4194304 | tf_op jit(solution)/shard_map/all_to_all | solution.py:19
  92.4 5.3 %copy.37 = f32[2048,512]{1,0:T(8,128)} copy(f32[2048,512]{0,1:T(8,128)} %bitcast.62) | data formatting | bytes 8388608 | tf_op jit(solution)/shard_map/dot_general | solution.py:84
  97.8 0.3 copy_multiply_fusion
  98.1 0.3 copy.35
  98.4 20.3 %all-to-all-done.4 = f32[8,256,256]{2,1,0:T(8,128)S(1)} async-done(((f32[8,256,256]{2,1,0:T(8,128)}), f32[8,256,256]{2,1,0:T(8,128)S(1)}, u32[]{:S(2)}, u32[]{:S(2)}) %all-to-all-start.4) | async-done | bytes 2097184 | tf_op jit(solution)/shard_map/all_to_all | solution.py:19
  118.7 0.1 reduce_sum.46
  119.1 11.7 %cholesky.50 = f32[128,128]{1,0:T(8,128)S(1)} custom-call(f32[128,128]{1,0:T(8,128)S(1)} %cholesky.118), custom_call_target="Cholesky" | custom-call | tf_op jit(solution)/shard_map/jit(cholesky)/cholesky | solution.py:82
  130.9 9.8 %custom-call.14 = f32[1,128,128]{1,2,0:T(8,128)S(1)} custom-call(f32[1,128,128]{2,1,0:T(8,128)S(1)} %get-tuple-element.38), custom_call_target="InvertDiagBlocksLowerTriangular" | custom-call | tf_op jit(solution)/shard_map/jit(cholesky)/cholesky | solution.py:82
  140.7 0.2 constant_dynamic-update-slice_fusion
  140.9 0.3 convolution_subtract_fusion.1
  141.2 11.7 %cholesky.105 = f32[128,128]{1,0:T(8,128)S(1)} custom-call(f32[128,128]{1,0:T(8,128)S(1)} %convolution_subtract_fusion.1), custom_call_target="Cholesky" | custom-call | tf_op jit(solution)/shard_map/jit(cholesky)/cholesky | solution.py:82
  152.9 0.7 compare_reduce_fusion
  154.9 3.9 %while.1 = (s32[]{:T(128)}, f32[256,256]{1,0:T(8,128)S(1)}, s32[2,2]{1,0:T(2,128)S(1)}, f32[2,128,128]{2,1,0:T(8,128)S(1)}, s32[]{:T(128)}) while((s32[]{:T(128)}, f32[256,256]{1,0:T(8,128)S(1)}, s32[2,2]{1,0:T(2,128)S(1)}, f32[2,128,128]{2,1,0:T(8,128)S(1)}, s32[]{:T(128)}) %tuple.32), condition=%wide.while_cond, body=%wide.while_body.sunk | while | flops 2 | bytes 131181 | solution.py:83
  155.0 0.6 fusion.26
  155.5 1.4 bitcast_dynamic-update-slice_fusion.2
  156.9 0.6 fusion.26
  157.5 1.4 bitcast_dynamic-update-slice_fusion.2
  158.9 19.9 %custom-call.15 = f32[2,128,128]{1,2,0:T(8,128)S(1)} custom-call(f32[2,128,128]{2,1,0:T(8,128)S(1)} %get-tuple-element.10), custom_call_target="InvertDiagBlocksLowerTriangular" | custom-call | tf_op jit(solution)/shard_map/triangular_solve | solution.py:83
  178.8 0.4 fusion.3
  179.2 0.6 convolution_subtract_fusion
  179.8 0.4 fusion.6
  180.2 5.9 %fusion.1 = f32[64,32,256]{2,1,0:T(8,128)S(1)} fusion(f32[64,32,512]{2,1,0:T(8,128)} %bitcast.65, f32[512,128]{0,1:T(8,128)S(1)} %fusion.6, f32[512,128]{0,1:T(8,128)S(1)} %fusion.3), kind=kOutput, calls=%fused_computation.13 | convolution fusion | flops 3221356544 | bytes 6815744 | tf_op jit(solution)/shard_map/dot_general | solution.py:84
  186.2 57.8 %all_to_all.44 = f32[64,32,256]{2,1,0:T(8,128)S(1)} all-to-all(f32[64,32,256]{2,1,0:T(8,128)S(1)} %fusion.1), channel_id=1, replica_groups=mesh['fsdp_0'=4,'fsdp_1'=2,'tensor'=4,'replica'=8] {'fsdp_0','fsdp_1','r..., dimensions={0} | all-to-all | bytes 4194304 | tf_op jit(solution)/shard_map/all_to_all | solution.py:45
  244.0 0.1 reduce_sum.47
  244.1 1.6 broadcast_in_dim.20
  245.7 5.8 %all-to-all-start.6 = ((f32[64,32,256]{2,1,0:T(8,128)}), f32[64,32,256]{2,1,0:T(8,128)}, u32[]{:S(2)}, u32[]{:S(2)}) async-start(f32[64,32,256]{2,1,0:T(8,128)} %broadcast_in_dim.20), calls=%async_computation.6 | async-start | bytes 4194304 | tf_op jit(solution)/shard_map/all_to_all | solution.py:19
  251.4 51.7 %all-to-all-done.6 = f32[64,32,256]{2,1,0:T(8,128)} async-done(((f32[64,32,256]{2,1,0:T(8,128)}), f32[64,32,256]{2,1,0:T(8,128)}, u32[]{:S(2)}, u32[]{:S(2)}) %all-to-all-start.6) | async-done | bytes 2097184 | tf_op jit(solution)/shard_map/all_to_all | solution.py:19
  303.2 1.9 broadcast_multiply_fusion
  305.1 0.6 broadcast_in_dim.21
  305.7 3.5 %all-to-all-start.7 = ((f32[4,1,256]{2,1,0:T(1,128)}), f32[4,1,256]{2,1,0:T(1,128)S(1)}, u32[]{:S(2)}, u32[]{:S(2)}) async-start(f32[4,1,256]{2,1,0:T(1,128)} %broadcast_in_dim.21), calls=%async_computation.7 | async-start | bytes 8192 | tf_op jit(solution)/shard_map/all_to_all | solution.py:19
  309.2 9.9 %fusion = f32[1,512,2048]{2,1,0:T(8,128)} fusion(f32[1,512,2048]{2,1,0:T(8,128)} %convert_add_fusion, f32[2048,256]{1,0:T(8,128)S(1)} %bitcast.64, f32[512,128]{0,1:T(8,128)S(1)} %fusion.6, f32[512,128]{0,1:T(8,128)S(1)} %fusion.3), kind=kOutput, calls=%fused_computation.3 | convolution fusion | flops 3223453696 | bytes 11010048 | tf_op jit(solution)/shard_map/dot_general | solution.py:89
  319.2 0.1 broadcast_divide_fusion
  319.3 8.0 %multiply_convert_fusion = bf16[512,2048]{1,0:T(8,128)(2,1)} fusion(f32[2048,256]{1,0:T(8,128)S(1)} %broadcast_divide_fusion, f32[512,128]{0,1:T(8,128)S(1)} %fusion.6, f32[512,128]{0,1:T(8,128)S(1)} %fusion.3), kind=kOutput, calls=%fused_computation.4 | convolution fusion | flops 3223453696 | bytes 4718592 | tf_op jit(solution)/shard_map/dot_general | solution.py:93
  327.3 0.3 constant_dynamic-slice_fusion.1
  327.6 1.0 copy.40
  (20 shorter events, 0.5 us)
Async XLA Ops:
  0.6 7.2 %copy-start.1 = (bf16[1,512,2048]{2,1,0:T(8,128)(2,1)S(1)}, bf16[1,512,2048]{2,1,0:T(8,128)(2,1)}, u32[]{:S(2)}) copy-start(bf16[1,512,2048]{2,1,0:T(8,128)(2,1)} %param.3) | copy-start | bytes 6291460
  2.8 18.4 %all-to-all-start = ((f32[4,2048,32]{1,2,0:T(8,128)}), f32[4,2048,32]{1,2,0:T(8,128)S(1)}, u32[]{:S(2)}, u32[]{:S(2)}) async-start(f32[4,2048,32]{1,2,0:T(8,128)} %broadcast_in_dim.15), calls=%async_computation | async-start | bytes 2097152 | tf_op jit(solution)/shard_map/all_to_all | solution.py:19
  29.2 2.2 copy-start
  84.9 33.9 %all-to-all-start.4 = ((f32[8,256,256]{2,1,0:T(8,128)}), f32[8,256,256]{2,1,0:T(8,128)S(1)}, u32[]{:S(2)}, u32[]{:S(2)}) async-start(f32[8,256,256]{2,1,0:T(8,128)} %broadcast_in_dim.19), calls=%async_computation.4 | async-start | bytes 4194304 | tf_op jit(solution)/shard_map/all_to_all | solution.py:19
  245.7 57.5 %all-to-all-start.6 = ((f32[64,32,256]{2,1,0:T(8,128)}), f32[64,32,256]{2,1,0:T(8,128)}, u32[]{:S(2)}, u32[]{:S(2)}) async-start(f32[64,32,256]{2,1,0:T(8,128)} %broadcast_in_dim.20), calls=%async_computation.6 | async-start | bytes 4194304 | tf_op jit(solution)/shard_map/all_to_all | solution.py:19
  305.7 13.4 %all-to-all-start.7 = ((f32[4,1,256]{2,1,0:T(1,128)}), f32[4,1,256]{2,1,0:T(1,128)S(1)}, u32[]{:S(2)}, u32[]{:S(2)}) async-start(f32[4,1,256]{2,1,0:T(1,128)} %broadcast_in_dim.21), calls=%async_computation.7 | async-start | bytes 8192 | tf_op jit(solution)/shard_map/all_to_all | solution.py:19
where the time goes:
time: 329 us
  blocking collectives  112 us (34%)
  waiting for transfers between devices  80.4 us (24%)
  other arithmetic  61.8 us (19%)
  matrix products  30.7 us (9%)
  starting transfers between devices  21.8 us (7%)
  local copies, waits for them, and re-layouts  19.4 us (6%)
    all_to_all x2, blocking collectives, sum_at_owner(): lax.all_to_all(blocks, axis, split_axis=0, concat_axis=0, tiled=True)  82.8 us
    all_to_all x4, waiting for transfers between devices, from_everyone(): lax.all_to_all(jnp.broadcast_to(value[None], (size, *value.shape)), axis,...  80.4 us
    another operation x6, other arithmetic, local(): chol = jnp.linalg.cholesky(gram)  34 us
    all_to_all x2, blocking collectives, from_everyone(): lax.all_to_all(jnp.broadcast_to(value[None], (size, *value.shape)), axis,...  29.7 us
    all_to_all x4, starting transfers between devices, from_everyone(): lax.all_to_all(jnp.broadcast_to(value[None], (size, *value.shape)), axis,...  21.8 us
    another operation x3, other arithmetic, local(): lax.linalg.triangular_solve(chol, left, left_side=False, lower=True, tran...  19.9 us
    dot_general x1, matrix products, local(): jnp.dot(ortho, right.T, precision=HIGH, preferred_element_type=jnp.float32)  9.91 us
    dot_general x1, matrix products, local(): jnp.dot(ortho, basis_full.T, precision=HIGH, preferred_element_type=jnp.f...  7.99 us
  transfers between devices with their start and end apart: 4, of which 3 were waited for; matrix products, arithmetic and copies ran while one was open for 6% of the time, Pallas kernels for 0%

commit v1 on v0

v1 whole, which is shorter than its diff:
```python
import functools
import jax, jax.numpy as jnp
from jax import lax
from jax.experimental import pallas as pl
from jax.experimental.pallas import tpu as pltpu
from jax.sharding import Mesh
from jax.sharding import PartitionSpec as P

M_ROWS = 4096
NCOLS = 8192
HIGH = lax.Precision.HIGHEST
RANK = 256
LEAF = 64

def leaf_inverse(block):
    side = block.shape[0]
    groups = side // 8
    lane = lax.broadcasted_iota(jnp.int32, (side, side), 1)
    line = lax.broadcasted_iota(jnp.int32, (side, side), 0)
    unit = jnp.where(lane == line, 1.0, 0.0).astype(jnp.float32)
    both = jnp.concatenate([block, unit], axis=1)
    tiles = [both[8 * g : 8 * g + 8] for g in range(groups)]
    width = 2 * side
    sub = lax.broadcasted_iota(jnp.int32, (8, width), 0)
    scales = [jnp.zeros((8, width), jnp.float32) for _ in range(groups)]
    for k in range(side):
        own, at = divmod(k, 8)
        row = jnp.broadcast_to(tiles[own][at : at + 1], (8, width))
        pivot = jnp.broadcast_to(row[:, k : k + 1], (8, width))
        scales[own] = jnp.where(sub == at, pivot, scales[own])
        if k == side - 1:
            break
        scaled = row / pivot
        for g in range(own, groups):
            if g == own and at == 7:
                continue
            column = jnp.broadcast_to(tiles[g][:, k : k + 1], (8, width))
            if g == own:
                column = jnp.where(sub > at, column, 0.0)
            tiles[g] = tiles[g] - column * scaled
    full = jnp.concatenate([t[:, side:] * lax.rsqrt(s)[:, side:] for t, s in zip(tiles, scales)], axis=0)
    return full

def factor_kernel(first, last, gram_ref, inv_ref, gram_out, inv_out):
    gram_out[...] = gram_ref[...]
    inv_out[...] = inv_ref[...]
    for i in range(first, last):
        lo, hi = i * LEAF, (i + 1) * LEAF
        leaf = leaf_inverse(gram_out[lo:hi, lo:hi])
        rows_g = jnp.dot(leaf, gram_out[lo:hi, :], precision=HIGH, preferred_element_type=jnp.float32)
        rows_i = jnp.dot(leaf, inv_out[lo:hi, :], precision=HIGH, preferred_element_type=jnp.float32)
        inv_out[lo:hi, :] = rows_i
        if hi < RANK:
            cols = rows_g[:, hi:] if hi % 128 == 0 else rows_g[:, hi - 64:]
            tall = cols.T
            if hi % 128: tall = tall[64:]
            gram_out[hi:, :] = gram_out[hi:, :] - jnp.dot(tall, rows_g, precision=HIGH, preferred_element_type=jnp.float32)
            inv_out[hi:, :] = inv_out[hi:, :] - jnp.dot(tall, rows_i, precision=HIGH, preferred_element_type=jnp.float32)

def factor_part(gram, inv, first, last):
    shape = jax.ShapeDtypeStruct((RANK, RANK), jnp.float32)
    return pl.pallas_call(
        functools.partial(factor_kernel, first, last),
        out_shape=(shape, shape),
        compiler_params=pltpu.CompilerParams(vmem_limit_bytes=16 << 20),
        cost_estimate=pl.CostEstimate(flops=0, bytes_accessed=(last-first)*15_000_000, transcendentals=0),
    )(gram, inv)


def to_everyone(value, axis):
    size = lax.axis_size(axis)
    return lax.all_to_all(
        jnp.broadcast_to(value[None], (size, *value.shape)), axis, 0, 0, tiled=True
    )


def stacked(value, axis):
    blocks = to_everyone(value, axis)
    return blocks.reshape(blocks.shape[0] * blocks.shape[1], *blocks.shape[2:])


def scattered_sum(value, axis):
    size = lax.axis_size(axis)
    blocks = value.reshape(size, value.shape[0] // size, *value.shape[1:])
    return lax.all_to_all(blocks, axis, 0, 0, tiled=True).sum(axis=0)


def swapped(value):
    return lax.ppermute(value, "core", [(0, 1), (1, 0)])


def core_scattered(value):
    half = value.shape[0] // 2
    core = lax.axis_index("core")
    sent = lax.dynamic_slice_in_dim(value, (1 - core) * half, half, 0)
    kept = lax.dynamic_slice_in_dim(value, core * half, half, 0)
    return kept + swapped(sent)


def core_joined(value):
    other = swapped(value)
    first = lax.axis_index("core") == 0
    return jnp.concatenate([jnp.where(first, value, other), jnp.where(first, other, value)], axis=0)


def pair_sum(value, mask):
    return value + lax.ppermute(value, "y", [(i, i ^ mask) for i in range(4)])


def product(a, b, dims):
    return lax.dot_general(a, b, (dims, ((), ())), precision=HIGH, preferred_element_type=jnp.float32)


def local(gradient, momentum, basis):
    replicas = lax.axis_size("replica")
    rank_local = basis.shape[1]
    buffer = momentum[0] + gradient[0].astype(jnp.float32)

    lines = to_everyone(basis.T, "y")
    other = swapped(lines)
    first = lax.axis_index("core") == 0
    both = jnp.stack([jnp.where(first, lines, other), jnp.where(first, other, lines)], axis=1)
    basis_t = both.reshape(RANK, basis.shape[0])

    part = product(buffer, basis_t, ((1,), (1,)))
    own = scattered_sum(scattered_sum(part, "tensor"), "replica") / replicas
    left = stacked(stacked(own, "replica"), "tensor")

    gram = core_scattered(product(left, left, ((0,), (0,))))
    gram = core_joined(pair_sum(pair_sum(gram, 1), 3))
    inverse = jnp.eye(RANK, dtype=jnp.float32)
    for i in range(RANK // LEAF):
        gram, inverse = factor_part(gram, inverse, i, i + 1)

    raw = product(left, buffer, ((0,), (0,)))
    own = scattered_sum(core_scattered(raw), "y")
    size = own.shape[1] // replicas
    pieces = own.reshape(own.shape[0], replicas, size).swapaxes(0, 1)
    piece = lax.all_to_all(pieces, "replica", 0, 0, tiled=True).sum(axis=0) / replicas
    pieces = to_everyone(piece, "replica")
    own = pieces.swapaxes(0, 1).reshape(own.shape)
    raw = core_joined(stacked(own, "y"))

    right = product(inverse, raw, ((1,), (0,)))
    ortho = product(left, inverse, ((1,), (1,)))
    squares = to_everyone(jnp.sum(right * right, axis=1)[None], "tensor").sum(axis=0)[0]
    norms = jnp.sqrt(squares + 1e-12)
    lowrank = product(ortho, right, ((1,), (0,)))
    momentum_new = (buffer - 0.05 * lowrank)[None]
    scale = (M_ROWS * NCOLS / RANK) ** 0.5
    update = (scale * product(ortho / norms[None], right, ((1,), (0,)))).astype(jnp.bfloat16)
    offset = (lax.axis_index("y") * 2 + lax.axis_index("core")) * rank_local
    mine = lax.dynamic_slice_in_dim(right, offset, rank_local, 0)
    basis_new = (mine / lax.dynamic_slice_in_dim(norms, offset, rank_local, 0)[:, None]).T
    return (update, momentum_new, basis_new)


def solution(mesh):
    finer = Mesh(
        mesh.devices.reshape(4, 2, mesh.shape["tensor"], mesh.shape["replica"]),
        ("y", "core", "tensor", "replica"),
    )
    fsdp = ("y", "core")
    placed = (P("replica", fsdp, "tensor"), P("replica", fsdp, "tensor"), P("tensor", fsdp))
    return jax.shard_map(
        local,
        mesh=finer,
        in_specs=placed,
        out_specs=(P(fsdp, "tensor"), P("replica", fsdp, "tensor"), P("tensor", fsdp)),
        check_vma=False,
    )
```

time: 329 us -> 232 us (0.71)
  waiting for transfers between devices: 80.4 us -> 26.6 us
  other arithmetic: 61.8 us -> 9 us
  Pallas kernels: 0 us -> 36.7 us
  local copies, waits for them, and re-layouts: 19.4 us -> 5.08 us
  blocking collectives: 112 us -> 100 us
  starting transfers between devices: 21.8 us -> 28.5 us
  matrix products: 30.7 us -> 24.1 us
    all_to_all x4 -> x3, waiting for transfers between devices: 80.4 us -> 13.6 us  [to_everyone(): lax.all_to_all(jnp.broadcast_to(value[None], (size, *value.shape)), axis,...]
    another operation x9 -> x2, other arithmetic: 53.9 us -> 2.33 us  [local(): jnp.stack([jnp.where(first, lines, other), jnp.where(first, other, lines)...]
    pallas_call x0 -> x4, Pallas kernels: none -> 36.7 us  [factor_part(): pl.pallas_call(functools.partial(factor_kernel, first, last), out_shape=(...]
    ppermute x0 -> x7, starting transfers between devices: none -> 18.1 us  [the longest x5 16.5 us: swapped(): return lax.ppermute(value, 'core', [(0, 1), (1, 0)])]
    ppermute x0 -> x7, waiting for transfers between devices: none -> 13 us  [the longest x2 9.36 us: pair_sum(): return value + lax.ppermute(value, 'y', [(i, i ^ mask) for i in range(4)])]
    all_to_all x4 -> x7, blocking collectives: 112 us -> 100 us  [the longest x3 46.4 us: scattered_sum(): return lax.all_to_all(blocks, axis, 0, 0, tiled=True).sum(axis=0)]
    all_to_all x4 -> x3, starting transfers between devices: 21.8 us -> 10.5 us  [to_everyone(): lax.all_to_all(jnp.broadcast_to(value[None], (size, *value.shape)), axis,...]
    dot_general x1 -> x0, local copies, waits for them, and re-layouts: 5.35 us -> none  [local(): jnp.dot(buffer.T, ortho, precision=HIGH, preferred_element_type=jnp.float32)]
  transfers between devices with their start and end apart: 4 -> 10, of which waited for: 3 -> 6; matrix products, arithmetic and copies ran while one was open for 6% -> 5% of each run, Pallas kernels for 0% -> 16%
where the time goes in v1:
time: 232 us; the launch traced here: 231 us
  blocking collectives  100 us (43%)
  Pallas kernels  36.7 us (16%)
  starting transfers between devices  28.5 us (12%)
  waiting for transfers between devices  26.6 us (11%)
  matrix products  24.1 us (10%)
  other arithmetic  9 us (4%)
  local copies, waits for them, and re-layouts  5.08 us (2%)
    all_to_all x3, blocking collectives, scattered_sum(): return lax.all_to_all(blocks, axis, 0, 0, tiled=True).sum(axis=0)  46.4 us
    all_to_all x3, blocking collectives, to_everyone(): lax.all_to_all(jnp.broadcast_to(value[None], (size, *value.shape)), axis,...  41.5 us
    pallas_call x4, Pallas kernels, factor_part(): pl.pallas_call(functools.partial(factor_kernel, first, last), out_shape=(...  36.7 us
    dot_general x7, matrix products, product(): lax.dot_general(a, b, (dims, ((), ())), precision=HIGH, preferred_element...  24.1 us
    ppermute x5, starting transfers between devices, swapped(): return lax.ppermute(value, 'core', [(0, 1), (1, 0)])  16.5 us
    all_to_all x3, waiting for transfers between devices, to_everyone(): lax.all_to_all(jnp.broadcast_to(value[None], (size, *value.shape)), axis,...  13.6 us
    all_to_all x1, blocking collectives, local(): lax.all_to_all(pieces, 'replica', 0, 0, tiled=True).sum(axis=0) / replicas  12.5 us
    all_to_all x3, starting transfers between devices, to_everyone(): lax.all_to_all(jnp.broadcast_to(value[None], (size, *value.shape)), axis,...  10.5 us
  transfers between devices with their start and end apart: 10, of which 6 were waited for; matrix products, arithmetic and copies ran while one was open for 5% of the time, Pallas kernels for 16%

profile of v1, /device:TPU:1, one launch (start us, length us, event | category | flops | bytes accessed | tf_op | source)
XLA Modules:
  0.0 231.3 jit_solution(4756223071597727381)
XLA Ops:
  0.6 1.2 broadcast_in_dim.18
  1.8 19.0 %all_to_all.50 = f32[4,32,2048]{2,1,0:T(8,128)S(1)} all-to-all(f32[4,32,2048]{2,1,0:T(8,128)S(1)} %broadcast_in_dim.18), channel_id=1, replica_groups=mesh['y'=4,'core'=2,'tensor'=4,'replica'=8] {'y'}, dimensions={0} | all-to-all | bytes 2097152 | tf_op jit(solution)/shard_map/all_to_all | solution.py:72
  20.8 1.9 collective-permute-start
  22.7 2.8 %convert_add_fusion = f32[1,512,2048]{2,1,0:T(8,128)S(1)} fusion(f32[1,512,2048]{2,1,0:T(8,128)} %param.4, bf16[1,512,2048]{2,1,0:T(8,128)(2,1)S(1)} %copy-done.1), kind=kLoop, calls=%fused_computation.5 | loop fusion | flops 2097152 | bytes 10485760 | tf_op jit(solution)/shard_map/add | solution.py:117
  25.5 2.2 select_bitcast_fusion.1
  27.7 0.1 pad_maximum_fusion
  27.9 3.5 %fusion.11 = f32[4,128,256]{2,1,0:T(8,128)S(1)} fusion(f32[4,128,2048]{2,1,0:T(8,128)S(1)} %bitcast.48, f32[256,2048,1]{1,0,2:T(8,128)S(1)} %bitcast.51), kind=kOutput, calls=%fused_computation.33 | convolution fusion | flops 3221225472 | bytes 6815744 | tf_op jit(solution)/shard_map/dot_general | solution.py:111
  31.4 13.1 %all_to_all.51 = f32[4,128,256]{2,1,0:T(8,128)S(1)} all-to-all(f32[4,128,256]{2,1,0:T(8,128)S(1)} %fusion.11), channel_id=1, replica_groups=mesh['y'=4,'core'=2,'tensor'=4,'replica'=8] {'tensor'}, dimensions={0} | all-to-all | bytes 1048576 | tf_op jit(solution)/shard_map/all_to_all | solution.py:85
  44.6 16.0 %all_to_all.52 = f32[8,16,256]{2,1,0:T(8,128)S(1)} all-to-all(f32[8,16,256]{2,1,0:T(8,128)S(1)} %bitcast.59), channel_id=1, replica_groups=mesh['y'=4,'core'=2,'tensor'=4,'replica'=8] {'replica'}, dimensions={0} | all-to-all | bytes 262144 | tf_op jit(solution)/shard_map/all_to_all | solution.py:85
  60.6 10.4 %all_to_all.53 = f32[8,16,256]{2,1,0:T(8,128)S(1)} all-to-all(f32[8,16,256]{2,1,0:T(8,128)S(1)} %broadcast_in_dim.19), channel_id=1, replica_groups=mesh['y'=4,'core'=2,'tensor'=4,'replica'=8] {'replica'}, dimensions={0} | all-to-all | bytes 262144 | tf_op jit(solution)/shard_map/all_to_all | solution.py:72
  71.0 0.8 broadcast_in_dim.21
  71.9 3.5 %all-to-all-start.4 = ((f32[4,128,256]{2,1,0:T(8,128)}), f32[4,128,256]{2,1,0:T(8,128)S(1)}, u32[]{:S(2)}, u32[]{:S(2)}) async-start(f32[4,128,256]{2,1,0:T(8,128)} %broadcast_in_dim.21), calls=%async_computation.4 | async-start | bytes 1048576 | tf_op jit(solution)/shard_map/all_to_all | solution.py:72
  75.4 6.9 %all-to-all-done.4 = f32[4,128,256]{2,1,0:T(8,128)S(1)} async-done(((f32[4,128,256]{2,1,0:T(8,128)}), f32[4,128,256]{2,1,0:T(8,128)S(1)}, u32[]{:S(2)}, u32[]{:S(2)}) %all-to-all-start.4) | async-done | bytes 524320 | tf_op jit(solution)/shard_map/all_to_all | solution.py:72
  82.2 5.4 %fusion = f32[256,2048]{1,0:T(8,128)S(1)} fusion(f32[512,256]{1,0:T(8,128)S(1)} %bitcast.49, f32[1,512,2048]{2,1,0:T(8,128)} %copy-done), kind=kOutput, calls=%fused_computation.1 | convolution fusion | flops 3221225472 | bytes 6815744 | tf_op jit(solution)/shard_map/dot_general | solution.py:111
  87.6 1.1 constant_dynamic-slice_fusion
  88.7 4.6 %collective-permute-start.5 = (f32[128,2048]{1,0:T(8,128)}, f32[128,2048]{1,0:T(8,128)}, u32[]{:S(2)}, u32[]{:S(2)}) collective-permute-start(f32[128,2048]{1,0:T(8,128)} %constant_dynamic-slice_fusion), channel_id=1, source_target_pairs={{0,32},{32,0},{1,33},{33,1},{2,34},{34,2},{3,35},{35,3},{4,36},{36... | collective-permute-start | bytes 3145736 | tf_op jit(solution)/shard_map/ppermute | solution.py:89
  93.3 2.6 %collective-permute-done.5 = f32[128,2048]{1,0:T(8,128)} collective-permute-done((f32[128,2048]{1,0:T(8,128)}, f32[128,2048]{1,0:T(8,128)}, u32[]{:S(2)}, u32[]{:S(2)}) %collective-permute-start.5) | collective-permute-done | bytes 1048608 | tf_op jit(solution)/shard_map/ppermute | solution.py:89
  95.9 1.3 dynamic-slice_add_fusion
  97.3 17.3 %all_to_all.54 = f32[4,32,2048]{2,1,0:T(8,128)S(1)} all-to-all(f32[4,32,2048]{2,1,0:T(8,128)S(1)} %bitcast.53), channel_id=1, replica_groups=mesh['y'=4,'core'=2,'tensor'=4,'replica'=8] {'y'}, dimensions={0} | all-to-all | bytes 2097152 | tf_op jit(solution)/shard_map/all_to_all | solution.py:85
  114.6 0.1 copy.26
  114.7 0.1 copy.20
  114.8 12.5 %all_to_all.55 = f32[8,32,256]{2,1,0:T(8,128)S(1)} all-to-all(f32[8,32,256]{2,1,0:T(8,128)S(1)} %copy.20), channel_id=1, replica_groups=mesh['y'=4,'core'=2,'tensor'=4,'replica'=8] {'replica'}, dimensions={0} | all-to-all | bytes 524288 | tf_op jit(solution)/shard_map/all_to_all | solution.py:139
  127.4 12.1 %all_to_all.56 = f32[8,32,256]{2,1,0:T(8,128)S(1)} all-to-all(f32[8,32,256]{2,1,0:T(8,128)S(1)} %broadcast_in_dim.22), channel_id=1, replica_groups=mesh['y'=4,'core'=2,'tensor'=4,'replica'=8] {'replica'}, dimensions={0} | all-to-all | bytes 524288 | tf_op jit(solution)/shard_map/all_to_all | solution.py:72
  139.5 1.1 broadcast_in_dim.48
  140.6 3.5 %all-to-all-start.8 = ((f32[4,32,2048]{2,1,0:T(8,128)}), f32[4,32,2048]{2,1,0:T(8,128)S(1)}, u32[]{:S(2)}, u32[]{:S(2)}) async-start(f32[4,32,2048]{2,1,0:T(8,128)} %broadcast_in_dim.48), calls=%async_computation.8 | async-start | bytes 2097152 | tf_op jit(solution)/shard_map/all_to_all | solution.py:72
  144.1 1.0 convolution_bitcast_fusion
  145.2 3.6 %collective-permute-start.1 = (f32[128,256]{1,0:T(8,128)S(1)}, f32[128,256]{1,0:T(8,128)S(1)}, u32[]{:S(2)}, u32[]{:S(2)}) collective-permute-start(f32[128,256]{1,0:T(8,128)S(1)} %constant_dynamic-slice_fusion.1), channel_id=1, source_target_pairs={{0,32},{32,0},{1,33},{33,1},{2,34},{34,2},{3,35},{35,3},{4,36},{36... | collective-permute-start | bytes 393224 | tf_op jit(solution)/shard_map/ppermute | solution.py:89
  148.7 6.7 %all-to-all-done.8 = f32[4,32,2048]{2,1,0:T(8,128)S(1)} async-done(((f32[4,32,2048]{2,1,0:T(8,128)}), f32[4,32,2048]{2,1,0:T(8,128)S(1)}, u32[]{:S(2)}, u32[]{:S(2)}) %all-to-all-start.8) | async-done | bytes 1048608 | tf_op jit(solution)/shard_map/all_to_all | solution.py:72
  155.5 4.7 %collective-permute-start.6 = (f32[128,2048]{1,0:T(8,128)S(1)}, f32[128,2048]{1,0:T(8,128)}, u32[]{:S(2)}, u32[]{:S(2)}) collective-permute-start(f32[128,2048]{1,0:T(8,128)S(1)} %bitcast.52), channel_id=1, source_target_pairs={{0,32},{32,0},{1,33},{33,1},{2,34},{34,2},{3,35},{35,3},{4,36},{36... | collective-permute-start | bytes 3145736 | tf_op jit(solution)/shard_map/ppermute | solution.py:89
  160.2 0.6 collective-permute-start.2
  160.7 4.8 %collective-permute-done.2 = f32[128,256]{1,0:T(8,128)S(1)} collective-permute-done((f32[128,256]{1,0:T(8,128)S(1)}, f32[128,256]{1,0:T(8,128)S(1)}, u32[]{:S(2)}, u32[]{:S(2)}) %collective-permute-start.2) | collective-permute-done | bytes 131104 | tf_op jit(solution)/shard_map/ppermute | solution.py:107
  165.6 1.0 collective-permute-start.3
  166.6 4.5 %collective-permute-done.3 = f32[128,256]{1,0:T(8,128)S(1)} collective-permute-done((f32[128,256]{1,0:T(8,128)S(1)}, f32[128,256]{1,0:T(8,128)S(1)}, u32[]{:S(2)}, u32[]{:S(2)}) %collective-permute-start.3) | collective-permute-done | bytes 131104 | tf_op jit(solution)/shard_map/ppermute | solution.py:107
  171.1 1.8 collective-permute-start.4
  172.9 1.0 collective-permute-done.4
  173.9 9.2 %shard_map.58 = (f32[256,256]{1,0:T(8,128)S(1)}, f32[256,256]{1,0:T(8,128)S(1)}) custom-call(f32[256,256]{1,0:T(8,128)S(1)} %pad_maximum_fusion.1.gram_ref, f32[256,256]{1,0:T(8,128)S(1)} %fusion.9.inv_ref), custom_call_target="tpu_custom_call" | custom-call | bytes 15000000 | tf_op jit(solution)/shard_map/pallas_call | solution.py:62
  183.2 9.2 %shard_map.59 = (f32[256,256]{1,0:T(8,128)S(1)}, f32[256,256]{1,0:T(8,128)S(1)}) custom-call(f32[256,256]{1,0:T(8,128)S(1)} %get-tuple-element.10.gram_ref, f32[256,256]{1,0:T(8,128)S(1)} %get-tuple-element.11.inv_ref), custom_call_target="tpu_custom_call" | custom-call | bytes 15000000 | tf_op jit(solution)/shard_map/pallas_call | solution.py:62
  192.3 9.0 %shard_map.60 = (f32[256,256]{1,0:T(8,128)S(1)}, f32[256,256]{1,0:T(8,128)S(1)}) custom-call(f32[256,256]{1,0:T(8,128)S(1)} %get-tuple-element.12.gram_ref, f32[256,256]{1,0:T(8,128)S(1)} %get-tuple-element.13.inv_ref), custom_call_target="tpu_custom_call" | custom-call | bytes 15000000 | tf_op jit(solution)/shard_map/pallas_call | solution.py:62
  201.3 9.3 %shard_map.61 = (f32[256,256]{1,0:T(8,128)}, f32[256,256]{1,0:T(8,128)S(1)}) custom-call(f32[256,256]{1,0:T(8,128)S(1)} %get-tuple-element.14.gram_ref, f32[256,256]{1,0:T(8,128)S(1)} %get-tuple-element.15.inv_ref), custom_call_target="tpu_custom_call" | custom-call | bytes 15000000 | tf_op jit(solution)/shard_map/pallas_call | solution.py:62
  210.6 0.6 fusion.12
  211.3 1.5 broadcast_select_fusion.1
  212.7 2.0 multiply_reduce_fusion
  214.8 0.6 broadcast_in_dim.49
  215.4 3.5 %all-to-all-start.9 = ((f32[4,1,256]{2,1,0:T(1,128)}), f32[4,1,256]{2,1,0:T(1,128)S(1)}, u32[]{:S(2)}, u32[]{:S(2)}) async-start(f32[4,1,256]{2,1,0:T(1,128)} %broadcast_in_dim.49), calls=%async_computation.9 | async-start | bytes 8192 | tf_op jit(solution)/shard_map/all_to_all | solution.py:72
  218.8 6.8 %fusion.2 = f32[1,512,2048]{2,1,0:T(8,128)} fusion(f32[1,512,2048]{2,1,0:T(8,128)} %copy-done, f32[512,256]{1,0:T(8,128)S(1)} %fusion.12, f32[256,2048]{1,0:T(8,128)S(1)} %get-tuple-element.24), kind=kOutput, calls=%fused_computation.3 | convolution fusion | flops 3223322624 | bytes 11010048 | tf_op jit(solution)/shard_map/dot_general | solution.py:111
  225.7 4.7 %multiply_convert_fusion = bf16[512,2048]{1,0:T(8,128)(2,1)} fusion(f32[256,2048]{1,0:T(8,128)S(1)} %get-tuple-element.24, f32[512,256]{1,0:T(8,128)S(1)} %fusion.12, f32[256]{0:T(256)S(1)} %add_sqrt_fusion), kind=kOutput, calls=%fused_computation.4 | convolution fusion | flops 3223453696 | bytes 4719616 | tf_op jit(solution)/shard_map/dot_general | solution.py:111
  230.4 0.1 dynamic_slice.23
  230.5 0.8 divide_bitcast_fusion
  (26 shorter events, 0.4 us)
Async XLA Ops:
  0.6 22.1 %copy-start.1 = (bf16[1,512,2048]{2,1,0:T(8,128)(2,1)S(1)}, bf16[1,512,2048]{2,1,0:T(8,128)(2,1)}, u32[]{:S(2)}) copy-start(bf16[1,512,2048]{2,1,0:T(8,128)(2,1)} %param.3) | copy-start | bytes 6291460
  20.8 4.7 %collective-permute-start = (f32[4,32,2048]{2,1,0:T(8,128)S(1)}, f32[4,32,2048]{2,1,0:T(8,128)}, u32[]{:S(2)}, u32[]{:S(2)}) collective-permute-start(f32[4,32,2048]{2,1,0:T(8,128)S(1)} %all_to_all.50), channel_id=1, source_target_pairs={{0,32},{32,0},{1,33},{33,1},{2,34},{34,2},{3,35},{35,3},{4,36},{36... | collective-permute-start | bytes 3145736 | tf_op jit(solution)/shard_map/ppermute | solution.py:89
  25.5 2.4 %copy-start = (f32[1,512,2048]{2,1,0:T(8,128)}, f32[1,512,2048]{2,1,0:T(8,128)S(1)}, u32[]{:S(2)}) copy-start(f32[1,512,2048]{2,1,0:T(8,128)S(1)} %convert_add_fusion) | copy-start | bytes 12582916
  71.9 10.4 %all-to-all-start.4 = ((f32[4,128,256]{2,1,0:T(8,128)}), f32[4,128,256]{2,1,0:T(8,128)S(1)}, u32[]{:S(2)}, u32[]{:S(2)}) async-start(f32[4,128,256]{2,1,0:T(8,128)} %broadcast_in_dim.21), calls=%async_computation.4 | async-start | bytes 1048576 | tf_op jit(solution)/shard_map/all_to_all | solution.py:72
  88.7 7.3 %collective-permute-start.5 = (f32[128,2048]{1,0:T(8,128)}, f32[128,2048]{1,0:T(8,128)}, u32[]{:S(2)}, u32[]{:S(2)}) collective-permute-start(f32[128,2048]{1,0:T(8,128)} %constant_dynamic-slice_fusion), channel_id=1, source_target_pairs={{0,32},{32,0},{1,33},{33,1},{2,34},{34,2},{3,35},{35,3},{4,36},{36... | collective-permute-start | bytes 3145736 | tf_op jit(solution)/shard_map/ppermute | solution.py:89
  140.6 14.8 %all-to-all-start.8 = ((f32[4,32,2048]{2,1,0:T(8,128)}), f32[4,32,2048]{2,1,0:T(8,128)S(1)}, u32[]{:S(2)}, u32[]{:S(2)}) async-start(f32[4,32,2048]{2,1,0:T(8,128)} %broadcast_in_dim.48), calls=%async_computation.8 | async-start | bytes 2097152 | tf_op jit(solution)/shard_map/all_to_all | solution.py:72
  145.2 15.0 %collective-permute-start.1 = (f32[128,256]{1,0:T(8,128)S(1)}, f32[128,256]{1,0:T(8,128)S(1)}, u32[]{:S(2)}, u32[]{:S(2)}) collective-permute-start(f32[128,256]{1,0:T(8,128)S(1)} %constant_dynamic-slice_fusion.1), channel_id=1, source_target_pairs={{0,32},{32,0},{1,33},{33,1},{2,34},{34,2},{3,35},{35,3},{4,36},{36... | collective-permute-start | bytes 393224 | tf_op jit(solution)/shard_map/ppermute | solution.py:89
  155.5 55.8 %collective-permute-start.6 = (f32[128,2048]{1,0:T(8,128)S(1)}, f32[128,2048]{1,0:T(8,128)}, u32[]{:S(2)}, u32[]{:S(2)}) collective-permute-start(f32[128,2048]{1,0:T(8,128)S(1)} %bitcast.52), channel_id=1, source_target_pairs={{0,32},{32,0},{1,33},{33,1},{2,34},{34,2},{3,35},{35,3},{4,36},{36... | collective-permute-start | bytes 3145736 | tf_op jit(solution)/shard_map/ppermute | solution.py:89
  160.2 5.4 %collective-permute-start.2 = (f32[128,256]{1,0:T(8,128)S(1)}, f32[128,256]{1,0:T(8,128)S(1)}, u32[]{:S(2)}, u32[]{:S(2)}) collective-permute-start(f32[128,256]{1,0:T(8,128)S(1)} %dynamic-slice_add_fusion.1), channel_id=1, source_target_pairs={{0,64},{64,0},{128,192},{192,128},{1,65},{65,1},{129,193},{193,129... | collective-permute-start | bytes 393224 | tf_op jit(solution)/shard_map/ppermute | solution.py:107
  165.6 5.5 %collective-permute-start.3 = (f32[128,256]{1,0:T(8,128)S(1)}, f32[128,256]{1,0:T(8,128)S(1)}, u32[]{:S(2)}, u32[]{:S(2)}) collective-permute-start(f32[128,256]{1,0:T(8,128)S(1)} %add.53), channel_id=1, source_target_pairs={{0,192},{64,128},{128,64},{192,0},{1,193},{65,129},{129,65},{193,1... | collective-permute-start | bytes 393224 | tf_op jit(solution)/shard_map/ppermute | solution.py:107
  171.1 2.7 %collective-permute-start.4 = (f32[128,256]{1,0:T(8,128)S(1)}, f32[128,256]{1,0:T(8,128)S(1)}, u32[]{:S(2)}, u32[]{:S(2)}) collective-permute-start(f32[128,256]{1,0:T(8,128)S(1)} %add.54), channel_id=1, source_target_pairs={{0,32},{32,0},{1,33},{33,1},{2,34},{34,2},{3,35},{35,3},{4,36},{36... | collective-permute-start | bytes 393224 | tf_op jit(solution)/shard_map/ppermute | solution.py:89
  215.4 10.2 %all-to-all-start.9 = ((f32[4,1,256]{2,1,0:T(1,128)}), f32[4,1,256]{2,1,0:T(1,128)S(1)}, u32[]{:S(2)}, u32[]{:S(2)}) async-start(f32[4,1,256]{2,1,0:T(1,128)} %broadcast_in_dim.49), calls=%async_computation.9 | async-start | bytes 8192 | tf_op jit(solution)/shard_map/all_to_all | solution.py:72

commit v2 on v1

v2 whole, which is shorter than its diff:
```python
import functools
import jax, jax.numpy as jnp
from jax import lax
from jax.experimental import pallas as pl
from jax.experimental.pallas import tpu as pltpu
from jax.sharding import Mesh
from jax.sharding import PartitionSpec as P

M_ROWS = 4096
NCOLS = 8192
HIGH = lax.Precision.HIGHEST
RANK = 256
LEAF = 64

def inverted(value):
    near = pl.reciprocal(value, approx=True)
    near = near * (2.0 - value * near)
    return near * (2.0 - value * near)


def leaf_inverse(block):
    side = block.shape[0]
    lane = lax.broadcasted_iota(jnp.int32, (side, side), 1)
    line = lax.broadcasted_iota(jnp.int32, (side, side), 0)
    both = jnp.concatenate([block, jnp.where(lane == line, 1.0, 0.0)], axis=1)
    tiles = [both[at : at + 8] for at in range(0, side, 8)]
    tile = (8, 2 * side)
    sub = lax.broadcasted_iota(jnp.int32, tile, 0)
    for own, rows in enumerate(tiles):
        base = 8 * own
        pivots = [
            [jnp.broadcast_to(rows[i : i + 1, base + j : base + j + 1], tile) for j in range(i + 1)]
            for i in range(8)
        ]
        columns = [
            [jnp.broadcast_to(t[:, base + j : base + j + 1], tile) for j in range(8)]
            for t in tiles[own + 1 :]
        ]
        done = [jnp.broadcast_to(rows[i : i + 1], tile) for i in range(8)]
        lower, inverses = {}, []
        for j in range(8):
            inverse = inverted(pivots[j][j])
            inverses.append(inverse)
            for i in range(j + 1, 8):
                lower[i, j] = pivots[i][j] * inverse
            for i in range(j + 1, 8):
                for m in range(j + 1, i + 1):
                    pivots[i][m] = pivots[i][m] - lower[i, j] * pivots[m][j]
                done[i] = done[i] - lower[i, j] * done[j]
        if own + 1 < len(tiles):
            solved = [None] * 8
            for i in reversed(range(8)):
                solved[i] = done[i] * inverses[i]
                for m in range(i + 1, 8):
                    solved[i] = solved[i] - lower[m, i] * solved[m]
            for g, column in enumerate(columns, own + 1):
                total = column[7] * solved[7]
                for j in reversed(range(7)):
                    total = total + column[j] * solved[j]
                tiles[g] = tiles[g] - total
        final = done[0] * lax.rsqrt(pivots[0][0])
        for i in range(1, 8):
            final = jnp.where(sub == i, done[i] * lax.rsqrt(pivots[i][i]), final)
        tiles[own] = final
    return jnp.concatenate([t[:, side:] for t in tiles], axis=0)


def factor_kernel(first, last, gram_ref, inv_ref, gram_out, inv_out):
    gram_out[...] = gram_ref[...]
    inv_out[...] = inv_ref[...]
    for i in range(first, last):
        lo, hi = i * LEAF, (i + 1) * LEAF
        leaf = leaf_inverse(gram_out[lo:hi, lo:hi])
        rows_g = jnp.dot(leaf, gram_out[lo:hi, :], precision=HIGH, preferred_element_type=jnp.float32)
        rows_i = jnp.dot(leaf, inv_out[lo:hi, :], precision=HIGH, preferred_element_type=jnp.float32)
        inv_out[lo:hi, :] = rows_i
        if hi < RANK:
            cols = rows_g[:, hi:] if hi % 128 == 0 else rows_g[:, hi - 64:]
            tall = cols.T
            if hi % 128: tall = tall[64:]
            gram_out[hi:, :] = gram_out[hi:, :] - jnp.dot(tall, rows_g, precision=HIGH, preferred_element_type=jnp.float32)
            inv_out[hi:, :] = inv_out[hi:, :] - jnp.dot(tall, rows_i, precision=HIGH, preferred_element_type=jnp.float32)

def factor_part(gram, inv, first, last):
    shape = jax.ShapeDtypeStruct((RANK, RANK), jnp.float32)
    return pl.pallas_call(
        functools.partial(factor_kernel, first, last),
        out_shape=(shape, shape),
        compiler_params=pltpu.CompilerParams(vmem_limit_bytes=16 << 20),
        cost_estimate=pl.CostEstimate(flops=0, bytes_accessed=(last-first)*15_000_000, transcendentals=0),
    )(gram, inv)

def to_everyone(value, axis):
    size = lax.axis_size(axis)
    return lax.all_to_all(
        jnp.broadcast_to(value[None], (size, *value.shape)), axis, 0, 0, tiled=True
    )


def stacked(value, axis):
    blocks = to_everyone(value, axis)
    return blocks.reshape(blocks.shape[0] * blocks.shape[1], *blocks.shape[2:])


def parted(value, axis):
    size = lax.axis_size(axis)
    blocks = value.reshape(size, value.shape[0] // size, *value.shape[1:])
    return lax.all_to_all(blocks, axis, 0, 0, tiled=True)


def scattered_sum(value, axis):
    return parted(value, axis).sum(axis=0)


def together(*values):
    return lax.optimization_barrier(values)


def swapped(value):
    return lax.ppermute(value, "core", [(0, 1), (1, 0)])


def core_scattered(value):
    half = value.shape[0] // 2
    core = lax.axis_index("core")
    sent = lax.dynamic_slice_in_dim(value, (1 - core) * half, half, 0)
    kept = lax.dynamic_slice_in_dim(value, core * half, half, 0)
    return kept + swapped(sent)


def core_joined(value):
    other = swapped(value)
    first = lax.axis_index("core") == 0
    return jnp.concatenate([jnp.where(first, value, other), jnp.where(first, other, value)], axis=0)


def pair_sum(value, mask, axis="y"):
    return value + lax.ppermute(value, axis, [(i, i ^ mask) for i in range(4)])


def product(a, b, dims, precision=HIGH):
    return lax.dot_general(a, b, (dims, ((), ())), precision=precision, preferred_element_type=jnp.float32)

def split(value):
    high = value.astype(jnp.bfloat16)
    return high, (value - high.astype(jnp.float32)).astype(jnp.bfloat16)


def three_dots(a, b):
    (a_high, a_low), (b_high, b_low) = a, b

    def dot(one, two):
        return jnp.dot(one, two, preferred_element_type=jnp.float32)

    return dot(a_high, b_high) + (dot(a_high, b_low) + dot(a_low, b_high))


WIDE = 256
IN_VMEM = pl.BlockSpec(memory_space=pltpu.VMEM)
IN_SMEM = pl.BlockSpec(memory_space=pltpu.SMEM)
ANYWHERE = pl.BlockSpec(memory_space=pl.ANY)


def block_of(ref, index):
    return ref.at[:, pl.ds(pl.multiple_of(index * WIDE, WIDE), WIDE)]


def call(kernel, flops, moved, **rest):
    return pl.pallas_call(
        kernel,
        compiler_params=pltpu.CompilerParams(vmem_limit_bytes=24 << 20),
        cost_estimate=pl.CostEstimate(flops=flops, bytes_accessed=moved, transcendentals=0),
        **rest,
    )


def right_kernel(half_ref, left_ref, buffer_ref, out_ref):
    count = out_ref.shape[0]
    left = split(left_ref[...].T)
    for i in range(count):
        block = block_of(buffer_ref, half_ref[0] * count + i)[...]
        out_ref[i] = three_dots(left, split(block))


def right_half(half, left, buffer):
    rows, columns = buffer.shape
    return call(
        right_kernel,
        3 * rows * RANK * columns,
        4 * rows * columns,
        in_specs=[IN_SMEM, IN_VMEM, IN_VMEM],
        out_specs=IN_VMEM,
        out_shape=jax.ShapeDtypeStruct((columns // WIDE // 2, RANK, WIDE), jnp.float32),
    )(half, left, buffer)


def own_kernel(inverse_ref, raw_ref, wide_ref, squares_ref):
    right = jnp.dot(inverse_ref[...], raw_ref[...], precision=HIGH, preferred_element_type=jnp.float32)
    for i in range(wide_ref.shape[0]):
        wide_ref[i] = right
    squares_ref[...] = lax.dot_general(
        jnp.ones((8, WIDE), jnp.float32),
        right * right,
        (((1,), (1,)), ((), ())),
        precision=HIGH,
        preferred_element_type=jnp.float32,
    )


def own_right(inverse, raw, copies):
    return call(
        own_kernel,
        RANK**3,
        RANK * RANK * 32,
        in_specs=[IN_VMEM, IN_VMEM],
        out_specs=(IN_VMEM, IN_VMEM),
        out_shape=(
            jax.ShapeDtypeStruct((copies, RANK, WIDE), jnp.float32),
            jax.ShapeDtypeStruct((8, RANK), jnp.float32),
        ),
    )(inverse, raw)


def change_block(ortho, right, buffer_ref, index, slot_ref, out_ref, sem):
    slot_ref[...] = block_of(buffer_ref, index)[...] + three_dots(ortho, right)
    copy = pltpu.make_async_copy(slot_ref, block_of(out_ref, index), sem)
    copy.start()
    return copy


def first_kernel(half_ref, ortho_ref, right_ref, buffer_ref, out_ref, slots, sems):
    count = right_ref.shape[0]
    ortho = split(ortho_ref[...] * -0.05)
    copies = []
    for i in range(count):
        index = half_ref[0] * count + i
        right = split(right_ref[i])
        copies.append(change_block(ortho, right, buffer_ref, index, slots.at[i], out_ref, sems.at[i]))
    for copy in copies:
        copy.wait()


def first_half(half, ortho, right, buffer):
    rows, columns = buffer.shape
    count = right.shape[0]
    return call(
        first_kernel,
        3 * rows * RANK * columns,
        4 * rows * columns,
        in_specs=[IN_SMEM, IN_VMEM, IN_VMEM, IN_VMEM],
        out_specs=ANYWHERE,
        out_shape=jax.ShapeDtypeStruct((rows, columns), jnp.float32),
        scratch_shapes=[pltpu.VMEM((count, rows, WIDE), jnp.float32), pltpu.SemaphoreType.DMA((count,))],
    )(half, ortho, right, buffer)


def last_kernel(
    place_ref, ortho_ref, mine_ref, other_ref, buffer_ref, squares_ref, filled_ref,
    out_ref, update_ref, lines_ref, column_ref, slots, small, sems, small_sems,
):
    core, offset = place_ref[0], pl.multiple_of(place_ref[1], 32)
    count = mine_ref.shape[0]
    norms = jnp.sqrt(squares_ref[...] + 1e-12)
    column_ref[...] = jnp.concatenate([norms] * 16, axis=0).T
    own_norms = column_ref[pl.ds(offset, 32), :][:, :1]
    ortho = split(ortho_ref[...] * -0.05)
    scaled = split(ortho_ref[...] * ((M_ROWS * NCOLS / RANK) ** 0.5 / norms[:1]))
    copies = []
    for i in range(count):
        index = (1 - core) * count + i
        right = split(other_ref[i])
        copies.append(change_block(ortho, right, buffer_ref, index, slots.at[i], out_ref, sems.at[i]))
    for half, (source, start) in enumerate(((other_ref, (1 - core) * count), (mine_ref, core * count))):
        for i in range(count):
            at = half * count + i
            small[at] = three_dots(scaled, split(source[i])).astype(jnp.bfloat16)
            copy = pltpu.make_async_copy(small.at[at], block_of(update_ref, start + i), small_sems.at[at])
            copy.start()
            copies.append(copy)
            lines = source[i, pl.ds(offset, 32), :] / own_norms
            lines_ref[:, pl.ds(pl.multiple_of((start + i) * WIDE, WIDE), WIDE)] = lines
    for copy in copies:
        copy.wait()


def last_half(place, ortho, mine, other, buffer, squares, filled):
    rows, columns = buffer.shape
    count = mine.shape[0]
    return call(
        last_kernel,
        9 * rows * RANK * columns,
        8 * rows * columns,
        in_specs=[IN_SMEM] + [IN_VMEM] * 5 + [ANYWHERE],
        out_specs=(ANYWHERE, ANYWHERE, IN_VMEM),
        out_shape=(
            jax.ShapeDtypeStruct((rows, columns), jnp.float32),
            jax.ShapeDtypeStruct((rows, columns), jnp.bfloat16),
            jax.ShapeDtypeStruct((32, columns), jnp.float32),
        ),
        scratch_shapes=[
            pltpu.VMEM((RANK, 128), jnp.float32),
            pltpu.VMEM((count, rows, WIDE), jnp.float32),
            pltpu.VMEM((2 * count, rows, WIDE), jnp.bfloat16),
            pltpu.SemaphoreType.DMA((count,)),
            pltpu.SemaphoreType.DMA((2 * count,)),
        ],
        input_output_aliases={6: 0},
    )(place, ortho, mine, other, buffer, squares, filled)


def local(gradient, momentum, basis):
    replicas = lax.axis_size("replica")
    rank_local = basis.shape[1]
    core = lax.axis_index("core")
    first = core == 0
    mine, theirs = jnp.full((1,), core, jnp.int32), jnp.full((1,), 1 - core, jnp.int32)

    wide = jnp.broadcast_to(basis.T[None], (4, rank_local, basis.shape[0]))
    wide, momentum, gradient = together(wide, momentum, gradient)
    lines = lax.all_to_all(wide, "y", 0, 0, tiled=True)
    buffer = momentum[0] + gradient[0].astype(jnp.float32)
    lines, buffer = together(lines, buffer)
    other = swapped(lines)
    both = jnp.stack([jnp.where(first, lines, other), jnp.where(first, other, lines)], axis=1)
    basis_t = both.reshape(RANK, basis.shape[0])

    part = product(buffer, basis_t, ((1,), (1,)), lax.Precision.HIGH)
    own = scattered_sum(scattered_sum(part, "tensor"), "replica") / replicas
    quarter = stacked(own, "replica")
    wide = jnp.broadcast_to(quarter[None], (4, *quarter.shape))
    wide, quarter = together(wide, quarter)
    left = lax.all_to_all(wide, "tensor", 0, 0, tiled=True).reshape(-1, RANK)
    gram = pair_sum(core_scattered(product(quarter, quarter, ((0,), (0,)))), 1)
    left, gram = together(left, gram)
    sent = right_half(theirs, left, buffer)
    gram = pair_sum(gram, 3)
    sent, left = together(sent, left)
    arrived = swapped(sent)
    kept = right_half(mine, left, buffer)
    arrived, kept, gram = together(arrived, kept, gram)
    blocks = lax.all_to_all(arrived + kept, "y", 0, 0, tiled=True)
    gram = core_joined(pair_sum(pair_sum(gram, 1, "tensor"), 3, "tensor"))
    blocks, gram = together(blocks, gram)
    own = blocks.sum(axis=0)
    own, gram = together(own, gram)
    pieces = parted(own, "replica")
    inverse = jnp.eye(RANK, dtype=jnp.float32)
    gram, inverse, pieces = together(*factor_part(gram, inverse, 0, 2), pieces)
    piece = pieces.sum(axis=0) / replicas
    wide = jnp.broadcast_to(piece[None], (replicas, *piece.shape))
    gram, wide = together(gram, wide)
    pieces = lax.all_to_all(wide, "replica", 0, 0, tiled=True)
    gram, inverse, pieces = together(*factor_part(gram, inverse, 2, 4), pieces)
    wide, squares = own_right(inverse, pieces.reshape(RANK, WIDE), 4)
    squares, wide, inverse, left = together(squares, wide, inverse, left)
    right_mine = lax.all_to_all(wide, "y", 0, 0, tiled=True)
    ortho = product(left, inverse, ((1,), (1,)))
    squares = pair_sum(pair_sum(squares, 1, "tensor"), 3, "tensor")
    squares = pair_sum(pair_sum(squares, 1), 3)
    right_mine, ortho, squares = together(right_mine, ortho, squares)
    right_other = swapped(right_mine)
    squares = squares + swapped(squares)

    momentum_new = first_half(mine, ortho, right_mine, buffer)
    momentum_new, right_other, squares = together(momentum_new, right_other, squares)
    place = jnp.stack([core, (lax.axis_index("y") * 2 + core) * rank_local]).astype(jnp.int32)
    momentum_new, update, lines = last_half(place, ortho, right_mine, right_other, buffer, squares, momentum_new)
    return (update, momentum_new[None], lines.T)


def solution(mesh):
    finer = Mesh(
        mesh.devices.reshape(4, 2, mesh.shape["tensor"], mesh.shape["replica"]),
        ("y", "core", "tensor", "replica"),
    )
    fsdp = ("y", "core")
    placed = (P("replica", fsdp, "tensor"), P("replica", fsdp, "tensor"), P("tensor", fsdp))
    return jax.shard_map(
        local,
        mesh=finer,
        in_specs=placed,
        out_specs=(P(fsdp, "tensor"), P("replica", fsdp, "tensor"), P("tensor", fsdp)),
        check_vma=False,
    )
```

time: 232 us -> 183 us (0.79)
  blocking collectives: 100 us -> 28.4 us
  waiting for transfers between devices: 26.6 us -> 56.3 us
  starting transfers between devices: 28.5 us -> 50.8 us
  matrix products: 24.1 us -> 2.95 us
  Pallas kernels: 36.7 us -> 25.6 us
  local copies, waits for them, and re-layouts: 5.08 us -> 8.65 us
    all_to_all x7 -> x2, blocking collectives: 100 us -> 28.4 us  [parted(): return lax.all_to_all(blocks, axis, 0, 0, tiled=True)]
    all_to_all x0 -> x6, starting transfers between devices: none -> 25.9 us  [the longest x1 5.69 us: local(): right_mine = lax.all_to_all(wide, 'y', 0, 0, tiled=True)]
    pallas_call x4 -> x2, Pallas kernels: 36.7 us -> 14.7 us  [factor_part(): pl.pallas_call(functools.partial(factor_kernel, first, last), out_shape=(...]
    dot_general x7 -> x3, matrix products: 24.1 us -> 2.95 us  [product(): lax.dot_general(a, b, (dims, ((), ())), precision=precision, preferred_el...]
    ppermute x2 -> x8, waiting for transfers between devices: 9.36 us -> 28.3 us  [pair_sum(): return value + lax.ppermute(value, axis, [(i, i ^ mask) for i in range(4)])]
    all_to_all x0 -> x6, waiting for transfers between devices: none -> 16.7 us  [the longest x1 7.66 us: local(): lines = lax.all_to_all(wide, 'y', 0, 0, tiled=True)]
    pallas_call x0 -> x5, Pallas kernels: none -> 11 us  [the longest x1 5.14 us: last_half(): call(last_kernel, 9 * rows * RANK * columns, 8 * rows * columns, in_specs...]
    all_to_all x3 -> x1, starting transfers between devices: 10.5 us -> 3.37 us  [to_everyone(): lax.all_to_all(jnp.broadcast_to(value[None], (size, *value.shape)), axis,...]
  transfers between devices with their start and end apart: 10 -> 21, of which waited for: 6 -> 16; matrix products, arithmetic and copies ran while one was open for 5% -> 4% of each run, Pallas kernels for 16% -> 10%
where the time goes in v2:
time: 183 us; the launch traced here: 182 us
  waiting for transfers between devices  56.3 us (31%)
  starting transfers between devices  50.8 us (28%)
  blocking collectives  28.4 us (16%)
  Pallas kernels  25.6 us (14%)
  local copies, waits for them, and re-layouts  8.65 us (5%)
  other arithmetic  8.29 us (5%)
  matrix products  2.95 us (2%)
    all_to_all x2, blocking collectives, parted(): return lax.all_to_all(blocks, axis, 0, 0, tiled=True)  28.4 us
    ppermute x8, waiting for transfers between devices, pair_sum(): return value + lax.ppermute(value, axis, [(i, i ^ mask) for i in range(4)])  28.3 us
    ppermute x6, starting transfers between devices, swapped(): return lax.ppermute(value, 'core', [(0, 1), (1, 0)])  14.7 us
    pallas_call x2, Pallas kernels, factor_part(): pl.pallas_call(functools.partial(factor_kernel, first, last), out_shape=(...  14.7 us
    all_to_all x1, waiting for transfers between devices, to_everyone(): lax.all_to_all(jnp.broadcast_to(value[None], (size, *value.shape)), axis,...  7.94 us
    all_to_all x1, waiting for transfers between devices, local(): lines = lax.all_to_all(wide, 'y', 0, 0, tiled=True)  7.66 us
    ppermute x8, starting transfers between devices, pair_sum(): return value + lax.ppermute(value, axis, [(i, i ^ mask) for i in range(4)])  6.77 us
    add x1, other arithmetic, local(): buffer = momentum[0] + gradient[0].astype(jnp.float32)  5.75 us
  transfers between devices with their start and end apart: 21, of which 16 were waited for; matrix products, arithmetic and copies ran while one was open for 4% of the time, Pallas kernels for 10%

profile of v2, /device:TPU:1, one launch (start us, length us, event | category | flops | bytes accessed | tf_op | source)
XLA Modules:
  0.0 182.1 jit_solution(7739651027058918003)
XLA Ops:
  0.6 2.0 %broadcast_in_dim.15 = f32[4,32,2048]{2,1,0:T(8,128)} broadcast(f32[32,2048]{1,0:T(8,128)} %bitcast.39), dimensions={1,2} | broadcast | bytes 1310720 | tf_op jit(solution)/shard_map/broadcast_in_dim | solution.py:318
  2.7 5.0 %all-to-all-start = ((f32[4,32,2048]{2,1,0:T(8,128)}), f32[4,32,2048]{2,1,0:T(8,128)S(1)}, u32[]{:S(2)}, u32[]{:S(2)}) async-start(f32[4,32,2048]{2,1,0:T(8,128)} %broadcast_in_dim.15), calls=%async_computation | async-start | bytes 2097152 | tf_op jit(solution)/shard_map/all_to_all | solution.py:320
  7.7 5.8 %add_bitcast_fusion.buffer_ref = f32[512,2048]{1,0:T(8,128)} fusion(f32[1,512,2048]{2,1,0:T(8,128)} %param.4, bf16[1,512,2048]{2,1,0:T(8,128)(2,1)} %param.3), kind=kLoop, calls=%fused_computation | loop fusion | flops 2097152 | bytes 10485760 | tf_op jit(solution)/shard_map/add | solution.py:321
  13.4 7.7 %all-to-all-done = f32[4,32,2048]{2,1,0:T(8,128)S(1)} async-done(((f32[4,32,2048]{2,1,0:T(8,128)}), f32[4,32,2048]{2,1,0:T(8,128)S(1)}, u32[]{:S(2)}, u32[]{:S(2)}) %all-to-all-start) | async-done | bytes 1048608 | tf_op jit(solution)/shard_map/all_to_all | solution.py:320
  21.1 2.6 %collective-permute-start = (f32[4,32,2048]{2,1,0:T(8,128)S(1)}, f32[4,32,2048]{2,1,0:T(8,128)S(1)}, u32[]{:S(2)}, u32[]{:S(2)}) collective-permute-start(f32[4,32,2048]{2,1,0:T(8,128)S(1)} %all-to-all-done), channel_id=1, source_target_pairs={{0,32},{32,0},{1,33},{33,1},{2,34},{34,2},{3,35},{35,3},{4,36},{36... | collective-permute-start | bytes 3145736 | tf_op jit(solution)/shard_map/ppermute | solution.py:120
  23.7 2.3 %collective-permute-done = f32[4,32,2048]{2,1,0:T(8,128)S(1)} collective-permute-done((f32[4,32,2048]{2,1,0:T(8,128)S(1)}, f32[4,32,2048]{2,1,0:T(8,128)S(1)}, u32[]{:S(2)}, u32[]{:S(2)}) %collective-permute-start) | collective-permute-done | bytes 1048608 | tf_op jit(solution)/shard_map/ppermute | solution.py:120
  26.4 1.9 %fusion.1 = f32[4,128,256]{2,1,0:T(8,128)S(1)} fusion(f32[4,128,2048]{2,1,0:T(8,128)S(1)} %bitcast.29, f32[256,2048,1]{1,0,2:T(8,128)S(1)} %bitcast.35), kind=kOutput, calls=%fused_computation.14 | convolution fusion | flops 1610612736 | bytes 6815744 | tf_op jit(solution)/shard_map/dot_general | solution.py:142
  28.3 12.4 %all_to_all.45 = f32[4,128,256]{2,1,0:T(8,128)S(1)} all-to-all(f32[4,128,256]{2,1,0:T(8,128)S(1)} %fusion.1), channel_id=1, replica_groups=mesh['y'=4,'core'=2,'tensor'=4,'replica'=8] {'tensor'}, dimensions={0} | all-to-all | bytes 1048576 | tf_op jit(solution)/shard_map/all_to_all | solution.py:108
  40.8 16.0 %all_to_all.46 = f32[8,16,256]{2,1,0:T(8,128)S(1)} all-to-all(f32[8,16,256]{2,1,0:T(8,128)S(1)} %bitcast.38), channel_id=1, replica_groups=mesh['y'=4,'core'=2,'tensor'=4,'replica'=8] {'replica'}, dimensions={0} | all-to-all | bytes 262144 | tf_op jit(solution)/shard_map/all_to_all | solution.py:108
  57.5 3.4 %all-to-all-start.3 = ((f32[8,16,256]{2,1,0:T(8,128)}), f32[8,16,256]{2,1,0:T(8,128)S(1)}, u32[]{:S(2)}, u32[]{:S(2)}) async-start(f32[8,16,256]{2,1,0:T(8,128)} %broadcast_in_dim.16), calls=%async_computation.3 | async-start | bytes 262144 | tf_op jit(solution)/shard_map/all_to_all | solution.py:95
  60.9 7.9 %all-to-all-done.3 = f32[8,16,256]{2,1,0:T(8,128)S(1)} async-done(((f32[8,16,256]{2,1,0:T(8,128)}), f32[8,16,256]{2,1,0:T(8,128)S(1)}, u32[]{:S(2)}, u32[]{:S(2)}) %all-to-all-start.3) | async-done | bytes 131104 | tf_op jit(solution)/shard_map/all_to_all | solution.py:95
  68.8 0.8 broadcast_in_dim.36
  70.1 4.3 %collective-permute-start.1 = (f32[128,256]{1,0:T(8,128)S(1)}, f32[128,256]{1,0:T(8,128)S(1)}, u32[]{:S(2)}, u32[]{:S(2)}) collective-permute-start(f32[128,256]{1,0:T(8,128)S(1)} %constant_dynamic-slice_fusion), channel_id=1, source_target_pairs={{0,32},{32,0},{1,33},{33,1},{2,34},{34,2},{3,35},{35,3},{4,36},{36... | collective-permute-start | bytes 393224 | tf_op jit(solution)/shard_map/ppermute | solution.py:120
  74.3 3.5 %all-to-all-start.4 = ((f32[4,128,256]{2,1,0:T(8,128)}), f32[4,128,256]{2,1,0:T(8,128)S(1)}, u32[]{:S(2)}, u32[]{:S(2)}) async-start(f32[4,128,256]{2,1,0:T(8,128)} %broadcast_in_dim.36), calls=%async_computation.4 | async-start | bytes 1048576 | tf_op jit(solution)/shard_map/all_to_all | solution.py:332
  78.2 4.8 %collective-permute-done.2 = f32[128,256]{1,0:T(8,128)S(1)} collective-permute-done((f32[128,256]{1,0:T(8,128)S(1)}, f32[128,256]{1,0:T(8,128)S(1)}, u32[]{:S(2)}, u32[]{:S(2)}) %collective-permute-start.2) | collective-permute-done | bytes 131104 | tf_op jit(solution)/shard_map/ppermute | solution.py:138
  83.1 4.3 %all-to-all-done.4 = f32[4,128,256]{2,1,0:T(8,128)S(1)} async-done(((f32[4,128,256]{2,1,0:T(8,128)}), f32[4,128,256]{2,1,0:T(8,128)S(1)}, u32[]{:S(2)}, u32[]{:S(2)}) %all-to-all-start.4) | async-done | bytes 524320 | tf_op jit(solution)/shard_map/all_to_all | solution.py:332
  87.4 2.2 %copy-done.1 = f32[512,2048]{1,0:T(8,128)S(1)} copy-done((f32[512,2048]{1,0:T(8,128)S(1)}, f32[512,2048]{1,0:T(8,128)}, u32[]{:S(2)}) %copy-start.1) | copy-done | bytes 4194328
  89.6 1.1 shard_map.58
  90.7 0.9 collective-permute-start.3
  91.6 0.9 collective-permute-start.4
  92.5 1.1 shard_map.59
  93.6 4.3 %collective-permute-done.4 = f32[128,256]{1,0:T(8,128)S(1)} collective-permute-done((f32[128,256]{1,0:T(8,128)S(1)}, f32[128,256]{1,0:T(8,128)S(1)}, u32[]{:S(2)}, u32[]{:S(2)}) %collective-permute-start.4) | collective-permute-done | bytes 131104 | tf_op jit(solution)/shard_map/ppermute | solution.py:138
  97.9 1.1 add.56
  99.0 3.5 %all-to-all-start.5 = ((f32[4,256,256]{2,1,0:T(8,128)}), f32[4,256,256]{2,1,0:T(8,128)S(1)}, u32[]{:S(2)}, u32[]{:S(2)}) async-start(f32[4,256,256]{2,1,0:T(8,128)} %add.56), calls=%async_computation.5 | async-start | bytes 2097152 | tf_op jit(solution)/shard_map/all_to_all | solution.py:341
  102.9 3.9 %collective-permute-done.5 = f32[128,256]{1,0:T(8,128)S(1)} collective-permute-done((f32[128,256]{1,0:T(8,128)S(1)}, f32[128,256]{1,0:T(8,128)S(1)}, u32[]{:S(2)}, u32[]{:S(2)}) %collective-permute-start.5) | collective-permute-done | bytes 131104 | tf_op jit(solution)/shard_map/ppermute | solution.py:138
  106.8 1.0 collective-permute-start.6
  107.7 4.4 %collective-permute-done.6 = f32[128,256]{1,0:T(8,128)S(1)} collective-permute-done((f32[128,256]{1,0:T(8,128)S(1)}, f32[128,256]{1,0:T(8,128)S(1)}, u32[]{:S(2)}, u32[]{:S(2)}) %collective-permute-start.6) | collective-permute-done | bytes 131104 | tf_op jit(solution)/shard_map/ppermute | solution.py:138
  112.2 2.7 %collective-permute-start.7 = (f32[128,256]{1,0:T(8,128)S(1)}, f32[128,256]{1,0:T(8,128)S(1)}, u32[]{:S(2)}, u32[]{:S(2)}) collective-permute-start(f32[128,256]{1,0:T(8,128)S(1)} %add.58), channel_id=1, source_target_pairs={{0,32},{32,0},{1,33},{33,1},{2,34},{34,2},{3,35},{35,3},{4,36},{36... | collective-permute-start | bytes 393224 | tf_op jit(solution)/shard_map/ppermute | solution.py:120
  114.9 1.0 collective-permute-done.7
  117.5 3.6 %all-to-all-start.6 = ((f32[8,32,256]{2,1,0:T(8,128)}), f32[8,32,256]{2,1,0:T(8,128)S(1)}, u32[]{:S(2)}, u32[]{:S(2)}) async-start(f32[8,32,256]{2,1,0:T(8,128)} %bitcast.14), calls=%async_computation.6 | async-start | bytes 524288 | tf_op jit(solution)/shard_map/all_to_all | solution.py:108
  121.2 7.4 %shard_map.60 = (f32[256,256]{1,0:T(8,128)S(1)}, f32[256,256]{1,0:T(8,128)S(1)}) custom-call(f32[256,256]{1,0:T(8,128)S(1)} %pad_maximum_fusion.1.gram_ref, f32[256,256]{1,0:T(8,128)S(1)} %fusion.inv_ref), custom_call_target="tpu_custom_call" | custom-call | bytes 30000000 | tf_op jit(solution)/shard_map/pallas_call | solution.py:86
  128.5 1.8 all-to-all-done.6
  131.1 4.6 %all-to-all-start.7 = ((f32[8,32,256]{2,1,0:T(8,128)}), f32[8,32,256]{2,1,0:T(8,128)S(1)}, u32[]{:S(2)}, u32[]{:S(2)}) async-start(f32[8,32,256]{2,1,0:T(8,128)} %broadcast_in_dim.37), calls=%async_computation.7 | async-start | bytes 524288 | tf_op jit(solution)/shard_map/all_to_all | solution.py:352
  135.7 7.3 %shard_map.61 = (f32[256,256]{1,0:T(8,128)}, f32[256,256]{1,0:T(8,128)S(1)}) custom-call(f32[256,256]{1,0:T(8,128)S(1)} %get-tuple-element.68.gram_ref, f32[256,256]{1,0:T(8,128)S(1)} %get-tuple-element.69.inv_ref), custom_call_target="tpu_custom_call" | custom-call | bytes 30000000 | tf_op jit(solution)/shard_map/pallas_call | solution.py:86
  143.0 2.2 %all-to-all-done.7 = f32[8,32,256]{2,1,0:T(8,128)S(1)} async-done(((f32[8,32,256]{2,1,0:T(8,128)}), f32[8,32,256]{2,1,0:T(8,128)S(1)}, u32[]{:S(2)}, u32[]{:S(2)}) %all-to-all-start.7) | async-done | bytes 262176 | tf_op jit(solution)/shard_map/all_to_all | solution.py:352
  145.2 1.6 shard_map.62
  146.7 5.7 %all-to-all-start.8 = ((f32[4,256,256]{2,1,0:T(8,128)}), f32[4,256,256]{2,1,0:T(8,128)S(1)}, u32[]{:S(2)}, u32[]{:S(2)}) async-start(f32[4,256,256]{2,1,0:T(8,128)} %get-tuple-element.76), calls=%async_computation.8 | async-start | bytes 2097152 | tf_op jit(solution)/shard_map/all_to_all | solution.py:356
  152.4 2.5 %collective-permute-done.8 = f32[8,256]{1,0:T(8,128)S(1)} collective-permute-done((f32[8,256]{1,0:T(8,128)S(1)}, f32[8,256]{1,0:T(8,128)S(1)}, u32[]{:S(2)}, u32[]{:S(2)}) %collective-permute-start.8) | collective-permute-done | bytes 8224 | tf_op jit(solution)/shard_map/ppermute | solution.py:138
  154.9 0.9 collective-permute-start.9
  155.8 2.8 %collective-permute-done.9 = f32[8,256]{1,0:T(8,128)S(1)} collective-permute-done((f32[8,256]{1,0:T(8,128)S(1)}, f32[8,256]{1,0:T(8,128)S(1)}, u32[]{:S(2)}, u32[]{:S(2)}) %collective-permute-start.9) | collective-permute-done | bytes 8224 | tf_op jit(solution)/shard_map/ppermute | solution.py:138
  158.6 1.5 collective-permute-start.10
  160.1 3.5 %collective-permute-done.10 = f32[8,256]{1,0:T(8,128)S(1)} collective-permute-done((f32[8,256]{1,0:T(8,128)S(1)}, f32[8,256]{1,0:T(8,128)S(1)}, u32[]{:S(2)}, u32[]{:S(2)}) %collective-permute-start.10) | collective-permute-done | bytes 8224 | tf_op jit(solution)/shard_map/ppermute | solution.py:138
  163.5 1.8 collective-permute-start.11
  166.0 2.2 %collective-permute-done.11 = f32[8,256]{1,0:T(8,128)S(1)} collective-permute-done((f32[8,256]{1,0:T(8,128)S(1)}, f32[8,256]{1,0:T(8,128)S(1)}, u32[]{:S(2)}, u32[]{:S(2)}) %collective-permute-start.11) | collective-permute-done | bytes 8224 | tf_op jit(solution)/shard_map/ppermute | solution.py:138
  168.1 4.0 %collective-permute-start.12 = (f32[4,256,256]{2,1,0:T(8,128)S(1)}, f32[4,256,256]{2,1,0:T(8,128)S(1)}, u32[]{:S(2)}, u32[]{:S(2)}) collective-permute-start(f32[4,256,256]{2,1,0:T(8,128)S(1)} %all-to-all-done.8.right_ref.mine_ref), channel_id=1, source_target_pairs={{0,32},{32,0},{1,33},{33,1},{2,34},{34,2},{3,35},{35,3},{4,36},{36... | collective-permute-start | bytes 3145736 | tf_op jit(solution)/shard_map/ppermute | solution.py:120
  172.4 2.2 %copy-done.3 = f32[512,2048]{1,0:T(8,128)S(1)} copy-done((f32[512,2048]{1,0:T(8,128)S(1)}, f32[512,2048]{1,0:T(8,128)}, u32[]{:S(2)}) %copy-start.3) | copy-done | bytes 4194328
  174.6 2.1 %shard_map.63.filled_ref = f32[512,2048]{1,0:T(8,128)} custom-call(s32[1]{0:T(128)} %bitcast.half_ref, f32[512,256]{1,0:T(8,128)S(1)} %fusion.3.ortho_ref, f32[4,256,256]{2,1,0:T(8,128)S(1)} %all-to-all-done.8.right_ref.mine_ref, f32[512,2048]{1,0:T(8,128)S(1)} %copy-done.3), custom_call_target="tpu_custom_call" | custom-call | flops 805306368 | bytes 4194304 | tf_op jit(solution)/shard_map/pallas_call | solution.py:246
  176.8 5.1 %shard_map.64 = (f32[512,2048]{1,0:T(8,128)}, bf16[512,2048]{1,0:T(8,128)(2,1)}, f32[32,2048]{1,0:T(8,128)}) custom-call(s32[2]{0:T(128)S(1)} %pad_add_fusion.place_ref, f32[512,256]{1,0:T(8,128)S(1)} %fusion.3.ortho_ref, f32[4,256,256]{2,1,0:T(8,128)S(1)} %all-to-all-done.8.right_ref.mine_ref, ...), custom_call_target="tpu_custom_call", output_to_operand_aliasing={{0}: (6, {})} | custom-call | flops 2415919104 | bytes 8388608 | tf_op jit(solution)/shard_map/pallas_call | solution.py:289
  (43 shorter events, 5.7 us)
Async XLA Ops:
  2.7 18.4 %all-to-all-start = ((f32[4,32,2048]{2,1,0:T(8,128)}), f32[4,32,2048]{2,1,0:T(8,128)S(1)}, u32[]{:S(2)}, u32[]{:S(2)}) async-start(f32[4,32,2048]{2,1,0:T(8,128)} %broadcast_in_dim.15), calls=%async_computation | async-start | bytes 2097152 | tf_op jit(solution)/shard_map/all_to_all | solution.py:320
  21.1 4.9 %collective-permute-start = (f32[4,32,2048]{2,1,0:T(8,128)S(1)}, f32[4,32,2048]{2,1,0:T(8,128)S(1)}, u32[]{:S(2)}, u32[]{:S(2)}) collective-permute-start(f32[4,32,2048]{2,1,0:T(8,128)S(1)} %all-to-all-done), channel_id=1, source_target_pairs={{0,32},{32,0},{1,33},{33,1},{2,34},{34,2},{3,35},{35,3},{4,36},{36... | collective-permute-start | bytes 3145736 | tf_op jit(solution)/shard_map/ppermute | solution.py:120
  23.7 2.6 %copy-start = (f32[512,2048]{1,0:T(8,128)S(1)}, f32[512,2048]{1,0:T(8,128)}, u32[]{:S(2)}) copy-start(f32[512,2048]{1,0:T(8,128)} %add_bitcast_fusion.buffer_ref) | copy-start | bytes 12582916
  57.5 11.3 %all-to-all-start.3 = ((f32[8,16,256]{2,1,0:T(8,128)}), f32[8,16,256]{2,1,0:T(8,128)S(1)}, u32[]{:S(2)}, u32[]{:S(2)}) async-start(f32[8,16,256]{2,1,0:T(8,128)} %broadcast_in_dim.16), calls=%async_computation.3 | async-start | bytes 262144 | tf_op jit(solution)/shard_map/all_to_all | solution.py:95
  70.1 7.8 %collective-permute-start.1 = (f32[128,256]{1,0:T(8,128)S(1)}, f32[128,256]{1,0:T(8,128)S(1)}, u32[]{:S(2)}, u32[]{:S(2)}) collective-permute-start(f32[128,256]{1,0:T(8,128)S(1)} %constant_dynamic-slice_fusion), channel_id=1, source_target_pairs={{0,32},{32,0},{1,33},{33,1},{2,34},{34,2},{3,35},{35,3},{4,36},{36... | collective-permute-start | bytes 393224 | tf_op jit(solution)/shard_map/ppermute | solution.py:120
  74.3 13.1 %all-to-all-start.4 = ((f32[4,128,256]{2,1,0:T(8,128)}), f32[4,128,256]{2,1,0:T(8,128)S(1)}, u32[]{:S(2)}, u32[]{:S(2)}) async-start(f32[4,128,256]{2,1,0:T(8,128)} %broadcast_in_dim.36), calls=%async_computation.4 | async-start | bytes 1048576 | tf_op jit(solution)/shard_map/all_to_all | solution.py:332
  77.9 5.2 %collective-permute-start.2 = (f32[128,256]{1,0:T(8,128)S(1)}, f32[128,256]{1,0:T(8,128)S(1)}, u32[]{:S(2)}, u32[]{:S(2)}) collective-permute-start(f32[128,256]{1,0:T(8,128)S(1)} %dynamic-slice_add_fusion), channel_id=1, source_target_pairs={{0,64},{64,0},{128,192},{192,128},{1,65},{65,1},{129,193},{193,129... | collective-permute-start | bytes 393224 | tf_op jit(solution)/shard_map/ppermute | solution.py:138
  87.4 2.2 %copy-start.1 = (f32[512,2048]{1,0:T(8,128)S(1)}, f32[512,2048]{1,0:T(8,128)}, u32[]{:S(2)}) copy-start(f32[512,2048]{1,0:T(8,128)} %add_bitcast_fusion.buffer_ref) | copy-start | bytes 12582916
  89.6 2.9 %copy-start.2 = (f32[512,2048]{1,0:T(8,128)S(1)}, f32[512,2048]{1,0:T(8,128)}, u32[]{:S(2)}) copy-start(f32[512,2048]{1,0:T(8,128)} %add_bitcast_fusion.buffer_ref) | copy-start | bytes 12582916
  90.7 7.2 %collective-permute-start.3 = (f32[4,256,256]{2,1,0:T(8,128)S(1)}, f32[4,256,256]{2,1,0:T(8,128)S(1)}, u32[]{:S(2)}, u32[]{:S(2)}) collective-permute-start(f32[4,256,256]{2,1,0:T(8,128)S(1)} %shard_map.58), channel_id=1, source_target_pairs={{0,32},{32,0},{1,33},{33,1},{2,34},{34,2},{3,35},{35,3},{4,36},{36... | collective-permute-start | bytes 3145736 | tf_op jit(solution)/shard_map/ppermute | solution.py:120
  91.6 6.3 %collective-permute-start.4 = (f32[128,256]{1,0:T(8,128)S(1)}, f32[128,256]{1,0:T(8,128)S(1)}, u32[]{:S(2)}, u32[]{:S(2)}) collective-permute-start(f32[128,256]{1,0:T(8,128)S(1)} %add.54), channel_id=1, source_target_pairs={{0,192},{64,128},{128,64},{192,0},{1,193},{65,129},{129,65},{193,1... | collective-permute-start | bytes 393224 | tf_op jit(solution)/shard_map/ppermute | solution.py:138
  99.0 17.8 %all-to-all-start.5 = ((f32[4,256,256]{2,1,0:T(8,128)}), f32[4,256,256]{2,1,0:T(8,128)S(1)}, u32[]{:S(2)}, u32[]{:S(2)}) async-start(f32[4,256,256]{2,1,0:T(8,128)} %add.56), calls=%async_computation.5 | async-start | bytes 2097152 | tf_op jit(solution)/shard_map/all_to_all | solution.py:341
  102.5 4.2 %collective-permute-start.5 = (f32[128,256]{1,0:T(8,128)S(1)}, f32[128,256]{1,0:T(8,128)S(1)}, u32[]{:S(2)}, u32[]{:S(2)}) collective-permute-start(f32[128,256]{1,0:T(8,128)S(1)} %add.55), channel_id=1, source_target_pairs={{0,8},{8,0},{16,24},{24,16},{1,9},{9,1},{17,25},{25,17},{2,10},{10... | collective-permute-start | bytes 393224 | tf_op jit(solution)/shard_map/ppermute | solution.py:138
  106.8 5.4 %collective-permute-start.6 = (f32[128,256]{1,0:T(8,128)S(1)}, f32[128,256]{1,0:T(8,128)S(1)}, u32[]{:S(2)}, u32[]{:S(2)}) collective-permute-start(f32[128,256]{1,0:T(8,128)S(1)} %add.57), channel_id=1, source_target_pairs={{0,24},{8,16},{16,8},{24,0},{1,25},{9,17},{17,9},{25,1},{2,26},{10... | collective-permute-start | bytes 393224 | tf_op jit(solution)/shard_map/ppermute | solution.py:138
  112.2 3.7 %collective-permute-start.7 = (f32[128,256]{1,0:T(8,128)S(1)}, f32[128,256]{1,0:T(8,128)S(1)}, u32[]{:S(2)}, u32[]{:S(2)}) collective-permute-start(f32[128,256]{1,0:T(8,128)S(1)} %add.58), channel_id=1, source_target_pairs={{0,32},{32,0},{1,33},{33,1},{2,34},{34,2},{3,35},{35,3},{4,36},{36... | collective-permute-start | bytes 393224 | tf_op jit(solution)/shard_map/ppermute | solution.py:120
  117.5 12.8 %all-to-all-start.6 = ((f32[8,32,256]{2,1,0:T(8,128)}), f32[8,32,256]{2,1,0:T(8,128)S(1)}, u32[]{:S(2)}, u32[]{:S(2)}) async-start(f32[8,32,256]{2,1,0:T(8,128)} %bitcast.14), calls=%async_computation.6 | async-start | bytes 524288 | tf_op jit(solution)/shard_map/all_to_all | solution.py:108
  131.1 14.1 %all-to-all-start.7 = ((f32[8,32,256]{2,1,0:T(8,128)}), f32[8,32,256]{2,1,0:T(8,128)S(1)}, u32[]{:S(2)}, u32[]{:S(2)}) async-start(f32[8,32,256]{2,1,0:T(8,128)} %broadcast_in_dim.37), calls=%async_computation.7 | async-start | bytes 524288 | tf_op jit(solution)/shard_map/all_to_all | solution.py:352
  146.7 21.4 %all-to-all-start.8 = ((f32[4,256,256]{2,1,0:T(8,128)}), f32[4,256,256]{2,1,0:T(8,128)S(1)}, u32[]{:S(2)}, u32[]{:S(2)}) async-start(f32[4,256,256]{2,1,0:T(8,128)} %get-tuple-element.76), calls=%async_computation.8 | async-start | bytes 2097152 | tf_op jit(solution)/shard_map/all_to_all | solution.py:356
  152.4 2.5 %collective-permute-start.8 = (f32[8,256]{1,0:T(8,128)S(1)}, f32[8,256]{1,0:T(8,128)S(1)}, u32[]{:S(2)}, u32[]{:S(2)}) collective-permute-start(f32[8,256]{1,0:T(8,128)S(1)} %get-tuple-element.79), channel_id=1, source_target_pairs={{0,8},{8,0},{16,24},{24,16},{1,9},{9,1},{17,25},{25,17},{2,10},{10... | collective-permute-start | bytes 24584 | tf_op jit(solution)/shard_map/ppermute | solution.py:138
  154.9 3.7 %collective-permute-start.9 = (f32[8,256]{1,0:T(8,128)S(1)}, f32[8,256]{1,0:T(8,128)S(1)}, u32[]{:S(2)}, u32[]{:S(2)}) collective-permute-start(f32[8,256]{1,0:T(8,128)S(1)} %add.59), channel_id=1, source_target_pairs={{0,24},{8,16},{16,8},{24,0},{1,25},{9,17},{17,9},{25,1},{2,26},{10... | collective-permute-start | bytes 24584 | tf_op jit(solution)/shard_map/ppermute | solution.py:138
  158.6 4.9 %collective-permute-start.10 = (f32[8,256]{1,0:T(8,128)S(1)}, f32[8,256]{1,0:T(8,128)S(1)}, u32[]{:S(2)}, u32[]{:S(2)}) collective-permute-start(f32[8,256]{1,0:T(8,128)S(1)} %add.60), channel_id=1, source_target_pairs={{0,64},{64,0},{128,192},{192,128},{1,65},{65,1},{129,193},{193,129... | collective-permute-start | bytes 24584 | tf_op jit(solution)/shard_map/ppermute | solution.py:138
  163.5 4.6 %collective-permute-start.11 = (f32[8,256]{1,0:T(8,128)S(1)}, f32[8,256]{1,0:T(8,128)S(1)}, u32[]{:S(2)}, u32[]{:S(2)}) collective-permute-start(f32[8,256]{1,0:T(8,128)S(1)} %add.61), channel_id=1, source_target_pairs={{0,192},{64,128},{128,64},{192,0},{1,193},{65,129},{129,65},{193,1... | collective-permute-start | bytes 24584 | tf_op jit(solution)/shard_map/ppermute | solution.py:138
  168.1 8.6 %collective-permute-start.12 = (f32[4,256,256]{2,1,0:T(8,128)S(1)}, f32[4,256,256]{2,1,0:T(8,128)S(1)}, u32[]{:S(2)}, u32[]{:S(2)}) collective-permute-start(f32[4,256,256]{2,1,0:T(8,128)S(1)} %all-to-all-done.8.right_ref.mine_ref), channel_id=1, source_target_pairs={{0,32},{32,0},{1,33},{33,1},{2,34},{34,2},{3,35},{35,3},{4,36},{36... | collective-permute-start | bytes 3145736 | tf_op jit(solution)/shard_map/ppermute | solution.py:120
  172.2 4.6 %collective-permute-start.13 = (f32[8,256]{1,0:T(8,128)S(1)}, f32[8,256]{1,0:T(8,128)S(1)}, u32[]{:S(2)}, u32[]{:S(2)}) collective-permute-start(f32[8,256]{1,0:T(8,128)S(1)} %add.62), channel_id=1, source_target_pairs={{0,32},{32,0},{1,33},{33,1},{2,34},{34,2},{3,35},{35,3},{4,36},{36... | collective-permute-start | bytes 24584 | tf_op jit(solution)/shard_map/ppermute | solution.py:120
  172.4 2.2 %copy-start.3 = (f32[512,2048]{1,0:T(8,128)S(1)}, f32[512,2048]{1,0:T(8,128)}, u32[]{:S(2)}) copy-start(f32[512,2048]{1,0:T(8,128)} %add_bitcast_fusion.buffer_ref) | copy-start | bytes 12582916

commit v3 on v2

--- a/solution.py
+++ b/solution.py
@@ -87,7 +87,7 @@
         functools.partial(factor_kernel, first, last),
         out_shape=(shape, shape),
         compiler_params=pltpu.CompilerParams(vmem_limit_bytes=16 << 20),
-        cost_estimate=pl.CostEstimate(flops=0, bytes_accessed=(last-first)*15_000_000, transcendentals=0),
+        cost_estimate=pl.CostEstimate(flops=0, bytes_accessed=(last - first) * 10_000, transcendentals=0),
     )(gram, inv)
 
 def to_everyone(value, axis):
@@ -159,6 +159,7 @@
 IN_VMEM = pl.BlockSpec(memory_space=pltpu.VMEM)
 IN_SMEM = pl.BlockSpec(memory_space=pltpu.SMEM)
 ANYWHERE = pl.BlockSpec(memory_space=pl.ANY)
+IN_HBM = pl.BlockSpec(memory_space=pltpu.HBM)
 
 
 def block_of(ref, index):
@@ -172,6 +173,69 @@
         cost_estimate=pl.CostEstimate(flops=flops, bytes_accessed=moved, transcendentals=0),
         **rest,
     )
+
+
+PARTS = 4
+
+
+def rows_of(ref, i):
+    rows = ref.shape[0] // PARTS
+    return ref.at[pl.ds(i * rows, rows), :]
+
+
+def copied(source, target, sems):
+    copies = []
+    for i in range(PARTS):
+        copy = pltpu.make_async_copy(rows_of(source, i), rows_of(target, i), sems.at[i])
+        copy.start()
+        copies.append(copy)
+    return copies
+
+
+def added_kernel(momentum_ref, gradient_ref, near_ref, far_ref, low_ref, sems, low_sems, out_sems):
+    copies = copied(momentum_ref.at[0], near_ref, sems)
+    low_copies = copied(gradient_ref.at[0], low_ref, low_sems)
+    out_copies = []
+    for i in range(PARTS):
+        copies[i].wait()
+        low_copies[i].wait()
+        rows_of(near_ref, i)[...] = rows_of(near_ref, i)[...] + rows_of(low_ref, i)[...].astype(jnp.float32)
+        copy = pltpu.make_async_copy(rows_of(near_ref, i), rows_of(far_ref, i), out_sems.at[i])
+        copy.start()
+        out_copies.append(copy)
+    for copy in out_copies:
+        copy.wait()
+
+
+def added(momentum, gradient):
+    _, rows, columns = momentum.shape
+    shape = jax.ShapeDtypeStruct((rows, columns), jnp.float32)
+    return call(
+        added_kernel,
+        rows * columns,
+        14 * rows * columns,
+        in_specs=[IN_HBM, IN_HBM],
+        out_specs=(IN_VMEM, IN_HBM),
+        out_shape=(shape, shape),
+        scratch_shapes=[pltpu.VMEM((rows, columns), jnp.bfloat16)] + [pltpu.SemaphoreType.DMA((PARTS,))] * 3,
+    )(momentum, gradient)
+
+
+def staged_kernel(far_ref, near_ref, sems):
+    for copy in copied(far_ref, near_ref, sems):
+        copy.wait()
+
+
+def staged(far):
+    return call(
+        staged_kernel,
+        0,
+        8 * far.shape[0] * far.shape[1],
+        in_specs=[IN_HBM],
+        out_specs=IN_VMEM,
+        out_shape=jax.ShapeDtypeStruct(far.shape, jnp.float32),
+        scratch_shapes=[pltpu.SemaphoreType.DMA((PARTS,))],
+    )(far)
 
 
 def right_kernel(half_ref, left_ref, buffer_ref, out_ref):
@@ -194,28 +258,31 @@
     )(half, left, buffer)
 
 
-def own_kernel(inverse_ref, raw_ref, wide_ref, squares_ref):
-    right = jnp.dot(inverse_ref[...], raw_ref[...], precision=HIGH, preferred_element_type=jnp.float32)
-    for i in range(wide_ref.shape[0]):
-        wide_ref[i] = right
+def finished_kernel(inverse_ref, raw_ref, right_ref, squares_ref):
+    inverse = split(inverse_ref[...])
+    total = jnp.zeros((RANK, WIDE), jnp.float32)
+    for i in range(raw_ref.shape[0]):
+        right = three_dots(inverse, split(raw_ref[i]))
+        right_ref[i] = right
+        total = total + right * right
     squares_ref[...] = lax.dot_general(
         jnp.ones((8, WIDE), jnp.float32),
-        right * right,
+        total,
         (((1,), (1,)), ((), ())),
         precision=HIGH,
         preferred_element_type=jnp.float32,
     )
 
 
-def own_right(inverse, raw, copies):
-    return call(
-        own_kernel,
-        RANK**3,
+def finished(inverse, raw):
+    return call(
+        finished_kernel,
+        RANK**3 * 24,
         RANK * RANK * 32,
         in_specs=[IN_VMEM, IN_VMEM],
         out_specs=(IN_VMEM, IN_VMEM),
         out_shape=(
-            jax.ShapeDtypeStruct((copies, RANK, WIDE), jnp.float32),
+            jax.ShapeDtypeStruct(raw.shape, jnp.float32),
             jax.ShapeDtypeStruct((8, RANK), jnp.float32),
         ),
     )(inverse, raw)
@@ -308,63 +375,107 @@
     )(place, ortho, mine, other, buffer, squares, filled)
 
 
+def ordered(pieces, position):
+    for bit in (1, 2):
+        odd = (position & bit) != 0
+        pieces = [jnp.where(odd, pieces[j ^ bit], pieces[j]) for j in range(4)]
+    return pieces
+
+
+def turned(value, axis, mask):
+    return lax.ppermute(value, axis, [(i, i ^ mask) for i in range(4)])
+
+
+def product_kernel(a_ref, b_ref, out_ref):
+    out_ref[...] = lax.dot_general(
+        a_ref[...], b_ref[...], (((1,), (1,)), ((), ())), precision=HIGH, preferred_element_type=jnp.float32
+    )
+
+
+def lines_product(a, b):
+    return call(
+        product_kernel,
+        0,
+        14_000_000,
+        in_specs=[IN_VMEM, IN_VMEM],
+        out_specs=IN_VMEM,
+        out_shape=jax.ShapeDtypeStruct((a.shape[0], b.shape[0]), jnp.float32),
+    )(a, b)
+
+
+def whole_sum(value, axis):
+    near, across, away = (turned(value, axis, mask) for mask in (1, 2, 3))
+    return (value + near) + (across + away)
+
+
+def whole_sum(value, axis):
+    near, across, away = (turned(value, axis, mask) for mask in (1, 2, 3))
+    return (value + near) + (across + away)
+
+
 def local(gradient, momentum, basis):
     replicas = lax.axis_size("replica")
     rank_local = basis.shape[1]
-    core = lax.axis_index("core")
+    core, y = lax.axis_index("core"), lax.axis_index("y")
     first = core == 0
     mine, theirs = jnp.full((1,), core, jnp.int32), jnp.full((1,), 1 - core, jnp.int32)
-
-    wide = jnp.broadcast_to(basis.T[None], (4, rank_local, basis.shape[0]))
-    wide, momentum, gradient = together(wide, momentum, gradient)
-    lines = lax.all_to_all(wide, "y", 0, 0, tiled=True)
-    buffer = momentum[0] + gradient[0].astype(jnp.float32)
-    lines, buffer = together(lines, buffer)
-    other = swapped(lines)
-    both = jnp.stack([jnp.where(first, lines, other), jnp.where(first, other, lines)], axis=1)
-    basis_t = both.reshape(RANK, basis.shape[0])
+    place = jnp.stack([core, (y * 2 + core) * rank_local]).astype(jnp.int32)
+
+    lines = basis.T
+    lines, momentum, gradient = together(lines, momentum, gradient)
+    across, near, away = (turned(lines, "y", mask) for mask in (2, 1, 3))
+    buffer, far = added(momentum, gradient)
+    there = [swapped(lines)]
+    near, away, buffer = together(near, away, buffer)
+    there += [swapped(near), swapped(across), swapped(away)]
+    here = [lines, near, across, away]
+    blocks = []
+    for ours, others in ((here, there), (there, here)):
+        pieces = [jnp.where(first, one, two) for one, two in zip(ours, others)]
+        blocks.append(jnp.stack(ordered(pieces, y)))
+    basis_t = jnp.stack(blocks, axis=1).reshape(RANK, basis.shape[0])
 
     part = product(buffer, basis_t, ((1,), (1,)), lax.Precision.HIGH)
     own = scattered_sum(scattered_sum(part, "tensor"), "replica") / replicas
     quarter = stacked(own, "replica")
-    wide = jnp.broadcast_to(quarter[None], (4, *quarter.shape))
-    wide, quarter = together(wide, quarter)
-    left = lax.all_to_all(wide, "tensor", 0, 0, tiled=True).reshape(-1, RANK)
-    gram = pair_sum(core_scattered(product(quarter, quarter, ((0,), (0,)))), 1)
-    left, gram = together(left, gram)
+    quarter, far = together(quarter, far)
+    left = [quarter] + [turned(quarter, "tensor", mask) for mask in (1, 2, 3)]
+    buffer = staged(far)
+    *left, buffer = together(*left, buffer)
+    left = jnp.concatenate(ordered(left, lax.axis_index("tensor")), axis=0)
     sent = right_half(theirs, left, buffer)
-    gram = pair_sum(gram, 3)
     sent, left = together(sent, left)
     arrived = swapped(sent)
+    gram = product(left, left, ((0,), (0,)))
     kept = right_half(mine, left, buffer)
     arrived, kept, gram = together(arrived, kept, gram)
     blocks = lax.all_to_all(arrived + kept, "y", 0, 0, tiled=True)
-    gram = core_joined(pair_sum(pair_sum(gram, 1, "tensor"), 3, "tensor"))
+    gram = core_scattered(gram)
     blocks, gram = together(blocks, gram)
     own = blocks.sum(axis=0)
     own, gram = together(own, gram)
     pieces = parted(own, "replica")
-    inverse = jnp.eye(RANK, dtype=jnp.float32)
-    gram, inverse, pieces = together(*factor_part(gram, inverse, 0, 2), pieces)
+    gram = whole_sum(gram, "y")
+    gram, pieces = together(gram, pieces)
     piece = pieces.sum(axis=0) / replicas
     wide = jnp.broadcast_to(piece[None], (replicas, *piece.shape))
     gram, wide = together(gram, wide)
     pieces = lax.all_to_all(wide, "replica", 0, 0, tiled=True)
-    gram, inverse, pieces = together(*factor_part(gram, inverse, 2, 4), pieces)
-    wide, squares = own_right(inverse, pieces.reshape(RANK, WIDE), 4)
-    squares, wide, inverse, left = together(squares, wide, inverse, left)
-    right_mine = lax.all_to_all(wide, "y", 0, 0, tiled=True)
-    ortho = product(left, inverse, ((1,), (1,)))
-    squares = pair_sum(pair_sum(squares, 1, "tensor"), 3, "tensor")
-    squares = pair_sum(pair_sum(squares, 1), 3)
-    right_mine, ortho, squares = together(right_mine, ortho, squares)
+    inverse = jnp.eye(RANK, dtype=jnp.float32)
+    gram, inverse, pieces = together(*factor_part(core_joined(gram), inverse, 0, 1), pieces)
+    wide = jnp.broadcast_to(pieces.reshape(1, RANK, WIDE), (4, RANK, WIDE))
+    gram, wide = together(gram, wide)
+    raw = lax.all_to_all(wide, "y", 0, 0, tiled=True)
+    gram, inverse = factor_part(gram, inverse, 1, 4)
+    ortho = lines_product(left, inverse)
+    ortho, inverse, raw = together(ortho, inverse, raw)
+    right_mine, squares = finished(inverse, raw)
     right_other = swapped(right_mine)
+    squares = whole_sum(squares, "tensor")
+    momentum_new = first_half(mine, ortho, right_mine, far)
+    momentum_new, squares, right_other = together(momentum_new, squares, right_other)
     squares = squares + swapped(squares)
-
-    momentum_new = first_half(mine, ortho, right_mine, buffer)
-    momentum_new, right_other, squares = together(momentum_new, right_other, squares)
-    place = jnp.stack([core, (lax.axis_index("y") * 2 + core) * rank_local]).astype(jnp.int32)
-    momentum_new, update, lines = last_half(place, ortho, right_mine, right_other, buffer, squares, momentum_new)
+    momentum_new, update, lines = last_half(place, ortho, right_mine, right_other, far, squares, momentum_new)
     return (update, momentum_new[None], lines.T)
 
 

time: 183 us -> 172 us (0.940)
  waiting for transfers between devices: 56.3 us -> 35.5 us
  blocking collectives: 28.4 us -> 38.9 us
  local copies, waits for them, and re-layouts: 8.65 us -> 16.1 us
  other arithmetic: 8.29 us -> 3.07 us
  starting transfers between devices: 50.8 us -> 46.1 us
    ppermute x8 -> x12, waiting for transfers between devices: 28.3 us -> 5.87 us  [turned(): return lax.ppermute(value, axis, [(i, i ^ mask) for i in range(4)])]
    all_to_all x4 -> x1, waiting for transfers between devices: 19.9 us -> 3.12 us  [local(): raw = lax.all_to_all(wide, 'y', 0, 0, tiled=True)]
    all_to_all x4 -> x1, starting transfers between devices: 17.5 us -> 3.74 us  [local(): raw = lax.all_to_all(wide, 'y', 0, 0, tiled=True)]
    all_to_all x1, waiting for transfers between devices: 0.81 us -> 12.8 us  [local(): blocks = lax.all_to_all(arrived + kept, 'y', 0, 0, tiled=True)]
    all_to_all x0 -> x1, blocking collectives: none -> 10.4 us  [to_everyone(): lax.all_to_all(jnp.broadcast_to(value[None], (size, *value.shape)), axis,...]
    unnamed x8 -> x16, local copies, waits for them, and re-layouts: 4.38 us -> 14.2 us
    ppermute x8 -> x12, starting transfers between devices: 6.77 us -> 14.8 us  [turned(): return lax.ppermute(value, axis, [(i, i ^ mask) for i in range(4)])]
    all_to_all x1, waiting for transfers between devices: 2.16 us -> 8.5 us  [local(): pieces = lax.all_to_all(wide, 'replica', 0, 0, tiled=True)]
  transfers between devices with their start and end apart: 21 -> 25, of which waited for: 16 -> 13; matrix products, arithmetic and copies ran while one was open for 4% -> 1% of each run, Pallas kernels for 10% -> 12%
where the time goes in v3:
time: 172 us; the launch traced here: 171 us
  starting transfers between devices  46.1 us (27%)
  blocking collectives  38.9 us (23%)
  waiting for transfers between devices  35.5 us (21%)
  Pallas kernels  27.2 us (16%)
  local copies, waits for them, and re-layouts  16.1 us (9%)
  other arithmetic  3.07 us (2%)
  matrix products  2.94 us (2%)
    all_to_all x2, blocking collectives, parted(): return lax.all_to_all(blocks, axis, 0, 0, tiled=True)  28.4 us
    ppermute x9, starting transfers between devices, swapped(): return lax.ppermute(value, 'core', [(0, 1), (1, 0)])  16 us
    ppermute x12, starting transfers between devices, turned(): return lax.ppermute(value, axis, [(i, i ^ mask) for i in range(4)])  14.8 us
    pallas_call x2, Pallas kernels, factor_part(): pl.pallas_call(functools.partial(factor_kernel, first, last), out_shape=(...  14.5 us
    unnamed x16, local copies, waits for them, and re-layouts  14.2 us
    all_to_all x1, waiting for transfers between devices, local(): blocks = lax.all_to_all(arrived + kept, 'y', 0, 0, tiled=True)  12.8 us
    all_to_all x1, blocking collectives, to_everyone(): lax.all_to_all(jnp.broadcast_to(value[None], (size, *value.shape)), axis,...  10.4 us
    all_to_all x1, waiting for transfers between devices, local(): pieces = lax.all_to_all(wide, 'replica', 0, 0, tiled=True)  8.5 us
  transfers between devices with their start and end apart: 25, of which 13 were waited for; matrix products, arithmetic and copies ran while one was open for 1% of the time, Pallas kernels for 12%

profile of v3, /device:TPU:1, one launch (start us, length us, event | category | flops | bytes accessed | tf_op | source)
XLA Modules:
  0.0 171.0 jit_solution(16368905797505235630)
XLA Ops:
  0.6 3.7 %collective-permute-start.1 = (f32[32,2048]{1,0:T(8,128)}, f32[32,2048]{1,0:T(8,128)S(1)}, u32[]{:S(2)}, u32[]{:S(2)}) collective-permute-start(f32[32,2048]{1,0:T(8,128)} %bitcast.47), channel_id=1, source_target_pairs={{0,192},{64,128},{128,64},{192,0},{1,193},{65,129},{129,65},{193,1... | collective-permute-start | bytes 786440 | tf_op jit(solution)/shard_map/ppermute | solution.py:386
  4.3 1.3 collective-permute-start.3
  5.6 3.1 %collective-permute-start.6 = (f32[32,2048]{1,0:T(8,128)}, f32[32,2048]{1,0:T(8,128)S(1)}, u32[]{:S(2)}, u32[]{:S(2)}) collective-permute-start(f32[32,2048]{1,0:T(8,128)} %bitcast.50), channel_id=1, source_target_pairs={{0,32},{32,0},{1,33},{33,1},{2,34},{34,2},{3,35},{35,3},{4,36},{36... | collective-permute-start | bytes 786440 | tf_op jit(solution)/shard_map/ppermute | solution.py:120
  8.7 2.2 %copy-done.3 = f32[1,512,2048]{2,1,0:T(8,128)S(1)} copy-done((f32[1,512,2048]{2,1,0:T(8,128)S(1)}, f32[1,512,2048]{2,1,0:T(8,128)}, u32[]{:S(2)}) %copy-start.3) | copy-done | bytes 4194328
  10.8 1.6 copy-done.6
  12.4 1.2 shard_map.58
  13.7 1.9 %copy-done = f32[512,2048]{1,0:T(8,128)} copy-done((f32[512,2048]{1,0:T(8,128)}, f32[512,2048]{1,0:T(8,128)S(1)}, u32[]{:S(2)}) %copy-start) | copy-done | bytes 4194328
  15.6 2.0 %copy-done.4 = f32[512,2048]{1,0:T(8,128)} copy-done((f32[512,2048]{1,0:T(8,128)}, f32[512,2048]{1,0:T(8,128)S(1)}, u32[]{:S(2)}) %copy-start.4) | copy-done | bytes 4194328
  18.7 1.2 collective-permute-done.4
  21.2 2.0 %copy-done.5 = f32[512,2048]{1,0:T(8,128)S(1)} copy-done((f32[512,2048]{1,0:T(8,128)S(1)}, f32[512,2048]{1,0:T(8,128)}, u32[]{:S(2)}) %copy-start.5) | copy-done | bytes 4194328
  23.2 1.9 %fusion.1 = f32[4,128,256]{2,1,0:T(8,128)S(1)} fusion(f32[4,128,2048]{2,1,0:T(8,128)S(1)} %bitcast.38, f32[256,2048,1]{1,0,2:T(8,128)S(1)} %bitcast.40), kind=kOutput, calls=%fused_computation.48 | convolution fusion | flops 1610612736 | bytes 6815744 | tf_op jit(solution)/shard_map/dot_general | solution.py:142
  25.2 12.4 %all_to_all.35 = f32[4,128,256]{2,1,0:T(8,128)S(1)} all-to-all(f32[4,128,256]{2,1,0:T(8,128)S(1)} %fusion.1), channel_id=1, replica_groups=mesh['y'=4,'core'=2,'tensor'=4,'replica'=8] {'tensor'}, dimensions={0} | all-to-all | bytes 1048576 | tf_op jit(solution)/shard_map/all_to_all | solution.py:108
  37.6 16.0 %all_to_all.36 = f32[8,16,256]{2,1,0:T(8,128)S(1)} all-to-all(f32[8,16,256]{2,1,0:T(8,128)S(1)} %bitcast.46), channel_id=1, replica_groups=mesh['y'=4,'core'=2,'tensor'=4,'replica'=8] {'replica'}, dimensions={0} | all-to-all | bytes 262144 | tf_op jit(solution)/shard_map/all_to_all | solution.py:108
  53.7 10.4 %all_to_all.37 = f32[8,16,256]{2,1,0:T(8,128)S(1)} all-to-all(f32[8,16,256]{2,1,0:T(8,128)S(1)} %broadcast_in_dim.13), channel_id=1, replica_groups=mesh['y'=4,'core'=2,'tensor'=4,'replica'=8] {'replica'}, dimensions={0} | all-to-all | bytes 262144 | tf_op jit(solution)/shard_map/all_to_all | solution.py:95
  65.0 1.2 collective-permute-start.8
  66.2 1.2 collective-permute-start.7
  67.4 2.2 %copy-done.1 = f32[512,2048]{1,0:T(8,128)S(1)} copy-done((f32[512,2048]{1,0:T(8,128)S(1)}, f32[512,2048]{1,0:T(8,128)}, u32[]{:S(2)}) %copy-start.1) | copy-done | bytes 4194328
  71.2 1.1 shard_map.60
  72.3 5.9 %collective-permute-start.10 = (f32[4,256,256]{2,1,0:T(8,128)S(1)}, f32[4,256,256]{2,1,0:T(8,128)S(1)}, u32[]{:S(2)}, u32[]{:S(2)}) collective-permute-start(f32[4,256,256]{2,1,0:T(8,128)S(1)} %shard_map.60), channel_id=1, source_target_pairs={{0,32},{32,0},{1,33},{33,1},{2,34},{34,2},{3,35},{35,3},{4,36},{36... | collective-permute-start | bytes 3145736 | tf_op jit(solution)/shard_map/ppermute | solution.py:120
  78.2 1.1 shard_map.61
  79.3 1.0 fusion.2
  80.5 1.1 add.37
  81.6 3.9 %all-to-all-start.3 = ((f32[4,256,256]{2,1,0:T(8,128)}), f32[4,256,256]{2,1,0:T(8,128)S(1)}, u32[]{:S(2)}, u32[]{:S(2)}) async-start(f32[4,256,256]{2,1,0:T(8,128)} %add.37), calls=%async_computation.3 | async-start | bytes 2097152 | tf_op jit(solution)/shard_map/all_to_all | solution.py:452
  86.2 1.0 collective-permute-done.11
  87.2 12.8 %all-to-all-done.3 = f32[4,256,256]{2,1,0:T(8,128)S(1)} async-done(((f32[4,256,256]{2,1,0:T(8,128)}), f32[4,256,256]{2,1,0:T(8,128)S(1)}, u32[]{:S(2)}, u32[]{:S(2)}) %all-to-all-start.3) | async-done | bytes 1048608 | tf_op jit(solution)/shard_map/all_to_all | solution.py:452
  100.8 3.4 %all-to-all-start.4 = ((f32[8,32,256]{2,1,0:T(8,128)}), f32[8,32,256]{2,1,0:T(8,128)S(1)}, u32[]{:S(2)}, u32[]{:S(2)}) async-start(f32[8,32,256]{2,1,0:T(8,128)} %bitcast.19), calls=%async_computation.4 | async-start | bytes 524288 | tf_op jit(solution)/shard_map/all_to_all | solution.py:108
  105.2 1.2 collective-permute-start.13
  106.4 1.2 collective-permute-start.12
  107.5 3.5 %collective-permute-done.14 = f32[128,256]{1,0:T(8,128)S(1)} collective-permute-done((f32[128,256]{1,0:T(8,128)S(1)}, f32[128,256]{1,0:T(8,128)S(1)}, u32[]{:S(2)}, u32[]{:S(2)}) %collective-permute-start.14) | collective-permute-done | bytes 131104 | tf_op jit(solution)/shard_map/ppermute | solution.py:386
  111.1 1.1 collective-permute-done.12
  112.2 1.8 %all-to-all-done.4 = f32[8,32,256]{2,1,0:T(8,128)S(1)} async-done(((f32[8,32,256]{2,1,0:T(8,128)}), f32[8,32,256]{2,1,0:T(8,128)S(1)}, u32[]{:S(2)}, u32[]{:S(2)}) %all-to-all-start.4) | async-done | bytes 262176 | tf_op jit(solution)/shard_map/all_to_all | solution.py:108
  114.8 2.9 %collective-permute-start.15 = (f32[128,256]{1,0:T(8,128)S(1)}, f32[128,256]{1,0:T(8,128)S(1)}, u32[]{:S(2)}, u32[]{:S(2)}) collective-permute-start(f32[128,256]{1,0:T(8,128)S(1)} %add_add_fusion), channel_id=1, source_target_pairs={{0,32},{32,0},{1,33},{33,1},{2,34},{34,2},{3,35},{35,3},{4,36},{36... | collective-permute-start | bytes 393224 | tf_op jit(solution)/shard_map/ppermute | solution.py:120
  117.7 4.4 %all-to-all-start.5 = ((f32[8,32,256]{2,1,0:T(8,128)}), f32[8,32,256]{2,1,0:T(8,128)S(1)}, u32[]{:S(2)}, u32[]{:S(2)}) async-start(f32[8,32,256]{2,1,0:T(8,128)} %broadcast_in_dim.28), calls=%async_computation.5 | async-start | bytes 524288 | tf_op jit(solution)/shard_map/all_to_all | solution.py:463
  122.2 3.8 %shard_map.62 = (f32[256,256]{1,0:T(8,128)S(1)}, f32[256,256]{1,0:T(8,128)S(1)}) custom-call(f32[256,256]{1,0:T(8,128)S(1)} %pad_maximum_fusion.2.gram_ref, f32[256,256]{1,0:T(8,128)S(1)} %fusion.inv_ref), custom_call_target="tpu_custom_call" | custom-call | bytes 10000 | tf_op jit(solution)/shard_map/pallas_call | solution.py:86
  126.0 8.5 %all-to-all-done.5 = f32[8,32,256]{2,1,0:T(8,128)S(1)} async-done(((f32[8,32,256]{2,1,0:T(8,128)}), f32[8,32,256]{2,1,0:T(8,128)S(1)}, u32[]{:S(2)}, u32[]{:S(2)}) %all-to-all-start.5) | async-done | bytes 262176 | tf_op jit(solution)/shard_map/all_to_all | solution.py:463
  134.5 1.1 broadcast_in_dim.30
  135.5 3.7 %all-to-all-start.6 = ((f32[4,256,256]{2,1,0:T(8,128)}), f32[4,256,256]{2,1,0:T(8,128)S(1)}, u32[]{:S(2)}, u32[]{:S(2)}) async-start(f32[4,256,256]{2,1,0:T(8,128)} %broadcast_in_dim.30), calls=%async_computation.6 | async-start | bytes 2097152 | tf_op jit(solution)/shard_map/all_to_all | solution.py:468
  139.3 10.7 %shard_map.63 = (f32[256,256]{1,0:T(8,128)}, f32[256,256]{1,0:T(8,128)S(1)}) custom-call(f32[256,256]{1,0:T(8,128)S(1)} %get-tuple-element.82.gram_ref, f32[256,256]{1,0:T(8,128)S(1)} %get-tuple-element.83.inv_ref), custom_call_target="tpu_custom_call" | custom-call | bytes 30000 | tf_op jit(solution)/shard_map/pallas_call | solution.py:86
  150.6 3.1 %all-to-all-done.6.raw_ref = f32[4,256,256]{2,1,0:T(8,128)S(1)} async-done(((f32[4,256,256]{2,1,0:T(8,128)}), f32[4,256,256]{2,1,0:T(8,128)S(1)}, u32[]{:S(2)}, u32[]{:S(2)}) %all-to-all-start.6) | async-done | bytes 1048608 | tf_op jit(solution)/shard_map/all_to_all | solution.py:468
  153.7 1.1 shard_map.65
  154.8 1.3 collective-permute-start.19
  156.2 1.0 collective-permute-start.18
  157.2 1.1 collective-permute-start.17
  158.3 1.1 collective-permute-start.16
  159.4 2.2 %copy-done.2 = f32[512,2048]{1,0:T(8,128)S(1)} copy-done((f32[512,2048]{1,0:T(8,128)S(1)}, f32[512,2048]{1,0:T(8,128)}, u32[]{:S(2)}) %copy-start.2) | copy-done | bytes 4194328
  161.6 2.1 %shard_map.66.filled_ref = f32[512,2048]{1,0:T(8,128)} custom-call(s32[1]{0:T(128)} %bitcast.half_ref, f32[512,256]{1,0:T(8,128)S(1)} %shard_map.64.ortho_ref, f32[4,256,256]{2,1,0:T(8,128)S(1)} %get-tuple-element.89.right_ref.mine_ref, f32[512,2048]{1,0:T(8,128)S(1)} %copy-done.2), custom_call_target="tpu_custom_call" | custom-call | flops 805306368 | bytes 4194304 | tf_op jit(solution)/shard_map/pallas_call | solution.py:313
  163.8 1.0 collective-permute-start.20
  165.6 5.1 %shard_map.67 = (f32[512,2048]{1,0:T(8,128)}, bf16[512,2048]{1,0:T(8,128)(2,1)}, f32[32,2048]{1,0:T(8,128)}) custom-call(s32[2]{0:T(128)S(1)} %pad_add_fusion.place_ref, f32[512,256]{1,0:T(8,128)S(1)} %shard_map.64.ortho_ref, f32[4,256,256]{2,1,0:T(8,128)S(1)} %get-tuple-element.89.right_ref.mine_ref, ...), custom_call_target="tpu_custom_call", output_to_operand_aliasing={{0}: (6, {})} | custom-call | flops 2415919104 | bytes 8388608 | tf_op jit(solution)/shard_map/pallas_call | solution.py:356
  (60 shorter events, 9.9 us)
Async XLA Ops:
  0.6 17.0 %collective-permute-start.1 = (f32[32,2048]{1,0:T(8,128)}, f32[32,2048]{1,0:T(8,128)S(1)}, u32[]{:S(2)}, u32[]{:S(2)}) collective-permute-start(f32[32,2048]{1,0:T(8,128)} %bitcast.47), channel_id=1, source_target_pairs={{0,192},{64,128},{128,64},{192,0},{1,193},{65,129},{129,65},{193,1... | collective-permute-start | bytes 786440 | tf_op jit(solution)/shard_map/ppermute | solution.py:386
  4.3 13.4 %collective-permute-start = (f32[32,2048]{1,0:T(8,128)}, f32[32,2048]{1,0:T(8,128)S(1)}, u32[]{:S(2)}, u32[]{:S(2)}) collective-permute-start(f32[32,2048]{1,0:T(8,128)} %bitcast.48), channel_id=1, source_target_pairs={{0,64},{64,0},{128,192},{192,128},{1,65},{65,1},{129,193},{193,129... | collective-permute-start | bytes 786440 | tf_op jit(solution)/shard_map/ppermute | solution.py:386
  4.3 13.4 %collective-permute-start.3 = (f32[32,2048]{1,0:T(8,128)}, f32[32,2048]{1,0:T(8,128)S(1)}, u32[]{:S(2)}, u32[]{:S(2)}) collective-permute-start(f32[32,2048]{1,0:T(8,128)} %bitcast.49), channel_id=1, source_target_pairs={{0,128},{64,192},{128,0},{192,64},{1,129},{65,193},{129,1},{193,65... | collective-permute-start | bytes 786440 | tf_op jit(solution)/shard_map/ppermute | solution.py:386
  5.6 13.1 %collective-permute-start.6 = (f32[32,2048]{1,0:T(8,128)}, f32[32,2048]{1,0:T(8,128)S(1)}, u32[]{:S(2)}, u32[]{:S(2)}) collective-permute-start(f32[32,2048]{1,0:T(8,128)} %bitcast.50), channel_id=1, source_target_pairs={{0,32},{32,0},{1,33},{33,1},{2,34},{34,2},{3,35},{35,3},{4,36},{36... | collective-permute-start | bytes 786440 | tf_op jit(solution)/shard_map/ppermute | solution.py:120
  8.7 2.2 %copy-start.3 = (f32[1,512,2048]{2,1,0:T(8,128)S(1)}, f32[1,512,2048]{2,1,0:T(8,128)}, u32[]{:S(2)}) copy-start(f32[1,512,2048]{2,1,0:T(8,128)} %momentum_ref) | copy-start | bytes 12582916
  10.8 1.6 copy-start.6
  12.4 7.7 %copy-start.7 = (f32[2048,32]{0,1:T(8,128)S(1)}, f32[2048,32]{0,1:T(8,128)}, u32[]{:S(2)}) copy-start(f32[2048,32]{0,1:T(8,128)} %param.5) | copy-start | bytes 786436
  13.7 2.0 %copy-start = (f32[512,2048]{1,0:T(8,128)}, f32[512,2048]{1,0:T(8,128)S(1)}, u32[]{:S(2)}) copy-start(f32[512,2048]{1,0:T(8,128)S(1)} %get-tuple-element.59.far_ref.buffer_ref) | copy-start | bytes 12582916
  15.6 2.0 %copy-start.4 = (f32[512,2048]{1,0:T(8,128)}, f32[512,2048]{1,0:T(8,128)S(1)}, u32[]{:S(2)}) copy-start(f32[512,2048]{1,0:T(8,128)S(1)} %get-tuple-element.54) | copy-start | bytes 12582916
  17.6 2.2 %collective-permute-start.2 = (f32[32,2048]{1,0:T(8,128)S(1)}, f32[32,2048]{1,0:T(8,128)S(1)}, u32[]{:S(2)}, u32[]{:S(2)}) collective-permute-start(f32[32,2048]{1,0:T(8,128)S(1)} %collective-permute-done.1), channel_id=1, source_target_pairs={{0,32},{32,0},{1,33},{33,1},{2,34},{34,2},{3,35},{35,3},{4,36},{36... | collective-permute-start | bytes 786440 | tf_op jit(solution)/shard_map/ppermute | solution.py:120
  17.7 2.1 %collective-permute-start.4 = (f32[32,2048]{1,0:T(8,128)S(1)}, f32[32,2048]{1,0:T(8,128)S(1)}, u32[]{:S(2)}, u32[]{:S(2)}) collective-permute-start(f32[32,2048]{1,0:T(8,128)S(1)} %collective-permute-done.3), channel_id=1, source_target_pairs={{0,32},{32,0},{1,33},{33,1},{2,34},{34,2},{3,35},{35,3},{4,36},{36... | collective-permute-start | bytes 786440 | tf_op jit(solution)/shard_map/ppermute | solution.py:120
  18.6 1.5 collective-permute-start.5
  21.1 2.2 %copy-start.5 = (f32[512,2048]{1,0:T(8,128)S(1)}, f32[512,2048]{1,0:T(8,128)}, u32[]{:S(2)}) copy-start(f32[512,2048]{1,0:T(8,128)} %copy-done.4) | copy-start | bytes 12582916
  64.1 6.4 %collective-permute-start.9 = (f32[128,256]{1,0:T(8,128)S(1)}, f32[128,256]{1,0:T(8,128)S(1)}, u32[]{:S(2)}, u32[]{:S(2)}) collective-permute-start(f32[128,256]{1,0:T(8,128)S(1)} %bitcast.42), channel_id=1, source_target_pairs={{0,24},{8,16},{16,8},{24,0},{1,25},{9,17},{17,9},{25,1},{2,26},{10... | collective-permute-start | bytes 393224 | tf_op jit(solution)/shard_map/ppermute | solution.py:386
  65.0 5.6 %collective-permute-start.8 = (f32[128,256]{1,0:T(8,128)S(1)}, f32[128,256]{1,0:T(8,128)S(1)}, u32[]{:S(2)}, u32[]{:S(2)}) collective-permute-start(f32[128,256]{1,0:T(8,128)S(1)} %bitcast.43), channel_id=1, source_target_pairs={{0,16},{8,24},{16,0},{24,8},{1,17},{9,25},{17,1},{25,9},{2,18},{10... | collective-permute-start | bytes 393224 | tf_op jit(solution)/shard_map/ppermute | solution.py:386
  66.2 4.9 %collective-permute-start.7 = (f32[128,256]{1,0:T(8,128)S(1)}, f32[128,256]{1,0:T(8,128)S(1)}, u32[]{:S(2)}, u32[]{:S(2)}) collective-permute-start(f32[128,256]{1,0:T(8,128)S(1)} %bitcast.44), channel_id=1, source_target_pairs={{0,8},{8,0},{16,24},{24,16},{1,9},{9,1},{17,25},{25,17},{2,10},{10... | collective-permute-start | bytes 393224 | tf_op jit(solution)/shard_map/ppermute | solution.py:386
  67.4 2.2 %copy-start.1 = (f32[512,2048]{1,0:T(8,128)S(1)}, f32[512,2048]{1,0:T(8,128)}, u32[]{:S(2)}) copy-start(f32[512,2048]{1,0:T(8,128)} %copy-done) | copy-start | bytes 12582916
  72.3 8.2 %collective-permute-start.10 = (f32[4,256,256]{2,1,0:T(8,128)S(1)}, f32[4,256,256]{2,1,0:T(8,128)S(1)}, u32[]{:S(2)}, u32[]{:S(2)}) collective-permute-start(f32[4,256,256]{2,1,0:T(8,128)S(1)} %shard_map.60), channel_id=1, source_target_pairs={{0,32},{32,0},{1,33},{33,1},{2,34},{34,2},{3,35},{35,3},{4,36},{36... | collective-permute-start | bytes 3145736 | tf_op jit(solution)/shard_map/ppermute | solution.py:120
  81.6 18.4 %all-to-all-start.3 = ((f32[4,256,256]{2,1,0:T(8,128)}), f32[4,256,256]{2,1,0:T(8,128)S(1)}, u32[]{:S(2)}, u32[]{:S(2)}) async-start(f32[4,256,256]{2,1,0:T(8,128)} %add.37), calls=%async_computation.3 | async-start | bytes 2097152 | tf_op jit(solution)/shard_map/all_to_all | solution.py:452
  85.5 1.7 %collective-permute-start.11 = (f32[128,256]{1,0:T(8,128)S(1)}, f32[128,256]{1,0:T(8,128)S(1)}, u32[]{:S(2)}, u32[]{:S(2)}) collective-permute-start(f32[128,256]{1,0:T(8,128)S(1)} %constant_dynamic-slice_fusion), channel_id=1, source_target_pairs={{0,32},{32,0},{1,33},{33,1},{2,34},{34,2},{3,35},{35,3},{4,36},{36... | collective-permute-start | bytes 393224 | tf_op jit(solution)/shard_map/ppermute | solution.py:120
  100.8 13.2 %all-to-all-start.4 = ((f32[8,32,256]{2,1,0:T(8,128)}), f32[8,32,256]{2,1,0:T(8,128)S(1)}, u32[]{:S(2)}, u32[]{:S(2)}) async-start(f32[8,32,256]{2,1,0:T(8,128)} %bitcast.19), calls=%async_computation.4 | async-start | bytes 524288 | tf_op jit(solution)/shard_map/all_to_all | solution.py:108
  104.2 6.9 %collective-permute-start.14 = (f32[128,256]{1,0:T(8,128)S(1)}, f32[128,256]{1,0:T(8,128)S(1)}, u32[]{:S(2)}, u32[]{:S(2)}) collective-permute-start(f32[128,256]{1,0:T(8,128)S(1)} %dynamic-slice_add_fusion), channel_id=1, source_target_pairs={{0,192},{64,128},{128,64},{192,0},{1,193},{65,129},{129,65},{193,1... | collective-permute-start | bytes 393224 | tf_op jit(solution)/shard_map/ppermute | solution.py:386
  105.2 5.9 %collective-permute-start.13 = (f32[128,256]{1,0:T(8,128)S(1)}, f32[128,256]{1,0:T(8,128)S(1)}, u32[]{:S(2)}, u32[]{:S(2)}) collective-permute-start(f32[128,256]{1,0:T(8,128)S(1)} %dynamic-slice_add_fusion), channel_id=1, source_target_pairs={{0,128},{64,192},{128,0},{192,64},{1,129},{65,193},{129,1},{193,65... | collective-permute-start | bytes 393224 | tf_op jit(solution)/shard_map/ppermute | solution.py:386
  106.4 5.8 %collective-permute-start.12 = (f32[128,256]{1,0:T(8,128)S(1)}, f32[128,256]{1,0:T(8,128)S(1)}, u32[]{:S(2)}, u32[]{:S(2)}) collective-permute-start(f32[128,256]{1,0:T(8,128)S(1)} %dynamic-slice_add_fusion), channel_id=1, source_target_pairs={{0,64},{64,0},{128,192},{192,128},{1,65},{65,1},{129,193},{193,129... | collective-permute-start | bytes 393224 | tf_op jit(solution)/shard_map/ppermute | solution.py:386
  114.8 7.3 %collective-permute-start.15 = (f32[128,256]{1,0:T(8,128)S(1)}, f32[128,256]{1,0:T(8,128)S(1)}, u32[]{:S(2)}, u32[]{:S(2)}) collective-permute-start(f32[128,256]{1,0:T(8,128)S(1)} %add_add_fusion), channel_id=1, source_target_pairs={{0,32},{32,0},{1,33},{33,1},{2,34},{34,2},{3,35},{35,3},{4,36},{36... | collective-permute-start | bytes 393224 | tf_op jit(solution)/shard_map/ppermute | solution.py:120
  117.7 16.8 %all-to-all-start.5 = ((f32[8,32,256]{2,1,0:T(8,128)}), f32[8,32,256]{2,1,0:T(8,128)S(1)}, u32[]{:S(2)}, u32[]{:S(2)}) async-start(f32[8,32,256]{2,1,0:T(8,128)} %broadcast_in_dim.28), calls=%async_computation.5 | async-start | bytes 524288 | tf_op jit(solution)/shard_map/all_to_all | solution.py:463
  135.5 18.2 %all-to-all-start.6 = ((f32[4,256,256]{2,1,0:T(8,128)}), f32[4,256,256]{2,1,0:T(8,128)S(1)}, u32[]{:S(2)}, u32[]{:S(2)}) async-start(f32[4,256,256]{2,1,0:T(8,128)} %broadcast_in_dim.30), calls=%async_computation.6 | async-start | bytes 2097152 | tf_op jit(solution)/shard_map/all_to_all | solution.py:468
  154.8 9.0 %collective-permute-start.19 = (f32[4,256,256]{2,1,0:T(8,128)S(1)}, f32[4,256,256]{2,1,0:T(8,128)S(1)}, u32[]{:S(2)}, u32[]{:S(2)}) collective-permute-start(f32[4,256,256]{2,1,0:T(8,128)S(1)} %get-tuple-element.89.right_ref.mine_ref), channel_id=1, source_target_pairs={{0,32},{32,0},{1,33},{33,1},{2,34},{34,2},{3,35},{35,3},{4,36},{36... | collective-permute-start | bytes 3145736 | tf_op jit(solution)/shard_map/ppermute | solution.py:120
  156.2 7.6 %collective-permute-start.18 = (f32[8,256]{1,0:T(8,128)S(1)}, f32[8,256]{1,0:T(8,128)S(1)}, u32[]{:S(2)}, u32[]{:S(2)}) collective-permute-start(f32[8,256]{1,0:T(8,128)S(1)} %get-tuple-element.90), channel_id=1, source_target_pairs={{0,24},{8,16},{16,8},{24,0},{1,25},{9,17},{17,9},{25,1},{2,26},{10... | collective-permute-start | bytes 24584 | tf_op jit(solution)/shard_map/ppermute | solution.py:386
  157.2 6.6 %collective-permute-start.17 = (f32[8,256]{1,0:T(8,128)S(1)}, f32[8,256]{1,0:T(8,128)S(1)}, u32[]{:S(2)}, u32[]{:S(2)}) collective-permute-start(f32[8,256]{1,0:T(8,128)S(1)} %get-tuple-element.90), channel_id=1, source_target_pairs={{0,16},{8,24},{16,0},{24,8},{1,17},{9,25},{17,1},{25,9},{2,18},{10... | collective-permute-start | bytes 24584 | tf_op jit(solution)/shard_map/ppermute | solution.py:386
  158.3 5.5 %collective-permute-start.16 = (f32[8,256]{1,0:T(8,128)S(1)}, f32[8,256]{1,0:T(8,128)S(1)}, u32[]{:S(2)}, u32[]{:S(2)}) collective-permute-start(f32[8,256]{1,0:T(8,128)S(1)} %get-tuple-element.90), channel_id=1, source_target_pairs={{0,8},{8,0},{16,24},{24,16},{1,9},{9,1},{17,25},{25,17},{2,10},{10... | collective-permute-start | bytes 24584 | tf_op jit(solution)/shard_map/ppermute | solution.py:386
  159.4 2.2 %copy-start.2 = (f32[512,2048]{1,0:T(8,128)S(1)}, f32[512,2048]{1,0:T(8,128)}, u32[]{:S(2)}) copy-start(f32[512,2048]{1,0:T(8,128)} %copy-done) | copy-start | bytes 12582916
  163.8 1.8 %collective-permute-start.20 = (f32[8,256]{1,0:T(8,128)S(1)}, f32[8,256]{1,0:T(8,128)S(1)}, u32[]{:S(2)}, u32[]{:S(2)}) collective-permute-start(f32[8,256]{1,0:T(8,128)S(1)} %add_add_fusion.1), channel_id=1, source_target_pairs={{0,32},{32,0},{1,33},{33,1},{2,34},{34,2},{3,35},{35,3},{4,36},{36... | collective-permute-start | bytes 24584 | tf_op jit(solution)/shard_map/ppermute | solution.py:120

commit v4 on v3

--- a/solution.py
+++ b/solution.py
@@ -238,24 +238,26 @@
     )(far)
 
 
-def right_kernel(half_ref, left_ref, buffer_ref, out_ref):
-    count = out_ref.shape[0]
+def right_kernel(place_ref, left_ref, buffer_ref, sent_ref, kept_ref):
+    count = kept_ref.shape[0]
     left = split(left_ref[...].T)
-    for i in range(count):
-        block = block_of(buffer_ref, half_ref[0] * count + i)[...]
-        out_ref[i] = three_dots(left, split(block))
-
-
-def right_half(half, left, buffer):
+    for core, out_ref in ((1 - place_ref[0], sent_ref), (place_ref[0], kept_ref)):
+        for turn in range(count):
+            block = block_of(buffer_ref, core * count + (place_ref[1] ^ turn))[...]
+            out_ref[turn] = three_dots(left, split(block))
+
+
+def right_parts(place, left, buffer):
     rows, columns = buffer.shape
+    shape = jax.ShapeDtypeStruct((columns // WIDE // 2, RANK, WIDE), jnp.float32)
     return call(
         right_kernel,
-        3 * rows * RANK * columns,
-        4 * rows * columns,
+        6 * rows * RANK * columns,
+        8 * rows * columns,
         in_specs=[IN_SMEM, IN_VMEM, IN_VMEM],
-        out_specs=IN_VMEM,
-        out_shape=jax.ShapeDtypeStruct((columns // WIDE // 2, RANK, WIDE), jnp.float32),
-    )(half, left, buffer)
+        out_specs=(IN_VMEM, IN_VMEM),
+        out_shape=(shape, shape),
+    )(place, left, buffer)
 
 
 def finished_kernel(inverse_ref, raw_ref, right_ref, squares_ref):
@@ -403,6 +405,16 @@
     )(a, b)
 
 
+def owner_sum(blocks, axis):
+    position = lax.axis_index(axis)
+
+    def picked(mask):
+        return lax.dynamic_index_in_dim(blocks, position ^ mask, 0, keepdims=False)
+
+    across, near, away = (turned(picked(mask), axis, mask) for mask in (2, 1, 3))
+    return (picked(0) + near) + (across + away)
+
+
 def whole_sum(value, axis):
     near, across, away = (turned(value, axis, mask) for mask in (1, 2, 3))
     return (value + near) + (across + away)
@@ -418,7 +430,7 @@
     rank_local = basis.shape[1]
     core, y = lax.axis_index("core"), lax.axis_index("y")
     first = core == 0
-    mine, theirs = jnp.full((1,), core, jnp.int32), jnp.full((1,), 1 - core, jnp.int32)
+    mine = jnp.full((1,), core, jnp.int32)
     place = jnp.stack([core, (y * 2 + core) * rank_local]).astype(jnp.int32)
 
     lines = basis.T
@@ -436,23 +448,23 @@
     basis_t = jnp.stack(blocks, axis=1).reshape(RANK, basis.shape[0])
 
     part = product(buffer, basis_t, ((1,), (1,)), lax.Precision.HIGH)
-    own = scattered_sum(scattered_sum(part, "tensor"), "replica") / replicas
+    part = owner_sum(part.reshape(4, -1, RANK), "tensor")
+    own = scattered_sum(part, "replica") / replicas
     quarter = stacked(own, "replica")
     quarter, far = together(quarter, far)
     left = [quarter] + [turned(quarter, "tensor", mask) for mask in (1, 2, 3)]
     buffer = staged(far)
     *left, buffer = together(*left, buffer)
     left = jnp.concatenate(ordered(left, lax.axis_index("tensor")), axis=0)
-    sent = right_half(theirs, left, buffer)
-    sent, left = together(sent, left)
+    sent, kept = right_parts(jnp.stack([core, y]).astype(jnp.int32), left, buffer)
+    sent, kept, left = together(sent, kept, left)
     arrived = swapped(sent)
     gram = product(left, left, ((0,), (0,)))
-    kept = right_half(mine, left, buffer)
-    arrived, kept, gram = together(arrived, kept, gram)
-    blocks = lax.all_to_all(arrived + kept, "y", 0, 0, tiled=True)
+    arrived, gram = together(arrived, gram)
+    own, *others = [arrived[turn] + kept[turn] for turn in range(4)]
+    across, near, away = (turned(others[mask - 1], "y", mask) for mask in (2, 1, 3))
+    own = (own + near) + (across + away)
     gram = core_scattered(gram)
-    blocks, gram = together(blocks, gram)
-    own = blocks.sum(axis=0)
     own, gram = together(own, gram)
     pieces = parted(own, "replica")
     gram = whole_sum(gram, "y")

time: 172 us -> 169 us (0.983)
  blocking collectives: 38.9 us -> 26.4 us
  waiting for transfers between devices: 35.5 us -> 41.2 us
  starting transfers between devices: 46.1 us -> 49.1 us
    ppermute x12 -> x18, waiting for transfers between devices: 5.87 us -> 24.2 us  [turned(): return lax.ppermute(value, axis, [(i, i ^ mask) for i in range(4)])]
    all_to_all x1 -> x0, waiting for transfers between devices: 12.8 us -> none  [local(): blocks = lax.all_to_all(arrived + kept, 'y', 0, 0, tiled=True)]
    all_to_all x2 -> x1, blocking collectives: 28.4 us -> 16 us  [parted(): return lax.all_to_all(blocks, axis, 0, 0, tiled=True)]
    ppermute x12 -> x18, starting transfers between devices: 14.8 us -> 21.5 us  [turned(): return lax.ppermute(value, axis, [(i, i ^ mask) for i in range(4)])]
    all_to_all x1 -> x0, starting transfers between devices: 3.85 us -> none  [local(): blocks = lax.all_to_all(arrived + kept, 'y', 0, 0, tiled=True)]
    add x1 -> x3, other arithmetic: 1.11 us -> 3.06 us  [the longest x1 1.82 us: local(): own = own + near + (across + away)]
  transfers between devices with their start and end apart: 25 -> 30, of which waited for: 13 -> 15; matrix products, arithmetic and copies ran while one was open for 1% -> 1% of each run, Pallas kernels for 12% -> 11%
where the time goes in v4:
time: 169 us
  starting transfers between devices  49.1 us (29%)
  waiting for transfers between devices  41.2 us (24%)
  Pallas kernels  27.5 us (16%)
  blocking collectives  26.4 us (16%)
  local copies, waits for them, and re-layouts  16.1 us (10%)
  other arithmetic  4.28 us (3%)
  matrix products  2.94 us (2%)
    ppermute x18, waiting for transfers between devices, turned(): return lax.ppermute(value, axis, [(i, i ^ mask) for i in range(4)])  24.2 us
    ppermute x18, starting transfers between devices, turned(): return lax.ppermute(value, axis, [(i, i ^ mask) for i in range(4)])  21.5 us
    all_to_all x1, blocking collectives, parted(): return lax.all_to_all(blocks, axis, 0, 0, tiled=True)  16 us
    ppermute x9, starting transfers between devices, swapped(): return lax.ppermute(value, 'core', [(0, 1), (1, 0)])  15.2 us
    pallas_call x2, Pallas kernels, factor_part(): pl.pallas_call(functools.partial(factor_kernel, first, last), out_shape=(...  14.5 us
    unnamed x16, local copies, waits for them, and re-layouts  14.2 us
    all_to_all x1, blocking collectives, to_everyone(): lax.all_to_all(jnp.broadcast_to(value[None], (size, *value.shape)), axis,...  10.4 us
    all_to_all x1, waiting for transfers between devices, local(): pieces = lax.all_to_all(wide, 'replica', 0, 0, tiled=True)  8.51 us
  transfers between devices with their start and end apart: 30, of which 15 were waited for; matrix products, arithmetic and copies ran while one was open for 1% of the time, Pallas kernels for 11%

profile of v4, /device:TPU:1, one launch (start us, length us, event | category | flops | bytes accessed | tf_op | source)
XLA Modules:
  0.0 168.8 jit_solution(11659806877369079587)
XLA Ops:
  0.6 3.7 %collective-permute-start.1 = (f32[32,2048]{1,0:T(8,128)}, f32[32,2048]{1,0:T(8,128)S(1)}, u32[]{:S(2)}, u32[]{:S(2)}) collective-permute-start(f32[32,2048]{1,0:T(8,128)} %bitcast.67), channel_id=1, source_target_pairs={{0,192},{64,128},{128,64},{192,0},{1,193},{65,129},{129,65},{193,1... | collective-permute-start | bytes 786440 | tf_op jit(solution)/shard_map/ppermute | solution.py:388
  4.3 1.3 collective-permute-start.3
  5.6 3.1 %collective-permute-start.6 = (f32[32,2048]{1,0:T(8,128)}, f32[32,2048]{1,0:T(8,128)S(1)}, u32[]{:S(2)}, u32[]{:S(2)}) collective-permute-start(f32[32,2048]{1,0:T(8,128)} %bitcast.70), channel_id=1, source_target_pairs={{0,32},{32,0},{1,33},{33,1},{2,34},{34,2},{3,35},{35,3},{4,36},{36... | collective-permute-start | bytes 786440 | tf_op jit(solution)/shard_map/ppermute | solution.py:120
  8.7 2.2 %copy-done.3 = f32[1,512,2048]{2,1,0:T(8,128)S(1)} copy-done((f32[1,512,2048]{2,1,0:T(8,128)S(1)}, f32[1,512,2048]{2,1,0:T(8,128)}, u32[]{:S(2)}) %copy-start.3) | copy-done | bytes 4194328
  10.8 1.6 copy-done.6
  12.4 1.2 shard_map.58
  13.7 2.0 %copy-done = f32[512,2048]{1,0:T(8,128)} copy-done((f32[512,2048]{1,0:T(8,128)}, f32[512,2048]{1,0:T(8,128)S(1)}, u32[]{:S(2)}) %copy-start) | copy-done | bytes 4194328
  15.6 2.0 %copy-done.4 = f32[512,2048]{1,0:T(8,128)} copy-done((f32[512,2048]{1,0:T(8,128)}, f32[512,2048]{1,0:T(8,128)S(1)}, u32[]{:S(2)}) %copy-start.4) | copy-done | bytes 4194328
  17.7 1.0 collective-permute-start.4
  18.7 1.2 collective-permute-done.4
  21.2 2.0 %copy-done.5 = f32[512,2048]{1,0:T(8,128)S(1)} copy-done((f32[512,2048]{1,0:T(8,128)S(1)}, f32[512,2048]{1,0:T(8,128)}, u32[]{:S(2)}) %copy-start.5) | copy-done | bytes 4194328
  23.2 1.9 %fusion.3 = f32[4,128,256]{2,1,0:T(8,128)S(1)} fusion(f32[4,128,2048]{2,1,0:T(8,128)S(1)} %bitcast.58, f32[256,2048,1]{1,0,2:T(8,128)S(1)} %bitcast.60), kind=kOutput, calls=%fused_computation.59 | convolution fusion | flops 1610612736 | bytes 6815744 | tf_op jit(solution)/shard_map/dot_general | solution.py:142
  25.2 2.6 %collective-permute-start.9 = (f32[128,256]{1,0:T(8,128)S(1)}, f32[128,256]{1,0:T(8,128)S(1)}, u32[]{:S(2)}, u32[]{:S(2)}) collective-permute-start(f32[128,256]{1,0:T(8,128)S(1)} %get-tuple-element.125), channel_id=1, source_target_pairs={{0,24},{8,16},{16,8},{24,0},{1,25},{9,17},{17,9},{25,1},{2,26},{10... | collective-permute-start | bytes 393224 | tf_op jit(solution)/shard_map/ppermute | solution.py:388
  28.6 4.6 %collective-permute-done.9 = f32[128,256]{1,0:T(8,128)S(1)} collective-permute-done((f32[128,256]{1,0:T(8,128)S(1)}, f32[128,256]{1,0:T(8,128)S(1)}, u32[]{:S(2)}, u32[]{:S(2)}) %collective-permute-start.9) | collective-permute-done | bytes 131104 | tf_op jit(solution)/shard_map/ppermute | solution.py:388
  34.4 16.0 %all_to_all.25 = f32[8,16,256]{2,1,0:T(8,128)S(1)} all-to-all(f32[8,16,256]{2,1,0:T(8,128)S(1)} %bitcast.66), channel_id=1, replica_groups=mesh['y'=4,'core'=2,'tensor'=4,'replica'=8] {'replica'}, dimensions={0} | all-to-all | bytes 262144 | tf_op jit(solution)/shard_map/all_to_all | solution.py:108
  50.5 10.4 %all_to_all.26 = f32[8,16,256]{2,1,0:T(8,128)S(1)} all-to-all(f32[8,16,256]{2,1,0:T(8,128)S(1)} %broadcast_in_dim.10), channel_id=1, replica_groups=mesh['y'=4,'core'=2,'tensor'=4,'replica'=8] {'replica'}, dimensions={0} | all-to-all | bytes 262144 | tf_op jit(solution)/shard_map/all_to_all | solution.py:95
  60.9 2.2 %collective-permute-start.12 = (f32[128,256]{1,0:T(8,128)S(1)}, f32[128,256]{1,0:T(8,128)S(1)}, u32[]{:S(2)}, u32[]{:S(2)}) collective-permute-start(f32[128,256]{1,0:T(8,128)S(1)} %bitcast.62), channel_id=1, source_target_pairs={{0,24},{8,16},{16,8},{24,0},{1,25},{9,17},{17,9},{25,1},{2,26},{10... | collective-permute-start | bytes 393224 | tf_op jit(solution)/shard_map/ppermute | solution.py:388
  64.2 2.2 %copy-done.1 = f32[512,2048]{1,0:T(8,128)S(1)} copy-done((f32[512,2048]{1,0:T(8,128)S(1)}, f32[512,2048]{1,0:T(8,128)}, u32[]{:S(2)}) %copy-start.1) | copy-done | bytes 4194328
  66.8 1.7 collective-permute-done.11
  68.5 2.5 %shard_map.60 = (f32[4,256,256]{2,1,0:T(8,128)S(1)}, f32[4,256,256]{2,1,0:T(8,128)S(1)}) custom-call(s32[2]{0:T(128)S(1)} %pad_add_fusion.1.place_ref, f32[512,256]{1,0:T(8,128)S(1)} %pad_maximum_fusion.1.left_ref.a_ref, f32[512,2048]{1,0:T(8,128)S(1)} %shard_map.59.buffer_ref), custom_call_target="tpu_custom_call" | custom-call | flops 1610612736 | bytes 8388608 | tf_op jit(solution)/shard_map/pallas_call | solution.py:253
  71.1 5.6 %collective-permute-start.13 = (f32[4,256,256]{2,1,0:T(8,128)S(1)}, f32[4,256,256]{2,1,0:T(8,128)}, u32[]{:S(2)}, u32[]{:S(2)}) collective-permute-start(f32[4,256,256]{2,1,0:T(8,128)S(1)} %get-tuple-element.68), channel_id=1, source_target_pairs={{0,32},{32,0},{1,33},{33,1},{2,34},{34,2},{3,35},{35,3},{4,36},{36... | collective-permute-start | bytes 3145736 | tf_op jit(solution)/shard_map/ppermute | solution.py:120
  76.7 1.0 fusion.4
  77.7 1.4 collective-permute-done.13
  79.5 1.2 add_bitcast_fusion
  80.8 2.7 %collective-permute-start.16 = (f32[256,256]{1,0:T(8,128)S(1)}, f32[256,256]{1,0:T(8,128)S(1)}, u32[]{:S(2)}, u32[]{:S(2)}) collective-permute-start(f32[256,256]{1,0:T(8,128)S(1)} %get-tuple-element.107), channel_id=1, source_target_pairs={{0,192},{64,128},{128,64},{192,0},{1,193},{65,129},{129,65},{193,1... | collective-permute-start | bytes 786440 | tf_op jit(solution)/shard_map/ppermute | solution.py:388
  84.1 11.3 %collective-permute-done.16 = f32[256,256]{1,0:T(8,128)S(1)} collective-permute-done((f32[256,256]{1,0:T(8,128)S(1)}, f32[256,256]{1,0:T(8,128)S(1)}, u32[]{:S(2)}, u32[]{:S(2)}) %collective-permute-start.16) | collective-permute-done | bytes 262176 | tf_op jit(solution)/shard_map/ppermute | solution.py:388
  95.9 1.8 %fusion = f32[256,256]{1,0:T(8,128)} fusion(f32[256,256]{1,0:T(8,128)} %collective-permute-done.14, f32[256,256]{1,0:T(8,128)S(1)} %collective-permute-done.15, f32[256,256]{1,0:T(8,128)S(1)} %collective-permute-done.16, f32[4,256,256]{2,1,0:T(8,128)S(1)} %get-tuple-element.70, f32[4,256,256]{2,1,0:T(8,128)} %collective-permute-done.13), kind=kLoop, calls=%fused_computation.6 | loop fusion | flops 262144 | bytes 1572864 | tf_op jit(solution)/shard_map/add | solution.py:466
  97.7 3.4 %all-to-all-start.2 = ((f32[8,32,256]{2,1,0:T(8,128)}), f32[8,32,256]{2,1,0:T(8,128)S(1)}, u32[]{:S(2)}, u32[]{:S(2)}) async-start(f32[8,32,256]{2,1,0:T(8,128)} %bitcast.27), calls=%async_computation.2 | async-start | bytes 524288 | tf_op jit(solution)/shard_map/all_to_all | solution.py:108
  101.1 2.7 %collective-permute-start.20 = (f32[128,256]{1,0:T(8,128)S(1)}, f32[128,256]{1,0:T(8,128)S(1)}, u32[]{:S(2)}, u32[]{:S(2)}) collective-permute-start(f32[128,256]{1,0:T(8,128)S(1)} %dynamic-slice_add_fusion), channel_id=1, source_target_pairs={{0,192},{64,128},{128,64},{192,0},{1,193},{65,129},{129,65},{193,1... | collective-permute-start | bytes 393224 | tf_op jit(solution)/shard_map/ppermute | solution.py:388
  104.4 4.3 %collective-permute-done.20 = f32[128,256]{1,0:T(8,128)S(1)} collective-permute-done((f32[128,256]{1,0:T(8,128)S(1)}, f32[128,256]{1,0:T(8,128)S(1)}, u32[]{:S(2)}, u32[]{:S(2)}) %collective-permute-start.20) | collective-permute-done | bytes 131104 | tf_op jit(solution)/shard_map/ppermute | solution.py:388
  109.4 1.7 all-to-all-done.2
  111.9 2.7 %collective-permute-start.21 = (f32[128,256]{1,0:T(8,128)S(1)}, f32[128,256]{1,0:T(8,128)S(1)}, u32[]{:S(2)}, u32[]{:S(2)}) collective-permute-start(f32[128,256]{1,0:T(8,128)S(1)} %add_add_fusion), channel_id=1, source_target_pairs={{0,32},{32,0},{1,33},{33,1},{2,34},{34,2},{3,35},{35,3},{4,36},{36... | collective-permute-start | bytes 393224 | tf_op jit(solution)/shard_map/ppermute | solution.py:120
  114.6 5.3 %all-to-all-start.3 = ((f32[8,32,256]{2,1,0:T(8,128)}), f32[8,32,256]{2,1,0:T(8,128)S(1)}, u32[]{:S(2)}, u32[]{:S(2)}) async-start(f32[8,32,256]{2,1,0:T(8,128)} %broadcast_in_dim.11), calls=%async_computation.3 | async-start | bytes 524288 | tf_op jit(solution)/shard_map/all_to_all | solution.py:475
  120.0 3.8 %shard_map.61 = (f32[256,256]{1,0:T(8,128)S(1)}, f32[256,256]{1,0:T(8,128)S(1)}) custom-call(f32[256,256]{1,0:T(8,128)S(1)} %pad_maximum_fusion.2.gram_ref, f32[256,256]{1,0:T(8,128)S(1)} %fusion.1.inv_ref), custom_call_target="tpu_custom_call" | custom-call | bytes 10000 | tf_op jit(solution)/shard_map/pallas_call | solution.py:86
  123.8 8.5 %all-to-all-done.3 = f32[8,32,256]{2,1,0:T(8,128)S(1)} async-done(((f32[8,32,256]{2,1,0:T(8,128)}), f32[8,32,256]{2,1,0:T(8,128)S(1)}, u32[]{:S(2)}, u32[]{:S(2)}) %all-to-all-start.3) | async-done | bytes 262176 | tf_op jit(solution)/shard_map/all_to_all | solution.py:475
  132.3 1.1 broadcast_in_dim.26
  133.3 3.7 %all-to-all-start.4 = ((f32[4,256,256]{2,1,0:T(8,128)}), f32[4,256,256]{2,1,0:T(8,128)S(1)}, u32[]{:S(2)}, u32[]{:S(2)}) async-start(f32[4,256,256]{2,1,0:T(8,128)} %broadcast_in_dim.26), calls=%async_computation.4 | async-start | bytes 2097152 | tf_op jit(solution)/shard_map/all_to_all | solution.py:480
  137.1 10.7 %shard_map.62 = (f32[256,256]{1,0:T(8,128)}, f32[256,256]{1,0:T(8,128)S(1)}) custom-call(f32[256,256]{1,0:T(8,128)S(1)} %get-tuple-element.82.gram_ref, f32[256,256]{1,0:T(8,128)S(1)} %get-tuple-element.83.inv_ref), custom_call_target="tpu_custom_call" | custom-call | bytes 30000 | tf_op jit(solution)/shard_map/pallas_call | solution.py:86
  148.4 3.1 %all-to-all-done.4.raw_ref = f32[4,256,256]{2,1,0:T(8,128)S(1)} async-done(((f32[4,256,256]{2,1,0:T(8,128)}), f32[4,256,256]{2,1,0:T(8,128)S(1)}, u32[]{:S(2)}, u32[]{:S(2)}) %all-to-all-start.4) | async-done | bytes 1048608 | tf_op jit(solution)/shard_map/all_to_all | solution.py:480
  151.6 1.1 shard_map.64
  152.6 1.3 collective-permute-start.25
  154.0 1.7 collective-permute-start.24
  156.2 1.0 collective-permute-start.22
  157.2 2.2 %copy-done.2 = f32[512,2048]{1,0:T(8,128)S(1)} copy-done((f32[512,2048]{1,0:T(8,128)S(1)}, f32[512,2048]{1,0:T(8,128)}, u32[]{:S(2)}) %copy-start.2) | copy-done | bytes 4194328
  159.4 2.1 %shard_map.65.filled_ref = f32[512,2048]{1,0:T(8,128)} custom-call(s32[1]{0:T(128)} %bitcast.half_ref, f32[512,256]{1,0:T(8,128)S(1)} %shard_map.63.ortho_ref, f32[4,256,256]{2,1,0:T(8,128)S(1)} %get-tuple-element.89.right_ref.mine_ref, f32[512,2048]{1,0:T(8,128)S(1)} %copy-done.2), custom_call_target="tpu_custom_call" | custom-call | flops 805306368 | bytes 4194304 | tf_op jit(solution)/shard_map/pallas_call | solution.py:315
  161.6 1.0 collective-permute-start.26
  162.7 0.8 collective-permute-done.26
  163.4 5.2 %shard_map.66 = (f32[512,2048]{1,0:T(8,128)}, bf16[512,2048]{1,0:T(8,128)(2,1)}, f32[32,2048]{1,0:T(8,128)}) custom-call(s32[2]{0:T(128)S(1)} %pad_add_fusion.place_ref, f32[512,256]{1,0:T(8,128)S(1)} %shard_map.63.ortho_ref, f32[4,256,256]{2,1,0:T(8,128)S(1)} %get-tuple-element.89.right_ref.mine_ref, ...), custom_call_target="tpu_custom_call", output_to_operand_aliasing={{0}: (6, {})} | custom-call | flops 2415919104 | bytes 8388608 | tf_op jit(solution)/shard_map/pallas_call | solution.py:358
  (70 shorter events, 10.1 us)
Async XLA Ops:
  0.6 17.0 %collective-permute-start.1 = (f32[32,2048]{1,0:T(8,128)}, f32[32,2048]{1,0:T(8,128)S(1)}, u32[]{:S(2)}, u32[]{:S(2)}) collective-permute-start(f32[32,2048]{1,0:T(8,128)} %bitcast.67), channel_id=1, source_target_pairs={{0,192},{64,128},{128,64},{192,0},{1,193},{65,129},{129,65},{193,1... | collective-permute-start | bytes 786440 | tf_op jit(solution)/shard_map/ppermute | solution.py:388
  4.3 13.4 %collective-permute-start = (f32[32,2048]{1,0:T(8,128)}, f32[32,2048]{1,0:T(8,128)S(1)}, u32[]{:S(2)}, u32[]{:S(2)}) collective-permute-start(f32[32,2048]{1,0:T(8,128)} %bitcast.68), channel_id=1, source_target_pairs={{0,64},{64,0},{128,192},{192,128},{1,65},{65,1},{129,193},{193,129... | collective-permute-start | bytes 786440 | tf_op jit(solution)/shard_map/ppermute | solution.py:388
  4.3 13.4 %collective-permute-start.3 = (f32[32,2048]{1,0:T(8,128)}, f32[32,2048]{1,0:T(8,128)S(1)}, u32[]{:S(2)}, u32[]{:S(2)}) collective-permute-start(f32[32,2048]{1,0:T(8,128)} %bitcast.69), channel_id=1, source_target_pairs={{0,128},{64,192},{128,0},{192,64},{1,129},{65,193},{129,1},{193,65... | collective-permute-start | bytes 786440 | tf_op jit(solution)/shard_map/ppermute | solution.py:388
  5.6 13.1 %collective-permute-start.6 = (f32[32,2048]{1,0:T(8,128)}, f32[32,2048]{1,0:T(8,128)S(1)}, u32[]{:S(2)}, u32[]{:S(2)}) collective-permute-start(f32[32,2048]{1,0:T(8,128)} %bitcast.70), channel_id=1, source_target_pairs={{0,32},{32,0},{1,33},{33,1},{2,34},{34,2},{3,35},{35,3},{4,36},{36... | collective-permute-start | bytes 786440 | tf_op jit(solution)/shard_map/ppermute | solution.py:120
  8.7 2.2 %copy-start.3 = (f32[1,512,2048]{2,1,0:T(8,128)S(1)}, f32[1,512,2048]{2,1,0:T(8,128)}, u32[]{:S(2)}) copy-start(f32[1,512,2048]{2,1,0:T(8,128)} %momentum_ref) | copy-start | bytes 12582916
  10.8 1.6 copy-start.6
  12.4 7.7 %copy-start.7 = (f32[2048,32]{0,1:T(8,128)S(1)}, f32[2048,32]{0,1:T(8,128)}, u32[]{:S(2)}) copy-start(f32[2048,32]{0,1:T(8,128)} %param.5) | copy-start | bytes 786436
  13.7 2.0 %copy-start = (f32[512,2048]{1,0:T(8,128)}, f32[512,2048]{1,0:T(8,128)S(1)}, u32[]{:S(2)}) copy-start(f32[512,2048]{1,0:T(8,128)S(1)} %get-tuple-element.59.far_ref.buffer_ref) | copy-start | bytes 12582916
  15.6 2.0 %copy-start.4 = (f32[512,2048]{1,0:T(8,128)}, f32[512,2048]{1,0:T(8,128)S(1)}, u32[]{:S(2)}) copy-start(f32[512,2048]{1,0:T(8,128)S(1)} %get-tuple-element.54) | copy-start | bytes 12582916
  17.7 2.2 %collective-permute-start.2 = (f32[32,2048]{1,0:T(8,128)S(1)}, f32[32,2048]{1,0:T(8,128)S(1)}, u32[]{:S(2)}, u32[]{:S(2)}) collective-permute-start(f32[32,2048]{1,0:T(8,128)S(1)} %collective-permute-done.1), channel_id=1, source_target_pairs={{0,32},{32,0},{1,33},{33,1},{2,34},{34,2},{3,35},{35,3},{4,36},{36... | collective-permute-start | bytes 786440 | tf_op jit(solution)/shard_map/ppermute | solution.py:120
  17.7 2.1 %collective-permute-start.4 = (f32[32,2048]{1,0:T(8,128)S(1)}, f32[32,2048]{1,0:T(8,128)S(1)}, u32[]{:S(2)}, u32[]{:S(2)}) collective-permute-start(f32[32,2048]{1,0:T(8,128)S(1)} %collective-permute-done.3), channel_id=1, source_target_pairs={{0,32},{32,0},{1,33},{33,1},{2,34},{34,2},{3,35},{35,3},{4,36},{36... | collective-permute-start | bytes 786440 | tf_op jit(solution)/shard_map/ppermute | solution.py:120
  18.6 1.5 collective-permute-start.5
  21.1 2.2 %copy-start.5 = (f32[512,2048]{1,0:T(8,128)S(1)}, f32[512,2048]{1,0:T(8,128)}, u32[]{:S(2)}) copy-start(f32[512,2048]{1,0:T(8,128)} %copy-done.4) | copy-start | bytes 12582916
  25.2 8.0 %collective-permute-start.9 = (f32[128,256]{1,0:T(8,128)S(1)}, f32[128,256]{1,0:T(8,128)S(1)}, u32[]{:S(2)}, u32[]{:S(2)}) collective-permute-start(f32[128,256]{1,0:T(8,128)S(1)} %get-tuple-element.125), channel_id=1, source_target_pairs={{0,24},{8,16},{16,8},{24,0},{1,25},{9,17},{17,9},{25,1},{2,26},{10... | collective-permute-start | bytes 393224 | tf_op jit(solution)/shard_map/ppermute | solution.py:388
  27.8 5.9 %collective-permute-start.8 = (f32[128,256]{1,0:T(8,128)S(1)}, f32[128,256]{1,0:T(8,128)S(1)}, u32[]{:S(2)}, u32[]{:S(2)}) collective-permute-start(f32[128,256]{1,0:T(8,128)S(1)} %get-tuple-element.126), channel_id=1, source_target_pairs={{0,16},{8,24},{16,0},{24,8},{1,17},{9,25},{17,1},{25,9},{2,18},{10... | collective-permute-start | bytes 393224 | tf_op jit(solution)/shard_map/ppermute | solution.py:388
  28.3 6.1 %collective-permute-start.7 = (f32[128,256]{1,0:T(8,128)S(1)}, f32[128,256]{1,0:T(8,128)S(1)}, u32[]{:S(2)}, u32[]{:S(2)}) collective-permute-start(f32[128,256]{1,0:T(8,128)S(1)} %get-tuple-element.127), channel_id=1, source_target_pairs={{0,8},{8,0},{16,24},{24,16},{1,9},{9,1},{17,25},{25,17},{2,10},{10... | collective-permute-start | bytes 393224 | tf_op jit(solution)/shard_map/ppermute | solution.py:388
  60.9 5.9 %collective-permute-start.12 = (f32[128,256]{1,0:T(8,128)S(1)}, f32[128,256]{1,0:T(8,128)S(1)}, u32[]{:S(2)}, u32[]{:S(2)}) collective-permute-start(f32[128,256]{1,0:T(8,128)S(1)} %bitcast.62), channel_id=1, source_target_pairs={{0,24},{8,16},{16,8},{24,0},{1,25},{9,17},{17,9},{25,1},{2,26},{10... | collective-permute-start | bytes 393224 | tf_op jit(solution)/shard_map/ppermute | solution.py:388
  63.1 5.3 %collective-permute-start.11 = (f32[128,256]{1,0:T(8,128)S(1)}, f32[128,256]{1,0:T(8,128)S(1)}, u32[]{:S(2)}, u32[]{:S(2)}) collective-permute-start(f32[128,256]{1,0:T(8,128)S(1)} %bitcast.63), channel_id=1, source_target_pairs={{0,16},{8,24},{16,0},{24,8},{1,17},{9,25},{17,1},{25,9},{2,18},{10... | collective-permute-start | bytes 393224 | tf_op jit(solution)/shard_map/ppermute | solution.py:388
  63.7 4.7 %collective-permute-start.10 = (f32[128,256]{1,0:T(8,128)S(1)}, f32[128,256]{1,0:T(8,128)S(1)}, u32[]{:S(2)}, u32[]{:S(2)}) collective-permute-start(f32[128,256]{1,0:T(8,128)S(1)} %bitcast.64), channel_id=1, source_target_pairs={{0,8},{8,0},{16,24},{24,16},{1,9},{9,1},{17,25},{25,17},{2,10},{10... | collective-permute-start | bytes 393224 | tf_op jit(solution)/shard_map/ppermute | solution.py:388
  64.2 2.2 %copy-start.1 = (f32[512,2048]{1,0:T(8,128)S(1)}, f32[512,2048]{1,0:T(8,128)}, u32[]{:S(2)}) copy-start(f32[512,2048]{1,0:T(8,128)} %copy-done) | copy-start | bytes 12582916
  71.1 8.0 %collective-permute-start.13 = (f32[4,256,256]{2,1,0:T(8,128)S(1)}, f32[4,256,256]{2,1,0:T(8,128)}, u32[]{:S(2)}, u32[]{:S(2)}) collective-permute-start(f32[4,256,256]{2,1,0:T(8,128)S(1)} %get-tuple-element.68), channel_id=1, source_target_pairs={{0,32},{32,0},{1,33},{33,1},{2,34},{34,2},{3,35},{35,3},{4,36},{36... | collective-permute-start | bytes 3145736 | tf_op jit(solution)/shard_map/ppermute | solution.py:120
  79.1 5.0 %collective-permute-start.17 = (f32[128,256]{1,0:T(8,128)S(1)}, f32[128,256]{1,0:T(8,128)S(1)}, u32[]{:S(2)}, u32[]{:S(2)}) collective-permute-start(f32[128,256]{1,0:T(8,128)S(1)} %constant_dynamic-slice_fusion), channel_id=1, source_target_pairs={{0,32},{32,0},{1,33},{33,1},{2,34},{34,2},{3,35},{35,3},{4,36},{36... | collective-permute-start | bytes 393224 | tf_op jit(solution)/shard_map/ppermute | solution.py:120
  80.8 14.7 %collective-permute-start.16 = (f32[256,256]{1,0:T(8,128)S(1)}, f32[256,256]{1,0:T(8,128)S(1)}, u32[]{:S(2)}, u32[]{:S(2)}) collective-permute-start(f32[256,256]{1,0:T(8,128)S(1)} %get-tuple-element.107), channel_id=1, source_target_pairs={{0,192},{64,128},{128,64},{192,0},{1,193},{65,129},{129,65},{193,1... | collective-permute-start | bytes 786440 | tf_op jit(solution)/shard_map/ppermute | solution.py:388
  83.4 12.0 %collective-permute-start.15 = (f32[256,256]{1,0:T(8,128)S(1)}, f32[256,256]{1,0:T(8,128)S(1)}, u32[]{:S(2)}, u32[]{:S(2)}) collective-permute-start(f32[256,256]{1,0:T(8,128)S(1)} %get-tuple-element.108), channel_id=1, source_target_pairs={{0,128},{64,192},{128,0},{192,64},{1,129},{65,193},{129,1},{193,65... | collective-permute-start | bytes 786440 | tf_op jit(solution)/shard_map/ppermute | solution.py:388
  83.4 12.4 %collective-permute-start.14 = (f32[256,256]{1,0:T(8,128)S(1)}, f32[256,256]{1,0:T(8,128)}, u32[]{:S(2)}, u32[]{:S(2)}) collective-permute-start(f32[256,256]{1,0:T(8,128)S(1)} %get-tuple-element.109), channel_id=1, source_target_pairs={{0,64},{64,0},{128,192},{192,128},{1,65},{65,1},{129,193},{193,129... | collective-permute-start | bytes 786440 | tf_op jit(solution)/shard_map/ppermute | solution.py:388
  97.7 13.5 %all-to-all-start.2 = ((f32[8,32,256]{2,1,0:T(8,128)}), f32[8,32,256]{2,1,0:T(8,128)S(1)}, u32[]{:S(2)}, u32[]{:S(2)}) async-start(f32[8,32,256]{2,1,0:T(8,128)} %bitcast.27), calls=%async_computation.2 | async-start | bytes 524288 | tf_op jit(solution)/shard_map/all_to_all | solution.py:108
  101.1 7.6 %collective-permute-start.20 = (f32[128,256]{1,0:T(8,128)S(1)}, f32[128,256]{1,0:T(8,128)S(1)}, u32[]{:S(2)}, u32[]{:S(2)}) collective-permute-start(f32[128,256]{1,0:T(8,128)S(1)} %dynamic-slice_add_fusion), channel_id=1, source_target_pairs={{0,192},{64,128},{128,64},{192,0},{1,193},{65,129},{129,65},{193,1... | collective-permute-start | bytes 393224 | tf_op jit(solution)/shard_map/ppermute | solution.py:388
  103.7 5.7 %collective-permute-start.19 = (f32[128,256]{1,0:T(8,128)S(1)}, f32[128,256]{1,0:T(8,128)S(1)}, u32[]{:S(2)}, u32[]{:S(2)}) collective-permute-start(f32[128,256]{1,0:T(8,128)S(1)} %dynamic-slice_add_fusion), channel_id=1, source_target_pairs={{0,128},{64,192},{128,0},{192,64},{1,129},{65,193},{129,1},{193,65... | collective-permute-start | bytes 393224 | tf_op jit(solution)/shard_map/ppermute | solution.py:388
  104.1 5.3 %collective-permute-start.18 = (f32[128,256]{1,0:T(8,128)S(1)}, f32[128,256]{1,0:T(8,128)S(1)}, u32[]{:S(2)}, u32[]{:S(2)}) collective-permute-start(f32[128,256]{1,0:T(8,128)S(1)} %dynamic-slice_add_fusion), channel_id=1, source_target_pairs={{0,64},{64,0},{128,192},{192,128},{1,65},{65,1},{129,193},{193,129... | collective-permute-start | bytes 393224 | tf_op jit(solution)/shard_map/ppermute | solution.py:388
  111.9 8.0 %collective-permute-start.21 = (f32[128,256]{1,0:T(8,128)S(1)}, f32[128,256]{1,0:T(8,128)S(1)}, u32[]{:S(2)}, u32[]{:S(2)}) collective-permute-start(f32[128,256]{1,0:T(8,128)S(1)} %add_add_fusion), channel_id=1, source_target_pairs={{0,32},{32,0},{1,33},{33,1},{2,34},{34,2},{3,35},{35,3},{4,36},{36... | collective-permute-start | bytes 393224 | tf_op jit(solution)/shard_map/ppermute | solution.py:120
  114.6 17.7 %all-to-all-start.3 = ((f32[8,32,256]{2,1,0:T(8,128)}), f32[8,32,256]{2,1,0:T(8,128)S(1)}, u32[]{:S(2)}, u32[]{:S(2)}) async-start(f32[8,32,256]{2,1,0:T(8,128)} %broadcast_in_dim.11), calls=%async_computation.3 | async-start | bytes 524288 | tf_op jit(solution)/shard_map/all_to_all | solution.py:475
  133.3 18.2 %all-to-all-start.4 = ((f32[4,256,256]{2,1,0:T(8,128)}), f32[4,256,256]{2,1,0:T(8,128)S(1)}, u32[]{:S(2)}, u32[]{:S(2)}) async-start(f32[4,256,256]{2,1,0:T(8,128)} %broadcast_in_dim.26), calls=%async_computation.4 | async-start | bytes 2097152 | tf_op jit(solution)/shard_map/all_to_all | solution.py:480
  152.6 9.0 %collective-permute-start.25 = (f32[4,256,256]{2,1,0:T(8,128)S(1)}, f32[4,256,256]{2,1,0:T(8,128)S(1)}, u32[]{:S(2)}, u32[]{:S(2)}) collective-permute-start(f32[4,256,256]{2,1,0:T(8,128)S(1)} %get-tuple-element.89.right_ref.mine_ref), channel_id=1, source_target_pairs={{0,32},{32,0},{1,33},{33,1},{2,34},{34,2},{3,35},{35,3},{4,36},{36... | collective-permute-start | bytes 3145736 | tf_op jit(solution)/shard_map/ppermute | solution.py:120
  154.0 7.6 %collective-permute-start.24 = (f32[8,256]{1,0:T(8,128)S(1)}, f32[8,256]{1,0:T(8,128)S(1)}, u32[]{:S(2)}, u32[]{:S(2)}) collective-permute-start(f32[8,256]{1,0:T(8,128)S(1)} %get-tuple-element.90), channel_id=1, source_target_pairs={{0,24},{8,16},{16,8},{24,0},{1,25},{9,17},{17,9},{25,1},{2,26},{10... | collective-permute-start | bytes 24584 | tf_op jit(solution)/shard_map/ppermute | solution.py:388
  155.7 5.9 %collective-permute-start.23 = (f32[8,256]{1,0:T(8,128)S(1)}, f32[8,256]{1,0:T(8,128)S(1)}, u32[]{:S(2)}, u32[]{:S(2)}) collective-permute-start(f32[8,256]{1,0:T(8,128)S(1)} %get-tuple-element.90), channel_id=1, source_target_pairs={{0,16},{8,24},{16,0},{24,8},{1,17},{9,25},{17,1},{25,9},{2,18},{10... | collective-permute-start | bytes 24584 | tf_op jit(solution)/shard_map/ppermute | solution.py:388
  156.2 5.4 %collective-permute-start.22 = (f32[8,256]{1,0:T(8,128)S(1)}, f32[8,256]{1,0:T(8,128)S(1)}, u32[]{:S(2)}, u32[]{:S(2)}) collective-permute-start(f32[8,256]{1,0:T(8,128)S(1)} %get-tuple-element.90), channel_id=1, source_target_pairs={{0,8},{8,0},{16,24},{24,16},{1,9},{9,1},{17,25},{25,17},{2,10},{10... | collective-permute-start | bytes 24584 | tf_op jit(solution)/shard_map/ppermute | solution.py:388
  157.2 2.2 %copy-start.2 = (f32[512,2048]{1,0:T(8,128)S(1)}, f32[512,2048]{1,0:T(8,128)}, u32[]{:S(2)}) copy-start(f32[512,2048]{1,0:T(8,128)} %copy-done) | copy-start | bytes 12582916
  161.6 1.8 %collective-permute-start.26 = (f32[8,256]{1,0:T(8,128)S(1)}, f32[8,256]{1,0:T(8,128)S(1)}, u32[]{:S(2)}, u32[]{:S(2)}) collective-permute-start(f32[8,256]{1,0:T(8,128)S(1)} %add_add_fusion.1), channel_id=1, source_target_pairs={{0,32},{32,0},{1,33},{33,1},{2,34},{34,2},{3,35},{35,3},{4,36},{36... | collective-permute-start | bytes 24584 | tf_op jit(solution)/shard_map/ppermute | solution.py:120

commit v5 on v4

--- a/solution.py
+++ b/solution.py
@@ -14,7 +14,6 @@
 
 def inverted(value):
     near = pl.reciprocal(value, approx=True)
-    near = near * (2.0 - value * near)
     return near * (2.0 - value * near)
 
 
@@ -291,7 +290,8 @@
 
 
 def change_block(ortho, right, buffer_ref, index, slot_ref, out_ref, sem):
-    slot_ref[...] = block_of(buffer_ref, index)[...] + three_dots(ortho, right)
+    change = jnp.dot(ortho, right.astype(jnp.bfloat16), preferred_element_type=jnp.float32)
+    slot_ref[...] = block_of(buffer_ref, index)[...] + change
     copy = pltpu.make_async_copy(slot_ref, block_of(out_ref, index), sem)
     copy.start()
     return copy
@@ -299,11 +299,11 @@
 
 def first_kernel(half_ref, ortho_ref, right_ref, buffer_ref, out_ref, slots, sems):
     count = right_ref.shape[0]
-    ortho = split(ortho_ref[...] * -0.05)
+    ortho = (ortho_ref[...] * -0.05).astype(jnp.bfloat16)
     copies = []
     for i in range(count):
         index = half_ref[0] * count + i
-        right = split(right_ref[i])
+        right = right_ref[i]
         copies.append(change_block(ortho, right, buffer_ref, index, slots.at[i], out_ref, sems.at[i]))
     for copy in copies:
         copy.wait()
@@ -332,12 +332,12 @@
     norms = jnp.sqrt(squares_ref[...] + 1e-12)
     column_ref[...] = jnp.concatenate([norms] * 16, axis=0).T
     own_norms = column_ref[pl.ds(offset, 32), :][:, :1]
-    ortho = split(ortho_ref[...] * -0.05)
+    ortho = (ortho_ref[...] * -0.05).astype(jnp.bfloat16)
     scaled = split(ortho_ref[...] * ((M_ROWS * NCOLS / RANK) ** 0.5 / norms[:1]))
     copies = []
     for i in range(count):
         index = (1 - core) * count + i
-        right = split(other_ref[i])
+        right = other_ref[i]
         copies.append(change_block(ortho, right, buffer_ref, index, slots.at[i], out_ref, sems.at[i]))
     for half, (source, start) in enumerate(((other_ref, (1 - core) * count), (mine_ref, core * count))):
         for i in range(count):

time: 169 us -> 168 us (level)
  Pallas kernels: 27.5 us -> 25.3 us
  transfers between devices with their start and end apart: 30 -> 30, of which waited for: 15 -> 15; matrix products, arithmetic and copies ran while one was open for 1% -> 1% of each run, Pallas kernels for 11% -> 10%
where the time goes in v5:
time: 168 us
  starting transfers between devices  49.1 us (29%)
  waiting for transfers between devices  42.4 us (25%)
  blocking collectives  26.4 us (16%)
  Pallas kernels  25.3 us (15%)
  local copies, waits for them, and re-layouts  16.1 us (10%)
  other arithmetic  4.28 us (3%)
  matrix products  2.94 us (2%)
    ppermute x18, waiting for transfers between devices, turned(): return lax.ppermute(value, axis, [(i, i ^ mask) for i in range(4)])  24.2 us
    ppermute x18, starting transfers between devices, turned(): return lax.ppermute(value, axis, [(i, i ^ mask) for i in range(4)])  21.5 us
    all_to_all x1, blocking collectives, parted(): return lax.all_to_all(blocks, axis, 0, 0, tiled=True)  16 us
    ppermute x9, starting transfers between devices, swapped(): return lax.ppermute(value, 'core', [(0, 1), (1, 0)])  15.2 us
    unnamed x16, local copies, waits for them, and re-layouts  14.2 us
    pallas_call x2, Pallas kernels, factor_part(): pl.pallas_call(functools.partial(factor_kernel, first, last), out_shape=(...  13.3 us
    all_to_all x1, blocking collectives, to_everyone(): lax.all_to_all(jnp.broadcast_to(value[None], (size, *value.shape)), axis,...  10.4 us
    all_to_all x1, waiting for transfers between devices, local(): pieces = lax.all_to_all(wide, 'replica', 0, 0, tiled=True)  8.82 us
  transfers between devices with their start and end apart: 30, of which 15 were waited for; matrix products, arithmetic and copies ran while one was open for 1% of the time, Pallas kernels for 10%

profile of v5, /device:TPU:1, one launch (start us, length us, event | category | flops | bytes accessed | tf_op | source)
XLA Modules:
  0.0 167.8 jit_solution(13702830941774471647)
XLA Ops:
  0.6 3.7 %collective-permute-start.1 = (f32[32,2048]{1,0:T(8,128)}, f32[32,2048]{1,0:T(8,128)S(1)}, u32[]{:S(2)}, u32[]{:S(2)}) collective-permute-start(f32[32,2048]{1,0:T(8,128)} %bitcast.67), channel_id=1, source_target_pairs={{0,192},{64,128},{128,64},{192,0},{1,193},{65,129},{129,65},{193,1... | collective-permute-start | bytes 786440 | tf_op jit(solution)/shard_map/ppermute | solution.py:388
  4.3 1.3 collective-permute-start.3
  5.6 3.1 %collective-permute-start.6 = (f32[32,2048]{1,0:T(8,128)}, f32[32,2048]{1,0:T(8,128)S(1)}, u32[]{:S(2)}, u32[]{:S(2)}) collective-permute-start(f32[32,2048]{1,0:T(8,128)} %bitcast.70), channel_id=1, source_target_pairs={{0,32},{32,0},{1,33},{33,1},{2,34},{34,2},{3,35},{35,3},{4,36},{36... | collective-permute-start | bytes 786440 | tf_op jit(solution)/shard_map/ppermute | solution.py:119
  8.7 2.2 %copy-done.3 = f32[1,512,2048]{2,1,0:T(8,128)S(1)} copy-done((f32[1,512,2048]{2,1,0:T(8,128)S(1)}, f32[1,512,2048]{2,1,0:T(8,128)}, u32[]{:S(2)}) %copy-start.3) | copy-done | bytes 4194328
  10.8 1.6 copy-done.6
  12.4 1.2 shard_map.58
  13.7 2.0 %copy-done = f32[512,2048]{1,0:T(8,128)} copy-done((f32[512,2048]{1,0:T(8,128)}, f32[512,2048]{1,0:T(8,128)S(1)}, u32[]{:S(2)}) %copy-start) | copy-done | bytes 4194328
  15.6 2.0 %copy-done.4 = f32[512,2048]{1,0:T(8,128)} copy-done((f32[512,2048]{1,0:T(8,128)}, f32[512,2048]{1,0:T(8,128)S(1)}, u32[]{:S(2)}) %copy-start.4) | copy-done | bytes 4194328
  17.7 1.0 collective-permute-start.4
  18.7 1.2 collective-permute-done.4
  21.2 2.0 %copy-done.5 = f32[512,2048]{1,0:T(8,128)S(1)} copy-done((f32[512,2048]{1,0:T(8,128)S(1)}, f32[512,2048]{1,0:T(8,128)}, u32[]{:S(2)}) %copy-start.5) | copy-done | bytes 4194328
  23.2 1.9 %fusion.3 = f32[4,128,256]{2,1,0:T(8,128)S(1)} fusion(f32[4,128,2048]{2,1,0:T(8,128)S(1)} %bitcast.58, f32[256,2048,1]{1,0,2:T(8,128)S(1)} %bitcast.60), kind=kOutput, calls=%fused_computation.59 | convolution fusion | flops 1610612736 | bytes 6815744 | tf_op jit(solution)/shard_map/dot_general | solution.py:141
  25.2 2.6 %collective-permute-start.9 = (f32[128,256]{1,0:T(8,128)S(1)}, f32[128,256]{1,0:T(8,128)S(1)}, u32[]{:S(2)}, u32[]{:S(2)}) collective-permute-start(f32[128,256]{1,0:T(8,128)S(1)} %get-tuple-element.125), channel_id=1, source_target_pairs={{0,24},{8,16},{16,8},{24,0},{1,25},{9,17},{17,9},{25,1},{2,26},{10... | collective-permute-start | bytes 393224 | tf_op jit(solution)/shard_map/ppermute | solution.py:388
  28.6 4.6 %collective-permute-done.9 = f32[128,256]{1,0:T(8,128)S(1)} collective-permute-done((f32[128,256]{1,0:T(8,128)S(1)}, f32[128,256]{1,0:T(8,128)S(1)}, u32[]{:S(2)}, u32[]{:S(2)}) %collective-permute-start.9) | collective-permute-done | bytes 131104 | tf_op jit(solution)/shard_map/ppermute | solution.py:388
  34.4 16.0 %all_to_all.25 = f32[8,16,256]{2,1,0:T(8,128)S(1)} all-to-all(f32[8,16,256]{2,1,0:T(8,128)S(1)} %bitcast.66), channel_id=1, replica_groups=mesh['y'=4,'core'=2,'tensor'=4,'replica'=8] {'replica'}, dimensions={0} | all-to-all | bytes 262144 | tf_op jit(solution)/shard_map/all_to_all | solution.py:107
  50.5 10.4 %all_to_all.26 = f32[8,16,256]{2,1,0:T(8,128)S(1)} all-to-all(f32[8,16,256]{2,1,0:T(8,128)S(1)} %broadcast_in_dim.10), channel_id=1, replica_groups=mesh['y'=4,'core'=2,'tensor'=4,'replica'=8] {'replica'}, dimensions={0} | all-to-all | bytes 262144 | tf_op jit(solution)/shard_map/all_to_all | solution.py:94
  60.9 2.2 %collective-permute-start.12 = (f32[128,256]{1,0:T(8,128)S(1)}, f32[128,256]{1,0:T(8,128)S(1)}, u32[]{:S(2)}, u32[]{:S(2)}) collective-permute-start(f32[128,256]{1,0:T(8,128)S(1)} %bitcast.62), channel_id=1, source_target_pairs={{0,24},{8,16},{16,8},{24,0},{1,25},{9,17},{17,9},{25,1},{2,26},{10... | collective-permute-start | bytes 393224 | tf_op jit(solution)/shard_map/ppermute | solution.py:388
  64.2 2.2 %copy-done.1 = f32[512,2048]{1,0:T(8,128)S(1)} copy-done((f32[512,2048]{1,0:T(8,128)S(1)}, f32[512,2048]{1,0:T(8,128)}, u32[]{:S(2)}) %copy-start.1) | copy-done | bytes 4194328
  66.8 1.7 collective-permute-done.11
  68.5 2.5 %shard_map.60 = (f32[4,256,256]{2,1,0:T(8,128)S(1)}, f32[4,256,256]{2,1,0:T(8,128)S(1)}) custom-call(s32[2]{0:T(128)S(1)} %pad_add_fusion.1.place_ref, f32[512,256]{1,0:T(8,128)S(1)} %pad_maximum_fusion.1.left_ref.a_ref, f32[512,2048]{1,0:T(8,128)S(1)} %shard_map.59.buffer_ref), custom_call_target="tpu_custom_call" | custom-call | flops 1610612736 | bytes 8388608 | tf_op jit(solution)/shard_map/pallas_call | solution.py:252
  71.1 5.6 %collective-permute-start.13 = (f32[4,256,256]{2,1,0:T(8,128)S(1)}, f32[4,256,256]{2,1,0:T(8,128)}, u32[]{:S(2)}, u32[]{:S(2)}) collective-permute-start(f32[4,256,256]{2,1,0:T(8,128)S(1)} %get-tuple-element.68), channel_id=1, source_target_pairs={{0,32},{32,0},{1,33},{33,1},{2,34},{34,2},{3,35},{35,3},{4,36},{36... | collective-permute-start | bytes 3145736 | tf_op jit(solution)/shard_map/ppermute | solution.py:119
  76.7 1.0 fusion.4
  77.7 1.4 collective-permute-done.13
  79.5 1.2 add_bitcast_fusion
  80.8 2.7 %collective-permute-start.16 = (f32[256,256]{1,0:T(8,128)S(1)}, f32[256,256]{1,0:T(8,128)S(1)}, u32[]{:S(2)}, u32[]{:S(2)}) collective-permute-start(f32[256,256]{1,0:T(8,128)S(1)} %get-tuple-element.107), channel_id=1, source_target_pairs={{0,192},{64,128},{128,64},{192,0},{1,193},{65,129},{129,65},{193,1... | collective-permute-start | bytes 786440 | tf_op jit(solution)/shard_map/ppermute | solution.py:388
  84.1 11.3 %collective-permute-done.16 = f32[256,256]{1,0:T(8,128)S(1)} collective-permute-done((f32[256,256]{1,0:T(8,128)S(1)}, f32[256,256]{1,0:T(8,128)S(1)}, u32[]{:S(2)}, u32[]{:S(2)}) %collective-permute-start.16) | collective-permute-done | bytes 262176 | tf_op jit(solution)/shard_map/ppermute | solution.py:388
  95.9 1.8 %fusion = f32[256,256]{1,0:T(8,128)} fusion(f32[256,256]{1,0:T(8,128)} %collective-permute-done.14, f32[256,256]{1,0:T(8,128)S(1)} %collective-permute-done.15, f32[256,256]{1,0:T(8,128)S(1)} %collective-permute-done.16, f32[4,256,256]{2,1,0:T(8,128)S(1)} %get-tuple-element.70, f32[4,256,256]{2,1,0:T(8,128)} %collective-permute-done.13), kind=kLoop, calls=%fused_computation.6 | loop fusion | flops 262144 | bytes 1572864 | tf_op jit(solution)/shard_map/add | solution.py:466
  97.7 3.4 %all-to-all-start.2 = ((f32[8,32,256]{2,1,0:T(8,128)}), f32[8,32,256]{2,1,0:T(8,128)S(1)}, u32[]{:S(2)}, u32[]{:S(2)}) async-start(f32[8,32,256]{2,1,0:T(8,128)} %bitcast.27), calls=%async_computation.2 | async-start | bytes 524288 | tf_op jit(solution)/shard_map/all_to_all | solution.py:107
  101.1 2.7 %collective-permute-start.20 = (f32[128,256]{1,0:T(8,128)S(1)}, f32[128,256]{1,0:T(8,128)S(1)}, u32[]{:S(2)}, u32[]{:S(2)}) collective-permute-start(f32[128,256]{1,0:T(8,128)S(1)} %dynamic-slice_add_fusion), channel_id=1, source_target_pairs={{0,192},{64,128},{128,64},{192,0},{1,193},{65,129},{129,65},{193,1... | collective-permute-start | bytes 393224 | tf_op jit(solution)/shard_map/ppermute | solution.py:388
  104.4 4.3 %collective-permute-done.20 = f32[128,256]{1,0:T(8,128)S(1)} collective-permute-done((f32[128,256]{1,0:T(8,128)S(1)}, f32[128,256]{1,0:T(8,128)S(1)}, u32[]{:S(2)}, u32[]{:S(2)}) %collective-permute-start.20) | collective-permute-done | bytes 131104 | tf_op jit(solution)/shard_map/ppermute | solution.py:388
  109.4 1.7 all-to-all-done.2
  111.9 2.7 %collective-permute-start.21 = (f32[128,256]{1,0:T(8,128)S(1)}, f32[128,256]{1,0:T(8,128)S(1)}, u32[]{:S(2)}, u32[]{:S(2)}) collective-permute-start(f32[128,256]{1,0:T(8,128)S(1)} %add_add_fusion), channel_id=1, source_target_pairs={{0,32},{32,0},{1,33},{33,1},{2,34},{34,2},{3,35},{35,3},{4,36},{36... | collective-permute-start | bytes 393224 | tf_op jit(solution)/shard_map/ppermute | solution.py:119
  114.6 5.3 %all-to-all-start.3 = ((f32[8,32,256]{2,1,0:T(8,128)}), f32[8,32,256]{2,1,0:T(8,128)S(1)}, u32[]{:S(2)}, u32[]{:S(2)}) async-start(f32[8,32,256]{2,1,0:T(8,128)} %broadcast_in_dim.11), calls=%async_computation.3 | async-start | bytes 524288 | tf_op jit(solution)/shard_map/all_to_all | solution.py:475
  120.0 3.4 %shard_map.61 = (f32[256,256]{1,0:T(8,128)S(1)}, f32[256,256]{1,0:T(8,128)S(1)}) custom-call(f32[256,256]{1,0:T(8,128)S(1)} %pad_maximum_fusion.2.gram_ref, f32[256,256]{1,0:T(8,128)S(1)} %fusion.1.inv_ref), custom_call_target="tpu_custom_call" | custom-call | bytes 10000 | tf_op jit(solution)/shard_map/pallas_call | solution.py:85
  123.5 8.8 %all-to-all-done.3 = f32[8,32,256]{2,1,0:T(8,128)S(1)} async-done(((f32[8,32,256]{2,1,0:T(8,128)}), f32[8,32,256]{2,1,0:T(8,128)S(1)}, u32[]{:S(2)}, u32[]{:S(2)}) %all-to-all-start.3) | async-done | bytes 262176 | tf_op jit(solution)/shard_map/all_to_all | solution.py:475
  132.3 1.1 broadcast_in_dim.26
  133.3 3.7 %all-to-all-start.4 = ((f32[4,256,256]{2,1,0:T(8,128)}), f32[4,256,256]{2,1,0:T(8,128)S(1)}, u32[]{:S(2)}, u32[]{:S(2)}) async-start(f32[4,256,256]{2,1,0:T(8,128)} %broadcast_in_dim.26), calls=%async_computation.4 | async-start | bytes 2097152 | tf_op jit(solution)/shard_map/all_to_all | solution.py:480
  137.1 9.9 %shard_map.62 = (f32[256,256]{1,0:T(8,128)}, f32[256,256]{1,0:T(8,128)S(1)}) custom-call(f32[256,256]{1,0:T(8,128)S(1)} %get-tuple-element.82.gram_ref, f32[256,256]{1,0:T(8,128)S(1)} %get-tuple-element.83.inv_ref), custom_call_target="tpu_custom_call" | custom-call | bytes 30000 | tf_op jit(solution)/shard_map/pallas_call | solution.py:85
  147.6 4.0 %all-to-all-done.4.raw_ref = f32[4,256,256]{2,1,0:T(8,128)S(1)} async-done(((f32[4,256,256]{2,1,0:T(8,128)}), f32[4,256,256]{2,1,0:T(8,128)S(1)}, u32[]{:S(2)}, u32[]{:S(2)}) %all-to-all-start.4) | async-done | bytes 1048608 | tf_op jit(solution)/shard_map/all_to_all | solution.py:480
  151.6 1.1 shard_map.64
  152.6 1.3 collective-permute-start.25
  154.0 1.7 %collective-permute-start.24 = (f32[8,256]{1,0:T(8,128)S(1)}, f32[8,256]{1,0:T(8,128)S(1)}, u32[]{:S(2)}, u32[]{:S(2)}) collective-permute-start(f32[8,256]{1,0:T(8,128)S(1)} %get-tuple-element.90), channel_id=1, source_target_pairs={{0,24},{8,16},{16,8},{24,0},{1,25},{9,17},{17,9},{25,1},{2,26},{10... | collective-permute-start | bytes 24584 | tf_op jit(solution)/shard_map/ppermute | solution.py:388
  156.2 1.0 collective-permute-start.22
  157.2 2.2 %copy-done.2 = f32[512,2048]{1,0:T(8,128)S(1)} copy-done((f32[512,2048]{1,0:T(8,128)S(1)}, f32[512,2048]{1,0:T(8,128)}, u32[]{:S(2)}) %copy-start.2) | copy-done | bytes 4194328
  159.4 1.7 %shard_map.65.filled_ref = f32[512,2048]{1,0:T(8,128)} custom-call(s32[1]{0:T(128)} %bitcast.half_ref, f32[512,256]{1,0:T(8,128)S(1)} %shard_map.63.ortho_ref, f32[4,256,256]{2,1,0:T(8,128)S(1)} %get-tuple-element.89.right_ref.mine_ref, f32[512,2048]{1,0:T(8,128)S(1)} %copy-done.2), custom_call_target="tpu_custom_call" | custom-call | flops 805306368 | bytes 4194304 | tf_op jit(solution)/shard_map/pallas_call | solution.py:315
  161.2 1.0 collective-permute-start.26
  162.3 0.8 collective-permute-done.26
  163.0 4.6 %shard_map.66 = (f32[512,2048]{1,0:T(8,128)}, bf16[512,2048]{1,0:T(8,128)(2,1)}, f32[32,2048]{1,0:T(8,128)}) custom-call(s32[2]{0:T(128)S(1)} %pad_add_fusion.place_ref, f32[512,256]{1,0:T(8,128)S(1)} %shard_map.63.ortho_ref, f32[4,256,256]{2,1,0:T(8,128)S(1)} %get-tuple-element.89.right_ref.mine_ref, ...), custom_call_target="tpu_custom_call", output_to_operand_aliasing={{0}: (6, {})} | custom-call | flops 2415919104 | bytes 8388608 | tf_op jit(solution)/shard_map/pallas_call | solution.py:358
  (70 shorter events, 10.1 us)
Async XLA Ops:
  0.6 17.0 %collective-permute-start.1 = (f32[32,2048]{1,0:T(8,128)}, f32[32,2048]{1,0:T(8,128)S(1)}, u32[]{:S(2)}, u32[]{:S(2)}) collective-permute-start(f32[32,2048]{1,0:T(8,128)} %bitcast.67), channel_id=1, source_target_pairs={{0,192},{64,128},{128,64},{192,0},{1,193},{65,129},{129,65},{193,1... | collective-permute-start | bytes 786440 | tf_op jit(solution)/shard_map/ppermute | solution.py:388
  4.3 13.4 %collective-permute-start = (f32[32,2048]{1,0:T(8,128)}, f32[32,2048]{1,0:T(8,128)S(1)}, u32[]{:S(2)}, u32[]{:S(2)}) collective-permute-start(f32[32,2048]{1,0:T(8,128)} %bitcast.68), channel_id=1, source_target_pairs={{0,64},{64,0},{128,192},{192,128},{1,65},{65,1},{129,193},{193,129... | collective-permute-start | bytes 786440 | tf_op jit(solution)/shard_map/ppermute | solution.py:388
  4.3 13.4 %collective-permute-start.3 = (f32[32,2048]{1,0:T(8,128)}, f32[32,2048]{1,0:T(8,128)S(1)}, u32[]{:S(2)}, u32[]{:S(2)}) collective-permute-start(f32[32,2048]{1,0:T(8,128)} %bitcast.69), channel_id=1, source_target_pairs={{0,128},{64,192},{128,0},{192,64},{1,129},{65,193},{129,1},{193,65... | collective-permute-start | bytes 786440 | tf_op jit(solution)/shard_map/ppermute | solution.py:388
  5.6 13.1 %collective-permute-start.6 = (f32[32,2048]{1,0:T(8,128)}, f32[32,2048]{1,0:T(8,128)S(1)}, u32[]{:S(2)}, u32[]{:S(2)}) collective-permute-start(f32[32,2048]{1,0:T(8,128)} %bitcast.70), channel_id=1, source_target_pairs={{0,32},{32,0},{1,33},{33,1},{2,34},{34,2},{3,35},{35,3},{4,36},{36... | collective-permute-start | bytes 786440 | tf_op jit(solution)/shard_map/ppermute | solution.py:119
  8.7 2.2 %copy-start.3 = (f32[1,512,2048]{2,1,0:T(8,128)S(1)}, f32[1,512,2048]{2,1,0:T(8,128)}, u32[]{:S(2)}) copy-start(f32[1,512,2048]{2,1,0:T(8,128)} %momentum_ref) | copy-start | bytes 12582916
  10.8 1.6 copy-start.6
  12.4 7.7 %copy-start.7 = (f32[2048,32]{0,1:T(8,128)S(1)}, f32[2048,32]{0,1:T(8,128)}, u32[]{:S(2)}) copy-start(f32[2048,32]{0,1:T(8,128)} %param.5) | copy-start | bytes 786436
  13.7 2.0 %copy-start = (f32[512,2048]{1,0:T(8,128)}, f32[512,2048]{1,0:T(8,128)S(1)}, u32[]{:S(2)}) copy-start(f32[512,2048]{1,0:T(8,128)S(1)} %get-tuple-element.59.far_ref.buffer_ref) | copy-start | bytes 12582916
  15.6 2.0 %copy-start.4 = (f32[512,2048]{1,0:T(8,128)}, f32[512,2048]{1,0:T(8,128)S(1)}, u32[]{:S(2)}) copy-start(f32[512,2048]{1,0:T(8,128)S(1)} %get-tuple-element.54) | copy-start | bytes 12582916
  17.7 2.2 %collective-permute-start.2 = (f32[32,2048]{1,0:T(8,128)S(1)}, f32[32,2048]{1,0:T(8,128)S(1)}, u32[]{:S(2)}, u32[]{:S(2)}) collective-permute-start(f32[32,2048]{1,0:T(8,128)S(1)} %collective-permute-done.1), channel_id=1, source_target_pairs={{0,32},{32,0},{1,33},{33,1},{2,34},{34,2},{3,35},{35,3},{4,36},{36... | collective-permute-start | bytes 786440 | tf_op jit(solution)/shard_map/ppermute | solution.py:119
  17.7 2.1 %collective-permute-start.4 = (f32[32,2048]{1,0:T(8,128)S(1)}, f32[32,2048]{1,0:T(8,128)S(1)}, u32[]{:S(2)}, u32[]{:S(2)}) collective-permute-start(f32[32,2048]{1,0:T(8,128)S(1)} %collective-permute-done.3), channel_id=1, source_target_pairs={{0,32},{32,0},{1,33},{33,1},{2,34},{34,2},{3,35},{35,3},{4,36},{36... | collective-permute-start | bytes 786440 | tf_op jit(solution)/shard_map/ppermute | solution.py:119
  18.6 1.5 collective-permute-start.5
  21.1 2.2 %copy-start.5 = (f32[512,2048]{1,0:T(8,128)S(1)}, f32[512,2048]{1,0:T(8,128)}, u32[]{:S(2)}) copy-start(f32[512,2048]{1,0:T(8,128)} %copy-done.4) | copy-start | bytes 12582916
  25.2 8.0 %collective-permute-start.9 = (f32[128,256]{1,0:T(8,128)S(1)}, f32[128,256]{1,0:T(8,128)S(1)}, u32[]{:S(2)}, u32[]{:S(2)}) collective-permute-start(f32[128,256]{1,0:T(8,128)S(1)} %get-tuple-element.125), channel_id=1, source_target_pairs={{0,24},{8,16},{16,8},{24,0},{1,25},{9,17},{17,9},{25,1},{2,26},{10... | collective-permute-start | bytes 393224 | tf_op jit(solution)/shard_map/ppermute | solution.py:388
  27.8 5.9 %collective-permute-start.8 = (f32[128,256]{1,0:T(8,128)S(1)}, f32[128,256]{1,0:T(8,128)S(1)}, u32[]{:S(2)}, u32[]{:S(2)}) collective-permute-start(f32[128,256]{1,0:T(8,128)S(1)} %get-tuple-element.126), channel_id=1, source_target_pairs={{0,16},{8,24},{16,0},{24,8},{1,17},{9,25},{17,1},{25,9},{2,18},{10... | collective-permute-start | bytes 393224 | tf_op jit(solution)/shard_map/ppermute | solution.py:388
  28.3 6.1 %collective-permute-start.7 = (f32[128,256]{1,0:T(8,128)S(1)}, f32[128,256]{1,0:T(8,128)S(1)}, u32[]{:S(2)}, u32[]{:S(2)}) collective-permute-start(f32[128,256]{1,0:T(8,128)S(1)} %get-tuple-element.127), channel_id=1, source_target_pairs={{0,8},{8,0},{16,24},{24,16},{1,9},{9,1},{17,25},{25,17},{2,10},{10... | collective-permute-start | bytes 393224 | tf_op jit(solution)/shard_map/ppermute | solution.py:388
  60.9 5.9 %collective-permute-start.12 = (f32[128,256]{1,0:T(8,128)S(1)}, f32[128,256]{1,0:T(8,128)S(1)}, u32[]{:S(2)}, u32[]{:S(2)}) collective-permute-start(f32[128,256]{1,0:T(8,128)S(1)} %bitcast.62), channel_id=1, source_target_pairs={{0,24},{8,16},{16,8},{24,0},{1,25},{9,17},{17,9},{25,1},{2,26},{10... | collective-permute-start | bytes 393224 | tf_op jit(solution)/shard_map/ppermute | solution.py:388
  63.1 5.3 %collective-permute-start.11 = (f32[128,256]{1,0:T(8,128)S(1)}, f32[128,256]{1,0:T(8,128)S(1)}, u32[]{:S(2)}, u32[]{:S(2)}) collective-permute-start(f32[128,256]{1,0:T(8,128)S(1)} %bitcast.63), channel_id=1, source_target_pairs={{0,16},{8,24},{16,0},{24,8},{1,17},{9,25},{17,1},{25,9},{2,18},{10... | collective-permute-start | bytes 393224 | tf_op jit(solution)/shard_map/ppermute | solution.py:388
  63.7 4.7 %collective-permute-start.10 = (f32[128,256]{1,0:T(8,128)S(1)}, f32[128,256]{1,0:T(8,128)S(1)}, u32[]{:S(2)}, u32[]{:S(2)}) collective-permute-start(f32[128,256]{1,0:T(8,128)S(1)} %bitcast.64), channel_id=1, source_target_pairs={{0,8},{8,0},{16,24},{24,16},{1,9},{9,1},{17,25},{25,17},{2,10},{10... | collective-permute-start | bytes 393224 | tf_op jit(solution)/shard_map/ppermute | solution.py:388
  64.2 2.2 %copy-start.1 = (f32[512,2048]{1,0:T(8,128)S(1)}, f32[512,2048]{1,0:T(8,128)}, u32[]{:S(2)}) copy-start(f32[512,2048]{1,0:T(8,128)} %copy-done) | copy-start | bytes 12582916
  71.1 8.0 %collective-permute-start.13 = (f32[4,256,256]{2,1,0:T(8,128)S(1)}, f32[4,256,256]{2,1,0:T(8,128)}, u32[]{:S(2)}, u32[]{:S(2)}) collective-permute-start(f32[4,256,256]{2,1,0:T(8,128)S(1)} %get-tuple-element.68), channel_id=1, source_target_pairs={{0,32},{32,0},{1,33},{33,1},{2,34},{34,2},{3,35},{35,3},{4,36},{36... | collective-permute-start | bytes 3145736 | tf_op jit(solution)/shard_map/ppermute | solution.py:119
  79.1 5.0 %collective-permute-start.17 = (f32[128,256]{1,0:T(8,128)S(1)}, f32[128,256]{1,0:T(8,128)S(1)}, u32[]{:S(2)}, u32[]{:S(2)}) collective-permute-start(f32[128,256]{1,0:T(8,128)S(1)} %constant_dynamic-slice_fusion), channel_id=1, source_target_pairs={{0,32},{32,0},{1,33},{33,1},{2,34},{34,2},{3,35},{35,3},{4,36},{36... | collective-permute-start | bytes 393224 | tf_op jit(solution)/shard_map/ppermute | solution.py:119
  80.8 14.7 %collective-permute-start.16 = (f32[256,256]{1,0:T(8,128)S(1)}, f32[256,256]{1,0:T(8,128)S(1)}, u32[]{:S(2)}, u32[]{:S(2)}) collective-permute-start(f32[256,256]{1,0:T(8,128)S(1)} %get-tuple-element.107), channel_id=1, source_target_pairs={{0,192},{64,128},{128,64},{192,0},{1,193},{65,129},{129,65},{193,1... | collective-permute-start | bytes 786440 | tf_op jit(solution)/shard_map/ppermute | solution.py:388
  83.4 12.0 %collective-permute-start.15 = (f32[256,256]{1,0:T(8,128)S(1)}, f32[256,256]{1,0:T(8,128)S(1)}, u32[]{:S(2)}, u32[]{:S(2)}) collective-permute-start(f32[256,256]{1,0:T(8,128)S(1)} %get-tuple-element.108), channel_id=1, source_target_pairs={{0,128},{64,192},{128,0},{192,64},{1,129},{65,193},{129,1},{193,65... | collective-permute-start | bytes 786440 | tf_op jit(solution)/shard_map/ppermute | solution.py:388
  83.4 12.4 %collective-permute-start.14 = (f32[256,256]{1,0:T(8,128)S(1)}, f32[256,256]{1,0:T(8,128)}, u32[]{:S(2)}, u32[]{:S(2)}) collective-permute-start(f32[256,256]{1,0:T(8,128)S(1)} %get-tuple-element.109), channel_id=1, source_target_pairs={{0,64},{64,0},{128,192},{192,128},{1,65},{65,1},{129,193},{193,129... | collective-permute-start | bytes 786440 | tf_op jit(solution)/shard_map/ppermute | solution.py:388
  97.7 13.5 %all-to-all-start.2 = ((f32[8,32,256]{2,1,0:T(8,128)}), f32[8,32,256]{2,1,0:T(8,128)S(1)}, u32[]{:S(2)}, u32[]{:S(2)}) async-start(f32[8,32,256]{2,1,0:T(8,128)} %bitcast.27), calls=%async_computation.2 | async-start | bytes 524288 | tf_op jit(solution)/shard_map/all_to_all | solution.py:107
  101.1 7.6 %collective-permute-start.20 = (f32[128,256]{1,0:T(8,128)S(1)}, f32[128,256]{1,0:T(8,128)S(1)}, u32[]{:S(2)}, u32[]{:S(2)}) collective-permute-start(f32[128,256]{1,0:T(8,128)S(1)} %dynamic-slice_add_fusion), channel_id=1, source_target_pairs={{0,192},{64,128},{128,64},{192,0},{1,193},{65,129},{129,65},{193,1... | collective-permute-start | bytes 393224 | tf_op jit(solution)/shard_map/ppermute | solution.py:388
  103.7 5.7 %collective-permute-start.19 = (f32[128,256]{1,0:T(8,128)S(1)}, f32[128,256]{1,0:T(8,128)S(1)}, u32[]{:S(2)}, u32[]{:S(2)}) collective-permute-start(f32[128,256]{1,0:T(8,128)S(1)} %dynamic-slice_add_fusion), channel_id=1, source_target_pairs={{0,128},{64,192},{128,0},{192,64},{1,129},{65,193},{129,1},{193,65... | collective-permute-start | bytes 393224 | tf_op jit(solution)/shard_map/ppermute | solution.py:388
  104.1 5.3 %collective-permute-start.18 = (f32[128,256]{1,0:T(8,128)S(1)}, f32[128,256]{1,0:T(8,128)S(1)}, u32[]{:S(2)}, u32[]{:S(2)}) collective-permute-start(f32[128,256]{1,0:T(8,128)S(1)} %dynamic-slice_add_fusion), channel_id=1, source_target_pairs={{0,64},{64,0},{128,192},{192,128},{1,65},{65,1},{129,193},{193,129... | collective-permute-start | bytes 393224 | tf_op jit(solution)/shard_map/ppermute | solution.py:388
  111.9 8.0 %collective-permute-start.21 = (f32[128,256]{1,0:T(8,128)S(1)}, f32[128,256]{1,0:T(8,128)S(1)}, u32[]{:S(2)}, u32[]{:S(2)}) collective-permute-start(f32[128,256]{1,0:T(8,128)S(1)} %add_add_fusion), channel_id=1, source_target_pairs={{0,32},{32,0},{1,33},{33,1},{2,34},{34,2},{3,35},{35,3},{4,36},{36... | collective-permute-start | bytes 393224 | tf_op jit(solution)/shard_map/ppermute | solution.py:119
  114.6 17.7 %all-to-all-start.3 = ((f32[8,32,256]{2,1,0:T(8,128)}), f32[8,32,256]{2,1,0:T(8,128)S(1)}, u32[]{:S(2)}, u32[]{:S(2)}) async-start(f32[8,32,256]{2,1,0:T(8,128)} %broadcast_in_dim.11), calls=%async_computation.3 | async-start | bytes 524288 | tf_op jit(solution)/shard_map/all_to_all | solution.py:475
  133.3 18.2 %all-to-all-start.4 = ((f32[4,256,256]{2,1,0:T(8,128)}), f32[4,256,256]{2,1,0:T(8,128)S(1)}, u32[]{:S(2)}, u32[]{:S(2)}) async-start(f32[4,256,256]{2,1,0:T(8,128)} %broadcast_in_dim.26), calls=%async_computation.4 | async-start | bytes 2097152 | tf_op jit(solution)/shard_map/all_to_all | solution.py:480
  152.6 8.5 %collective-permute-start.25 = (f32[4,256,256]{2,1,0:T(8,128)S(1)}, f32[4,256,256]{2,1,0:T(8,128)S(1)}, u32[]{:S(2)}, u32[]{:S(2)}) collective-permute-start(f32[4,256,256]{2,1,0:T(8,128)S(1)} %get-tuple-element.89.right_ref.mine_ref), channel_id=1, source_target_pairs={{0,32},{32,0},{1,33},{33,1},{2,34},{34,2},{3,35},{35,3},{4,36},{36... | collective-permute-start | bytes 3145736 | tf_op jit(solution)/shard_map/ppermute | solution.py:119
  154.0 7.1 %collective-permute-start.24 = (f32[8,256]{1,0:T(8,128)S(1)}, f32[8,256]{1,0:T(8,128)S(1)}, u32[]{:S(2)}, u32[]{:S(2)}) collective-permute-start(f32[8,256]{1,0:T(8,128)S(1)} %get-tuple-element.90), channel_id=1, source_target_pairs={{0,24},{8,16},{16,8},{24,0},{1,25},{9,17},{17,9},{25,1},{2,26},{10... | collective-permute-start | bytes 24584 | tf_op jit(solution)/shard_map/ppermute | solution.py:388
  155.7 5.5 %collective-permute-start.23 = (f32[8,256]{1,0:T(8,128)S(1)}, f32[8,256]{1,0:T(8,128)S(1)}, u32[]{:S(2)}, u32[]{:S(2)}) collective-permute-start(f32[8,256]{1,0:T(8,128)S(1)} %get-tuple-element.90), channel_id=1, source_target_pairs={{0,16},{8,24},{16,0},{24,8},{1,17},{9,25},{17,1},{25,9},{2,18},{10... | collective-permute-start | bytes 24584 | tf_op jit(solution)/shard_map/ppermute | solution.py:388
  156.2 4.9 %collective-permute-start.22 = (f32[8,256]{1,0:T(8,128)S(1)}, f32[8,256]{1,0:T(8,128)S(1)}, u32[]{:S(2)}, u32[]{:S(2)}) collective-permute-start(f32[8,256]{1,0:T(8,128)S(1)} %get-tuple-element.90), channel_id=1, source_target_pairs={{0,8},{8,0},{16,24},{24,16},{1,9},{9,1},{17,25},{25,17},{2,10},{10... | collective-permute-start | bytes 24584 | tf_op jit(solution)/shard_map/ppermute | solution.py:388
  157.2 2.2 %copy-start.2 = (f32[512,2048]{1,0:T(8,128)S(1)}, f32[512,2048]{1,0:T(8,128)}, u32[]{:S(2)}) copy-start(f32[512,2048]{1,0:T(8,128)} %copy-done) | copy-start | bytes 12582916
  161.2 1.8 %collective-permute-start.26 = (f32[8,256]{1,0:T(8,128)S(1)}, f32[8,256]{1,0:T(8,128)S(1)}, u32[]{:S(2)}, u32[]{:S(2)}) collective-permute-start(f32[8,256]{1,0:T(8,128)S(1)} %add_add_fusion.1), channel_id=1, source_target_pairs={{0,32},{32,0},{1,33},{33,1},{2,34},{34,2},{3,35},{35,3},{4,36},{36... | collective-permute-start | bytes 24584 | tf_op jit(solution)/shard_map/ppermute | solution.py:119

commit v6 on v5

--- a/solution.py
+++ b/solution.py
@@ -474,11 +474,11 @@
     gram, wide = together(gram, wide)
     pieces = lax.all_to_all(wide, "replica", 0, 0, tiled=True)
     inverse = jnp.eye(RANK, dtype=jnp.float32)
-    gram, inverse, pieces = together(*factor_part(core_joined(gram), inverse, 0, 1), pieces)
+    gram, inverse, pieces = together(*factor_part(core_joined(gram), inverse, 0, 2), pieces)
     wide = jnp.broadcast_to(pieces.reshape(1, RANK, WIDE), (4, RANK, WIDE))
     gram, wide = together(gram, wide)
     raw = lax.all_to_all(wide, "y", 0, 0, tiled=True)
-    gram, inverse = factor_part(gram, inverse, 1, 4)
+    gram, inverse = factor_part(gram, inverse, 2, 4)
     ortho = lines_product(left, inverse)
     ortho, inverse, raw = together(ortho, inverse, raw)
     right_mine, squares = finished(inverse, raw)

time: 168 us -> 168 us (level)
    all_to_all x1, waiting for transfers between devices: 8.82 us -> 5.54 us  [local(): pieces = lax.all_to_all(wide, 'replica', 0, 0, tiled=True)]
    all_to_all x1, waiting for transfers between devices: 4 us -> 7.2 us  [local(): raw = lax.all_to_all(wide, 'y', 0, 0, tiled=True)]
where the time goes in v6:
time: 168 us
  starting transfers between devices  49.1 us (29%)
  waiting for transfers between devices  42.3 us (25%)
  blocking collectives  26.4 us (16%)
  Pallas kernels  25.4 us (15%)
  local copies, waits for them, and re-layouts  16.1 us (10%)
  other arithmetic  4.28 us (3%)
  matrix products  2.94 us (2%)
    ppermute x18, waiting for transfers between devices, turned(): return lax.ppermute(value, axis, [(i, i ^ mask) for i in range(4)])  24.2 us
    ppermute x18, starting transfers between devices, turned(): return lax.ppermute(value, axis, [(i, i ^ mask) for i in range(4)])  21.5 us
    all_to_all x1, blocking collectives, parted(): return lax.all_to_all(blocks, axis, 0, 0, tiled=True)  16 us
    ppermute x9, starting transfers between devices, swapped(): return lax.ppermute(value, 'core', [(0, 1), (1, 0)])  15.2 us
    unnamed x16, local copies, waits for them, and re-layouts  14.2 us
    pallas_call x2, Pallas kernels, factor_part(): pl.pallas_call(functools.partial(factor_kernel, first, last), out_shape=(...  13.4 us
    all_to_all x1, blocking collectives, to_everyone(): lax.all_to_all(jnp.broadcast_to(value[None], (size, *value.shape)), axis,...  10.4 us
    all_to_all x1, waiting for transfers between devices, local(): raw = lax.all_to_all(wide, 'y', 0, 0, tiled=True)  7.2 us
  transfers between devices with their start and end apart: 30, of which 15 were waited for; matrix products, arithmetic and copies ran while one was open for 1% of the time, Pallas kernels for 10%

profile of v6, /device:TPU:1, one launch (start us, length us, event | category | flops | bytes accessed | tf_op | source)
XLA Modules:
  0.0 167.8 jit_solution(10350527370849421116)
XLA Ops:
  0.6 3.7 %collective-permute-start.1 = (f32[32,2048]{1,0:T(8,128)}, f32[32,2048]{1,0:T(8,128)S(1)}, u32[]{:S(2)}, u32[]{:S(2)}) collective-permute-start(f32[32,2048]{1,0:T(8,128)} %bitcast.67), channel_id=1, source_target_pairs={{0,192},{64,128},{128,64},{192,0},{1,193},{65,129},{129,65},{193,1... | collective-permute-start | bytes 786440 | tf_op jit(solution)/shard_map/ppermute | solution.py:388
  4.3 1.3 collective-permute-start.3
  5.6 3.1 %collective-permute-start.6 = (f32[32,2048]{1,0:T(8,128)}, f32[32,2048]{1,0:T(8,128)S(1)}, u32[]{:S(2)}, u32[]{:S(2)}) collective-permute-start(f32[32,2048]{1,0:T(8,128)} %bitcast.70), channel_id=1, source_target_pairs={{0,32},{32,0},{1,33},{33,1},{2,34},{34,2},{3,35},{35,3},{4,36},{36... | collective-permute-start | bytes 786440 | tf_op jit(solution)/shard_map/ppermute | solution.py:119
  8.7 2.2 %copy-done.3 = f32[1,512,2048]{2,1,0:T(8,128)S(1)} copy-done((f32[1,512,2048]{2,1,0:T(8,128)S(1)}, f32[1,512,2048]{2,1,0:T(8,128)}, u32[]{:S(2)}) %copy-start.3) | copy-done | bytes 4194328
  10.8 1.6 copy-done.6
  12.4 1.2 shard_map.58
  13.7 2.0 %copy-done = f32[512,2048]{1,0:T(8,128)} copy-done((f32[512,2048]{1,0:T(8,128)}, f32[512,2048]{1,0:T(8,128)S(1)}, u32[]{:S(2)}) %copy-start) | copy-done | bytes 4194328
  15.6 2.0 %copy-done.4 = f32[512,2048]{1,0:T(8,128)} copy-done((f32[512,2048]{1,0:T(8,128)}, f32[512,2048]{1,0:T(8,128)S(1)}, u32[]{:S(2)}) %copy-start.4) | copy-done | bytes 4194328
  17.7 1.0 collective-permute-start.4
  18.7 1.2 collective-permute-done.4
  21.2 2.0 %copy-done.5 = f32[512,2048]{1,0:T(8,128)S(1)} copy-done((f32[512,2048]{1,0:T(8,128)S(1)}, f32[512,2048]{1,0:T(8,128)}, u32[]{:S(2)}) %copy-start.5) | copy-done | bytes 4194328
  23.2 1.9 %fusion.3 = f32[4,128,256]{2,1,0:T(8,128)S(1)} fusion(f32[4,128,2048]{2,1,0:T(8,128)S(1)} %bitcast.58, f32[256,2048,1]{1,0,2:T(8,128)S(1)} %bitcast.60), kind=kOutput, calls=%fused_computation.59 | convolution fusion | flops 1610612736 | bytes 6815744 | tf_op jit(solution)/shard_map/dot_general | solution.py:141
  25.2 2.6 %collective-permute-start.9 = (f32[128,256]{1,0:T(8,128)S(1)}, f32[128,256]{1,0:T(8,128)S(1)}, u32[]{:S(2)}, u32[]{:S(2)}) collective-permute-start(f32[128,256]{1,0:T(8,128)S(1)} %get-tuple-element.125), channel_id=1, source_target_pairs={{0,24},{8,16},{16,8},{24,0},{1,25},{9,17},{17,9},{25,1},{2,26},{10... | collective-permute-start | bytes 393224 | tf_op jit(solution)/shard_map/ppermute | solution.py:388
  28.6 4.6 %collective-permute-done.9 = f32[128,256]{1,0:T(8,128)S(1)} collective-permute-done((f32[128,256]{1,0:T(8,128)S(1)}, f32[128,256]{1,0:T(8,128)S(1)}, u32[]{:S(2)}, u32[]{:S(2)}) %collective-permute-start.9) | collective-permute-done | bytes 131104 | tf_op jit(solution)/shard_map/ppermute | solution.py:388
  34.4 16.0 %all_to_all.25 = f32[8,16,256]{2,1,0:T(8,128)S(1)} all-to-all(f32[8,16,256]{2,1,0:T(8,128)S(1)} %bitcast.66), channel_id=1, replica_groups=mesh['y'=4,'core'=2,'tensor'=4,'replica'=8] {'replica'}, dimensions={0} | all-to-all | bytes 262144 | tf_op jit(solution)/shard_map/all_to_all | solution.py:107
  50.5 10.4 %all_to_all.26 = f32[8,16,256]{2,1,0:T(8,128)S(1)} all-to-all(f32[8,16,256]{2,1,0:T(8,128)S(1)} %broadcast_in_dim.10), channel_id=1, replica_groups=mesh['y'=4,'core'=2,'tensor'=4,'replica'=8] {'replica'}, dimensions={0} | all-to-all | bytes 262144 | tf_op jit(solution)/shard_map/all_to_all | solution.py:94
  60.9 2.2 %collective-permute-start.12 = (f32[128,256]{1,0:T(8,128)S(1)}, f32[128,256]{1,0:T(8,128)S(1)}, u32[]{:S(2)}, u32[]{:S(2)}) collective-permute-start(f32[128,256]{1,0:T(8,128)S(1)} %bitcast.62), channel_id=1, source_target_pairs={{0,24},{8,16},{16,8},{24,0},{1,25},{9,17},{17,9},{25,1},{2,26},{10... | collective-permute-start | bytes 393224 | tf_op jit(solution)/shard_map/ppermute | solution.py:388
  64.2 2.2 %copy-done.1 = f32[512,2048]{1,0:T(8,128)S(1)} copy-done((f32[512,2048]{1,0:T(8,128)S(1)}, f32[512,2048]{1,0:T(8,128)}, u32[]{:S(2)}) %copy-start.1) | copy-done | bytes 4194328
  66.8 1.7 collective-permute-done.11
  68.5 2.5 %shard_map.60 = (f32[4,256,256]{2,1,0:T(8,128)S(1)}, f32[4,256,256]{2,1,0:T(8,128)S(1)}) custom-call(s32[2]{0:T(128)S(1)} %pad_add_fusion.1.place_ref, f32[512,256]{1,0:T(8,128)S(1)} %pad_maximum_fusion.1.left_ref.a_ref, f32[512,2048]{1,0:T(8,128)S(1)} %shard_map.59.buffer_ref), custom_call_target="tpu_custom_call" | custom-call | flops 1610612736 | bytes 8388608 | tf_op jit(solution)/shard_map/pallas_call | solution.py:252
  71.1 5.6 %collective-permute-start.13 = (f32[4,256,256]{2,1,0:T(8,128)S(1)}, f32[4,256,256]{2,1,0:T(8,128)}, u32[]{:S(2)}, u32[]{:S(2)}) collective-permute-start(f32[4,256,256]{2,1,0:T(8,128)S(1)} %get-tuple-element.68), channel_id=1, source_target_pairs={{0,32},{32,0},{1,33},{33,1},{2,34},{34,2},{3,35},{35,3},{4,36},{36... | collective-permute-start | bytes 3145736 | tf_op jit(solution)/shard_map/ppermute | solution.py:119
  76.7 1.0 fusion.4
  77.7 1.4 collective-permute-done.13
  79.5 1.2 add_bitcast_fusion
  80.8 2.7 %collective-permute-start.16 = (f32[256,256]{1,0:T(8,128)S(1)}, f32[256,256]{1,0:T(8,128)S(1)}, u32[]{:S(2)}, u32[]{:S(2)}) collective-permute-start(f32[256,256]{1,0:T(8,128)S(1)} %get-tuple-element.107), channel_id=1, source_target_pairs={{0,192},{64,128},{128,64},{192,0},{1,193},{65,129},{129,65},{193,1... | collective-permute-start | bytes 786440 | tf_op jit(solution)/shard_map/ppermute | solution.py:388
  84.1 11.3 %collective-permute-done.16 = f32[256,256]{1,0:T(8,128)S(1)} collective-permute-done((f32[256,256]{1,0:T(8,128)S(1)}, f32[256,256]{1,0:T(8,128)S(1)}, u32[]{:S(2)}, u32[]{:S(2)}) %collective-permute-start.16) | collective-permute-done | bytes 262176 | tf_op jit(solution)/shard_map/ppermute | solution.py:388
  95.9 1.8 %fusion = f32[256,256]{1,0:T(8,128)} fusion(f32[256,256]{1,0:T(8,128)} %collective-permute-done.14, f32[256,256]{1,0:T(8,128)S(1)} %collective-permute-done.15, f32[256,256]{1,0:T(8,128)S(1)} %collective-permute-done.16, f32[4,256,256]{2,1,0:T(8,128)S(1)} %get-tuple-element.70, f32[4,256,256]{2,1,0:T(8,128)} %collective-permute-done.13), kind=kLoop, calls=%fused_computation.6 | loop fusion | flops 262144 | bytes 1572864 | tf_op jit(solution)/shard_map/add | solution.py:466
  97.7 3.4 %all-to-all-start.2 = ((f32[8,32,256]{2,1,0:T(8,128)}), f32[8,32,256]{2,1,0:T(8,128)S(1)}, u32[]{:S(2)}, u32[]{:S(2)}) async-start(f32[8,32,256]{2,1,0:T(8,128)} %bitcast.27), calls=%async_computation.2 | async-start | bytes 524288 | tf_op jit(solution)/shard_map/all_to_all | solution.py:107
  101.1 2.7 %collective-permute-start.20 = (f32[128,256]{1,0:T(8,128)S(1)}, f32[128,256]{1,0:T(8,128)S(1)}, u32[]{:S(2)}, u32[]{:S(2)}) collective-permute-start(f32[128,256]{1,0:T(8,128)S(1)} %dynamic-slice_add_fusion), channel_id=1, source_target_pairs={{0,192},{64,128},{128,64},{192,0},{1,193},{65,129},{129,65},{193,1... | collective-permute-start | bytes 393224 | tf_op jit(solution)/shard_map/ppermute | solution.py:388
  104.4 4.3 %collective-permute-done.20 = f32[128,256]{1,0:T(8,128)S(1)} collective-permute-done((f32[128,256]{1,0:T(8,128)S(1)}, f32[128,256]{1,0:T(8,128)S(1)}, u32[]{:S(2)}, u32[]{:S(2)}) %collective-permute-start.20) | collective-permute-done | bytes 131104 | tf_op jit(solution)/shard_map/ppermute | solution.py:388
  109.4 1.7 all-to-all-done.2
  111.9 2.7 %collective-permute-start.21 = (f32[128,256]{1,0:T(8,128)S(1)}, f32[128,256]{1,0:T(8,128)S(1)}, u32[]{:S(2)}, u32[]{:S(2)}) collective-permute-start(f32[128,256]{1,0:T(8,128)S(1)} %add_add_fusion), channel_id=1, source_target_pairs={{0,32},{32,0},{1,33},{33,1},{2,34},{34,2},{3,35},{35,3},{4,36},{36... | collective-permute-start | bytes 393224 | tf_op jit(solution)/shard_map/ppermute | solution.py:119
  114.6 5.3 %all-to-all-start.3 = ((f32[8,32,256]{2,1,0:T(8,128)}), f32[8,32,256]{2,1,0:T(8,128)S(1)}, u32[]{:S(2)}, u32[]{:S(2)}) async-start(f32[8,32,256]{2,1,0:T(8,128)} %broadcast_in_dim.11), calls=%async_computation.3 | async-start | bytes 524288 | tf_op jit(solution)/shard_map/all_to_all | solution.py:475
  120.0 6.7 %shard_map.61 = (f32[256,256]{1,0:T(8,128)S(1)}, f32[256,256]{1,0:T(8,128)S(1)}) custom-call(f32[256,256]{1,0:T(8,128)S(1)} %pad_maximum_fusion.2.gram_ref, f32[256,256]{1,0:T(8,128)S(1)} %fusion.1.inv_ref), custom_call_target="tpu_custom_call" | custom-call | bytes 20000 | tf_op jit(solution)/shard_map/pallas_call | solution.py:85
  126.7 5.5 %all-to-all-done.3 = f32[8,32,256]{2,1,0:T(8,128)S(1)} async-done(((f32[8,32,256]{2,1,0:T(8,128)}), f32[8,32,256]{2,1,0:T(8,128)S(1)}, u32[]{:S(2)}, u32[]{:S(2)}) %all-to-all-start.3) | async-done | bytes 262176 | tf_op jit(solution)/shard_map/all_to_all | solution.py:475
  132.3 1.1 broadcast_in_dim.26
  133.3 3.7 %all-to-all-start.4 = ((f32[4,256,256]{2,1,0:T(8,128)}), f32[4,256,256]{2,1,0:T(8,128)S(1)}, u32[]{:S(2)}, u32[]{:S(2)}) async-start(f32[4,256,256]{2,1,0:T(8,128)} %broadcast_in_dim.26), calls=%async_computation.4 | async-start | bytes 2097152 | tf_op jit(solution)/shard_map/all_to_all | solution.py:480
  137.1 6.7 %shard_map.62 = (f32[256,256]{1,0:T(8,128)}, f32[256,256]{1,0:T(8,128)S(1)}) custom-call(f32[256,256]{1,0:T(8,128)S(1)} %get-tuple-element.82.gram_ref, f32[256,256]{1,0:T(8,128)S(1)} %get-tuple-element.83.inv_ref), custom_call_target="tpu_custom_call" | custom-call | bytes 20000 | tf_op jit(solution)/shard_map/pallas_call | solution.py:85
  144.4 7.2 %all-to-all-done.4.raw_ref = f32[4,256,256]{2,1,0:T(8,128)S(1)} async-done(((f32[4,256,256]{2,1,0:T(8,128)}), f32[4,256,256]{2,1,0:T(8,128)S(1)}, u32[]{:S(2)}, u32[]{:S(2)}) %all-to-all-start.4) | async-done | bytes 1048608 | tf_op jit(solution)/shard_map/all_to_all | solution.py:480
  151.6 1.1 shard_map.64
  152.6 1.3 collective-permute-start.25
  154.0 1.7 %collective-permute-start.24 = (f32[8,256]{1,0:T(8,128)S(1)}, f32[8,256]{1,0:T(8,128)S(1)}, u32[]{:S(2)}, u32[]{:S(2)}) collective-permute-start(f32[8,256]{1,0:T(8,128)S(1)} %get-tuple-element.90), channel_id=1, source_target_pairs={{0,24},{8,16},{16,8},{24,0},{1,25},{9,17},{17,9},{25,1},{2,26},{10... | collective-permute-start | bytes 24584 | tf_op jit(solution)/shard_map/ppermute | solution.py:388
  156.2 1.0 collective-permute-start.22
  157.2 2.2 %copy-done.2 = f32[512,2048]{1,0:T(8,128)S(1)} copy-done((f32[512,2048]{1,0:T(8,128)S(1)}, f32[512,2048]{1,0:T(8,128)}, u32[]{:S(2)}) %copy-start.2) | copy-done | bytes 4194328
  159.4 1.7 %shard_map.65.filled_ref = f32[512,2048]{1,0:T(8,128)} custom-call(s32[1]{0:T(128)} %bitcast.half_ref, f32[512,256]{1,0:T(8,128)S(1)} %shard_map.63.ortho_ref, f32[4,256,256]{2,1,0:T(8,128)S(1)} %get-tuple-element.89.right_ref.mine_ref, f32[512,2048]{1,0:T(8,128)S(1)} %copy-done.2), custom_call_target="tpu_custom_call" | custom-call | flops 805306368 | bytes 4194304 | tf_op jit(solution)/shard_map/pallas_call | solution.py:315
  161.2 1.0 collective-permute-start.26
  162.3 0.8 collective-permute-done.26
  163.0 4.6 %shard_map.66 = (f32[512,2048]{1,0:T(8,128)}, bf16[512,2048]{1,0:T(8,128)(2,1)}, f32[32,2048]{1,0:T(8,128)}) custom-call(s32[2]{0:T(128)S(1)} %pad_add_fusion.place_ref, f32[512,256]{1,0:T(8,128)S(1)} %shard_map.63.ortho_ref, f32[4,256,256]{2,1,0:T(8,128)S(1)} %get-tuple-element.89.right_ref.mine_ref, ...), custom_call_target="tpu_custom_call", output_to_operand_aliasing={{0}: (6, {})} | custom-call | flops 2415919104 | bytes 8388608 | tf_op jit(solution)/shard_map/pallas_call | solution.py:358
  (70 shorter events, 10.1 us)
Async XLA Ops:
  0.6 17.0 %collective-permute-start.1 = (f32[32,2048]{1,0:T(8,128)}, f32[32,2048]{1,0:T(8,128)S(1)}, u32[]{:S(2)}, u32[]{:S(2)}) collective-permute-start(f32[32,2048]{1,0:T(8,128)} %bitcast.67), channel_id=1, source_target_pairs={{0,192},{64,128},{128,64},{192,0},{1,193},{65,129},{129,65},{193,1... | collective-permute-start | bytes 786440 | tf_op jit(solution)/shard_map/ppermute | solution.py:388
  4.3 13.4 %collective-permute-start = (f32[32,2048]{1,0:T(8,128)}, f32[32,2048]{1,0:T(8,128)S(1)}, u32[]{:S(2)}, u32[]{:S(2)}) collective-permute-start(f32[32,2048]{1,0:T(8,128)} %bitcast.68), channel_id=1, source_target_pairs={{0,64},{64,0},{128,192},{192,128},{1,65},{65,1},{129,193},{193,129... | collective-permute-start | bytes 786440 | tf_op jit(solution)/shard_map/ppermute | solution.py:388
  4.3 13.4 %collective-permute-start.3 = (f32[32,2048]{1,0:T(8,128)}, f32[32,2048]{1,0:T(8,128)S(1)}, u32[]{:S(2)}, u32[]{:S(2)}) collective-permute-start(f32[32,2048]{1,0:T(8,128)} %bitcast.69), channel_id=1, source_target_pairs={{0,128},{64,192},{128,0},{192,64},{1,129},{65,193},{129,1},{193,65... | collective-permute-start | bytes 786440 | tf_op jit(solution)/shard_map/ppermute | solution.py:388
  5.6 13.1 %collective-permute-start.6 = (f32[32,2048]{1,0:T(8,128)}, f32[32,2048]{1,0:T(8,128)S(1)}, u32[]{:S(2)}, u32[]{:S(2)}) collective-permute-start(f32[32,2048]{1,0:T(8,128)} %bitcast.70), channel_id=1, source_target_pairs={{0,32},{32,0},{1,33},{33,1},{2,34},{34,2},{3,35},{35,3},{4,36},{36... | collective-permute-start | bytes 786440 | tf_op jit(solution)/shard_map/ppermute | solution.py:119
  8.7 2.2 %copy-start.3 = (f32[1,512,2048]{2,1,0:T(8,128)S(1)}, f32[1,512,2048]{2,1,0:T(8,128)}, u32[]{:S(2)}) copy-start(f32[1,512,2048]{2,1,0:T(8,128)} %momentum_ref) | copy-start | bytes 12582916
  10.8 1.6 copy-start.6
  12.4 7.7 %copy-start.7 = (f32[2048,32]{0,1:T(8,128)S(1)}, f32[2048,32]{0,1:T(8,128)}, u32[]{:S(2)}) copy-start(f32[2048,32]{0,1:T(8,128)} %param.5) | copy-start | bytes 786436
  13.7 2.0 %copy-start = (f32[512,2048]{1,0:T(8,128)}, f32[512,2048]{1,0:T(8,128)S(1)}, u32[]{:S(2)}) copy-start(f32[512,2048]{1,0:T(8,128)S(1)} %get-tuple-element.59.far_ref.buffer_ref) | copy-start | bytes 12582916
  15.6 2.0 %copy-start.4 = (f32[512,2048]{1,0:T(8,128)}, f32[512,2048]{1,0:T(8,128)S(1)}, u32[]{:S(2)}) copy-start(f32[512,2048]{1,0:T(8,128)S(1)} %get-tuple-element.54) | copy-start | bytes 12582916
  17.7 2.2 %collective-permute-start.2 = (f32[32,2048]{1,0:T(8,128)S(1)}, f32[32,2048]{1,0:T(8,128)S(1)}, u32[]{:S(2)}, u32[]{:S(2)}) collective-permute-start(f32[32,2048]{1,0:T(8,128)S(1)} %collective-permute-done.1), channel_id=1, source_target_pairs={{0,32},{32,0},{1,33},{33,1},{2,34},{34,2},{3,35},{35,3},{4,36},{36... | collective-permute-start | bytes 786440 | tf_op jit(solution)/shard_map/ppermute | solution.py:119
  17.7 2.1 %collective-permute-start.4 = (f32[32,2048]{1,0:T(8,128)S(1)}, f32[32,2048]{1,0:T(8,128)S(1)}, u32[]{:S(2)}, u32[]{:S(2)}) collective-permute-start(f32[32,2048]{1,0:T(8,128)S(1)} %collective-permute-done.3), channel_id=1, source_target_pairs={{0,32},{32,0},{1,33},{33,1},{2,34},{34,2},{3,35},{35,3},{4,36},{36... | collective-permute-start | bytes 786440 | tf_op jit(solution)/shard_map/ppermute | solution.py:119
  18.6 1.5 collective-permute-start.5
  21.1 2.2 %copy-start.5 = (f32[512,2048]{1,0:T(8,128)S(1)}, f32[512,2048]{1,0:T(8,128)}, u32[]{:S(2)}) copy-start(f32[512,2048]{1,0:T(8,128)} %copy-done.4) | copy-start | bytes 12582916
  25.2 8.0 %collective-permute-start.9 = (f32[128,256]{1,0:T(8,128)S(1)}, f32[128,256]{1,0:T(8,128)S(1)}, u32[]{:S(2)}, u32[]{:S(2)}) collective-permute-start(f32[128,256]{1,0:T(8,128)S(1)} %get-tuple-element.125), channel_id=1, source_target_pairs={{0,24},{8,16},{16,8},{24,0},{1,25},{9,17},{17,9},{25,1},{2,26},{10... | collective-permute-start | bytes 393224 | tf_op jit(solution)/shard_map/ppermute | solution.py:388
  27.8 5.9 %collective-permute-start.8 = (f32[128,256]{1,0:T(8,128)S(1)}, f32[128,256]{1,0:T(8,128)S(1)}, u32[]{:S(2)}, u32[]{:S(2)}) collective-permute-start(f32[128,256]{1,0:T(8,128)S(1)} %get-tuple-element.126), channel_id=1, source_target_pairs={{0,16},{8,24},{16,0},{24,8},{1,17},{9,25},{17,1},{25,9},{2,18},{10... | collective-permute-start | bytes 393224 | tf_op jit(solution)/shard_map/ppermute | solution.py:388
  28.3 6.1 %collective-permute-start.7 = (f32[128,256]{1,0:T(8,128)S(1)}, f32[128,256]{1,0:T(8,128)S(1)}, u32[]{:S(2)}, u32[]{:S(2)}) collective-permute-start(f32[128,256]{1,0:T(8,128)S(1)} %get-tuple-element.127), channel_id=1, source_target_pairs={{0,8},{8,0},{16,24},{24,16},{1,9},{9,1},{17,25},{25,17},{2,10},{10... | collective-permute-start | bytes 393224 | tf_op jit(solution)/shard_map/ppermute | solution.py:388
  60.9 5.9 %collective-permute-start.12 = (f32[128,256]{1,0:T(8,128)S(1)}, f32[128,256]{1,0:T(8,128)S(1)}, u32[]{:S(2)}, u32[]{:S(2)}) collective-permute-start(f32[128,256]{1,0:T(8,128)S(1)} %bitcast.62), channel_id=1, source_target_pairs={{0,24},{8,16},{16,8},{24,0},{1,25},{9,17},{17,9},{25,1},{2,26},{10... | collective-permute-start | bytes 393224 | tf_op jit(solution)/shard_map/ppermute | solution.py:388
  63.1 5.3 %collective-permute-start.11 = (f32[128,256]{1,0:T(8,128)S(1)}, f32[128,256]{1,0:T(8,128)S(1)}, u32[]{:S(2)}, u32[]{:S(2)}) collective-permute-start(f32[128,256]{1,0:T(8,128)S(1)} %bitcast.63), channel_id=1, source_target_pairs={{0,16},{8,24},{16,0},{24,8},{1,17},{9,25},{17,1},{25,9},{2,18},{10... | collective-permute-start | bytes 393224 | tf_op jit(solution)/shard_map/ppermute | solution.py:388
  63.7 4.7 %collective-permute-start.10 = (f32[128,256]{1,0:T(8,128)S(1)}, f32[128,256]{1,0:T(8,128)S(1)}, u32[]{:S(2)}, u32[]{:S(2)}) collective-permute-start(f32[128,256]{1,0:T(8,128)S(1)} %bitcast.64), channel_id=1, source_target_pairs={{0,8},{8,0},{16,24},{24,16},{1,9},{9,1},{17,25},{25,17},{2,10},{10... | collective-permute-start | bytes 393224 | tf_op jit(solution)/shard_map/ppermute | solution.py:388
  64.2 2.2 %copy-start.1 = (f32[512,2048]{1,0:T(8,128)S(1)}, f32[512,2048]{1,0:T(8,128)}, u32[]{:S(2)}) copy-start(f32[512,2048]{1,0:T(8,128)} %copy-done) | copy-start | bytes 12582916
  71.1 8.0 %collective-permute-start.13 = (f32[4,256,256]{2,1,0:T(8,128)S(1)}, f32[4,256,256]{2,1,0:T(8,128)}, u32[]{:S(2)}, u32[]{:S(2)}) collective-permute-start(f32[4,256,256]{2,1,0:T(8,128)S(1)} %get-tuple-element.68), channel_id=1, source_target_pairs={{0,32},{32,0},{1,33},{33,1},{2,34},{34,2},{3,35},{35,3},{4,36},{36... | collective-permute-start | bytes 3145736 | tf_op jit(solution)/shard_map/ppermute | solution.py:119
  79.1 5.0 %collective-permute-start.17 = (f32[128,256]{1,0:T(8,128)S(1)}, f32[128,256]{1,0:T(8,128)S(1)}, u32[]{:S(2)}, u32[]{:S(2)}) collective-permute-start(f32[128,256]{1,0:T(8,128)S(1)} %constant_dynamic-slice_fusion), channel_id=1, source_target_pairs={{0,32},{32,0},{1,33},{33,1},{2,34},{34,2},{3,35},{35,3},{4,36},{36... | collective-permute-start | bytes 393224 | tf_op jit(solution)/shard_map/ppermute | solution.py:119
  80.8 14.7 %collective-permute-start.16 = (f32[256,256]{1,0:T(8,128)S(1)}, f32[256,256]{1,0:T(8,128)S(1)}, u32[]{:S(2)}, u32[]{:S(2)}) collective-permute-start(f32[256,256]{1,0:T(8,128)S(1)} %get-tuple-element.107), channel_id=1, source_target_pairs={{0,192},{64,128},{128,64},{192,0},{1,193},{65,129},{129,65},{193,1... | collective-permute-start | bytes 786440 | tf_op jit(solution)/shard_map/ppermute | solution.py:388
  83.4 12.0 %collective-permute-start.15 = (f32[256,256]{1,0:T(8,128)S(1)}, f32[256,256]{1,0:T(8,128)S(1)}, u32[]{:S(2)}, u32[]{:S(2)}) collective-permute-start(f32[256,256]{1,0:T(8,128)S(1)} %get-tuple-element.108), channel_id=1, source_target_pairs={{0,128},{64,192},{128,0},{192,64},{1,129},{65,193},{129,1},{193,65... | collective-permute-start | bytes 786440 | tf_op jit(solution)/shard_map/ppermute | solution.py:388
  83.4 12.4 %collective-permute-start.14 = (f32[256,256]{1,0:T(8,128)S(1)}, f32[256,256]{1,0:T(8,128)}, u32[]{:S(2)}, u32[]{:S(2)}) collective-permute-start(f32[256,256]{1,0:T(8,128)S(1)} %get-tuple-element.109), channel_id=1, source_target_pairs={{0,64},{64,0},{128,192},{192,128},{1,65},{65,1},{129,193},{193,129... | collective-permute-start | bytes 786440 | tf_op jit(solution)/shard_map/ppermute | solution.py:388
  97.7 13.5 %all-to-all-start.2 = ((f32[8,32,256]{2,1,0:T(8,128)}), f32[8,32,256]{2,1,0:T(8,128)S(1)}, u32[]{:S(2)}, u32[]{:S(2)}) async-start(f32[8,32,256]{2,1,0:T(8,128)} %bitcast.27), calls=%async_computation.2 | async-start | bytes 524288 | tf_op jit(solution)/shard_map/all_to_all | solution.py:107
  101.1 7.6 %collective-permute-start.20 = (f32[128,256]{1,0:T(8,128)S(1)}, f32[128,256]{1,0:T(8,128)S(1)}, u32[]{:S(2)}, u32[]{:S(2)}) collective-permute-start(f32[128,256]{1,0:T(8,128)S(1)} %dynamic-slice_add_fusion), channel_id=1, source_target_pairs={{0,192},{64,128},{128,64},{192,0},{1,193},{65,129},{129,65},{193,1... | collective-permute-start | bytes 393224 | tf_op jit(solution)/shard_map/ppermute | solution.py:388
  103.7 5.7 %collective-permute-start.19 = (f32[128,256]{1,0:T(8,128)S(1)}, f32[128,256]{1,0:T(8,128)S(1)}, u32[]{:S(2)}, u32[]{:S(2)}) collective-permute-start(f32[128,256]{1,0:T(8,128)S(1)} %dynamic-slice_add_fusion), channel_id=1, source_target_pairs={{0,128},{64,192},{128,0},{192,64},{1,129},{65,193},{129,1},{193,65... | collective-permute-start | bytes 393224 | tf_op jit(solution)/shard_map/ppermute | solution.py:388
  104.1 5.3 %collective-permute-start.18 = (f32[128,256]{1,0:T(8,128)S(1)}, f32[128,256]{1,0:T(8,128)S(1)}, u32[]{:S(2)}, u32[]{:S(2)}) collective-permute-start(f32[128,256]{1,0:T(8,128)S(1)} %dynamic-slice_add_fusion), channel_id=1, source_target_pairs={{0,64},{64,0},{128,192},{192,128},{1,65},{65,1},{129,193},{193,129... | collective-permute-start | bytes 393224 | tf_op jit(solution)/shard_map/ppermute | solution.py:388
  111.9 8.0 %collective-permute-start.21 = (f32[128,256]{1,0:T(8,128)S(1)}, f32[128,256]{1,0:T(8,128)S(1)}, u32[]{:S(2)}, u32[]{:S(2)}) collective-permute-start(f32[128,256]{1,0:T(8,128)S(1)} %add_add_fusion), channel_id=1, source_target_pairs={{0,32},{32,0},{1,33},{33,1},{2,34},{34,2},{3,35},{35,3},{4,36},{36... | collective-permute-start | bytes 393224 | tf_op jit(solution)/shard_map/ppermute | solution.py:119
  114.6 17.7 %all-to-all-start.3 = ((f32[8,32,256]{2,1,0:T(8,128)}), f32[8,32,256]{2,1,0:T(8,128)S(1)}, u32[]{:S(2)}, u32[]{:S(2)}) async-start(f32[8,32,256]{2,1,0:T(8,128)} %broadcast_in_dim.11), calls=%async_computation.3 | async-start | bytes 524288 | tf_op jit(solution)/shard_map/all_to_all | solution.py:475
  133.3 18.2 %all-to-all-start.4 = ((f32[4,256,256]{2,1,0:T(8,128)}), f32[4,256,256]{2,1,0:T(8,128)S(1)}, u32[]{:S(2)}, u32[]{:S(2)}) async-start(f32[4,256,256]{2,1,0:T(8,128)} %broadcast_in_dim.26), calls=%async_computation.4 | async-start | bytes 2097152 | tf_op jit(solution)/shard_map/all_to_all | solution.py:480
  152.6 8.5 %collective-permute-start.25 = (f32[4,256,256]{2,1,0:T(8,128)S(1)}, f32[4,256,256]{2,1,0:T(8,128)S(1)}, u32[]{:S(2)}, u32[]{:S(2)}) collective-permute-start(f32[4,256,256]{2,1,0:T(8,128)S(1)} %get-tuple-element.89.right_ref.mine_ref), channel_id=1, source_target_pairs={{0,32},{32,0},{1,33},{33,1},{2,34},{34,2},{3,35},{35,3},{4,36},{36... | collective-permute-start | bytes 3145736 | tf_op jit(solution)/shard_map/ppermute | solution.py:119
  154.0 7.1 %collective-permute-start.24 = (f32[8,256]{1,0:T(8,128)S(1)}, f32[8,256]{1,0:T(8,128)S(1)}, u32[]{:S(2)}, u32[]{:S(2)}) collective-permute-start(f32[8,256]{1,0:T(8,128)S(1)} %get-tuple-element.90), channel_id=1, source_target_pairs={{0,24},{8,16},{16,8},{24,0},{1,25},{9,17},{17,9},{25,1},{2,26},{10... | collective-permute-start | bytes 24584 | tf_op jit(solution)/shard_map/ppermute | solution.py:388
  155.7 5.5 %collective-permute-start.23 = (f32[8,256]{1,0:T(8,128)S(1)}, f32[8,256]{1,0:T(8,128)S(1)}, u32[]{:S(2)}, u32[]{:S(2)}) collective-permute-start(f32[8,256]{1,0:T(8,128)S(1)} %get-tuple-element.90), channel_id=1, source_target_pairs={{0,16},{8,24},{16,0},{24,8},{1,17},{9,25},{17,1},{25,9},{2,18},{10... | collective-permute-start | bytes 24584 | tf_op jit(solution)/shard_map/ppermute | solution.py:388
  156.2 4.9 %collective-permute-start.22 = (f32[8,256]{1,0:T(8,128)S(1)}, f32[8,256]{1,0:T(8,128)S(1)}, u32[]{:S(2)}, u32[]{:S(2)}) collective-permute-start(f32[8,256]{1,0:T(8,128)S(1)} %get-tuple-element.90), channel_id=1, source_target_pairs={{0,8},{8,0},{16,24},{24,16},{1,9},{9,1},{17,25},{25,17},{2,10},{10... | collective-permute-start | bytes 24584 | tf_op jit(solution)/shard_map/ppermute | solution.py:388
  157.2 2.2 %copy-start.2 = (f32[512,2048]{1,0:T(8,128)S(1)}, f32[512,2048]{1,0:T(8,128)}, u32[]{:S(2)}) copy-start(f32[512,2048]{1,0:T(8,128)} %copy-done) | copy-start | bytes 12582916
  161.2 1.8 %collective-permute-start.26 = (f32[8,256]{1,0:T(8,128)S(1)}, f32[8,256]{1,0:T(8,128)S(1)}, u32[]{:S(2)}, u32[]{:S(2)}) collective-permute-start(f32[8,256]{1,0:T(8,128)S(1)} %add_add_fusion.1), channel_id=1, source_target_pairs={{0,32},{32,0},{1,33},{33,1},{2,34},{34,2},{3,35},{35,3},{4,36},{36... | collective-permute-start | bytes 24584 | tf_op jit(solution)/shard_map/ppermute | solution.py:119
